TPU v7x, 32 devices: a whole 2x2x4 slice. The times are simulated.
32 devices in a mesh: lang: 16 (over z, y, x), rep: 2 (over core).
Axes of the slice: x: 2, y: 2, z: 4, core: 2. Of those that a mesh axis runs over, the one named last changes fastest.
Arguments:
- tokens: bfloat16 [4096, 1024], P(('lang', 'rep')), may hold values from -6 to 6
- grad_out: bfloat16 [4096, 1024], P(('lang', 'rep')), may hold values from -6 to 6
- lang_ids: int32 [4096], P(('lang', 'rep')), may hold values from 0 to 7, as said below
- slot_ids: int32 [4096], P(('lang', 'rep')), may hold values from 0 to 23, as said below
- w_up: bfloat16 [1024, 32768], P(None, 'lang'), may hold values from -0.1875 to 0.1875
- w_down_t: bfloat16 [1024, 32768], P(None, 'lang'), may hold values from -0.09375 to 0.09375
Outputs:
- ffn_out: bfloat16 [4096, 1024], P(('lang', 'rep'))
- grad_tokens: bfloat16 [4096, 1024], P(('lang', 'rep'))
- grad_up: float32 [1024, 32768], P('rep', 'lang')
- grad_down: float32 [1024, 32768], P('rep', 'lang')
Inputs may be any that keep to these rules, and one draw needn't show every extreme that they name: `lang_ids`: each device holds 128 consecutive tokens. On every device one language, the same on all devices, has exactly 24 tokens; every other language has at most 18 tokens on a device, and on every device one of them has exactly 18. `slot_ids`: on each device the tokens of one language hold the distinct slots 0 to their count minus 1, in no particular order.
All inputs are finite; a program needn't handle non-finite values.
Results may differ from a plain program's by a relative error of at most 0.0058.
Values may be sent and summed in bfloat16 or wider, within the bound.
No kernel may reach another device: no remote copies, remote signals or barrier semaphores. Data moves between devices by JAX's collectives and lax.ppermute only.
A program may use at most 128 MiB of HBM per device.

v0:
```python
import jax
import jax.numpy as jnp
from jax import lax
from jax.sharding import PartitionSpec as P

MODULES = 8
TOK_DEV = 128
CAPACITY = 18


INV_ROOT_TWO = 0.7071067811865476
INV_ROOT_TAU = 0.3989422804014327


def gelu_value(values):
    return 0.5 * values * (1.0 + lax.erf(values * INV_ROOT_TWO))


def gelu_slope(values):
    return (
        0.5 * (1.0 + lax.erf(values * INV_ROOT_TWO))
        + values * jnp.exp(-0.5 * values * values) * INV_ROOT_TAU
    )


def per_device(tokens, grad_out, lang_ids, slot_ids, w_up, w_down_t):
    groups = lax.axis_size("lang") // MODULES
    feature_width = tokens.shape[1]
    hid_units = w_up.shape[1]
    capacity = CAPACITY
    keep_mask = slot_ids < capacity
    target = jnp.where(keep_mask, lang_ids * capacity + slot_ids, MODULES * capacity)
    safe_slot = jnp.minimum(slot_ids, capacity - 1)
    token_scale = 1.0 / TOK_DEV

    def place(values):
        buffer = (
            jnp.zeros((MODULES * capacity, feature_width), values.dtype)
            .at[target]
            .set(values, mode="drop")
        )
        return buffer.reshape(MODULES, capacity, feature_width)

    def dispatch(values):
        return jnp.repeat(place(values), groups, axis=0)

    def collect(returned):
        picked = returned.reshape(MODULES, groups, capacity, feature_width)[lang_ids, :, safe_slot]
        total_sum = jnp.sum(picked, axis=1, dtype=jnp.float32)
        return jnp.where(keep_mask[:, None], total_sum, 0.0).astype(jnp.bfloat16)

    received = lax.all_to_all(dispatch(tokens), "lang", split_axis=0, concat_axis=0, tiled=True)
    src_count, slot_count, _ = received.shape
    pre_rows = jnp.dot(
        received.reshape(-1, feature_width), w_up, preferred_element_type=jnp.float32
    )
    hidden_rows = gelu_value(pre_rows).astype(jnp.bfloat16)
    partial_rows = (
        lax.dot_general(
            hidden_rows, w_down_t, (((1,), (1,)), ((), ())), preferred_element_type=jnp.float32
        )
        .astype(jnp.bfloat16)
        .reshape(src_count, slot_count, feature_width)
    )
    returned = lax.all_to_all(partial_rows, "lang", split_axis=0, concat_axis=0, tiled=True)
    pre_act = pre_rows.reshape(src_count, slot_count, hid_units)
    hidden = hidden_rows.reshape(src_count, slot_count, hid_units)
    recv_grads = lax.all_to_all(dispatch(grad_out), "lang", split_axis=0, concat_axis=0, tiled=True)
    flat_tokens = received.reshape(-1, feature_width)
    flat_grads = recv_grads.reshape(-1, feature_width)
    pre_flat = pre_act.reshape(-1, hid_units)
    hidden_flat = hidden.reshape(-1, hid_units)
    sliced = flat_grads
    grad_down = lax.psum_scatter(
        lax.dot_general(
            sliced, hidden_flat, (((0,), (0,)), ((), ())), preferred_element_type=jnp.float32
        )
        * token_scale,
        "rep",
        scatter_dimension=0,
        tiled=True,
    )
    d_hidden = jnp.dot(flat_grads, w_down_t, preferred_element_type=jnp.float32)
    d_pre = (d_hidden * gelu_slope(pre_flat)).astype(jnp.bfloat16)
    sliced = flat_tokens
    grad_up = lax.psum_scatter(
        lax.dot_general(sliced, d_pre, (((0,), (0,)), ((), ())), preferred_element_type=jnp.float32)
        * token_scale,
        "rep",
        scatter_dimension=0,
        tiled=True,
    )
    dx_part = lax.dot_general(
        d_pre, w_up, (((1,), (1,)), ((), ())), preferred_element_type=jnp.float32
    ).astype(jnp.bfloat16)
    dx_part = dx_part.reshape(received.shape)
    dx_back = lax.all_to_all(dx_part, "lang", split_axis=0, concat_axis=0, tiled=True)
    return (collect(returned), collect(dx_back), grad_up, grad_down)


def solution(mesh):
    placed = (
        P(("lang", "rep"), None),
        P(("lang", "rep"), None),
        P(("lang", "rep")),
        P(("lang", "rep")),
        P(None, "lang"),
        P(None, "lang"),
    )
    return jax.shard_map(
        per_device,
        mesh=mesh,
        in_specs=placed,
        out_specs=(
            P(("lang", "rep"), None),
            P(("lang", "rep"), None),
            P("rep", "lang"),
            P("rep", "lang"),
        ),
        check_vma=False,
    )
```

profile of v0, /device:TPU:0, one launch (start us, length us, event | category | flops | bytes accessed | tf_op | source)
XLA Modules:
  0.0 152.1 jit_solution(6746679959262715377)
XLA Ops:
  7.2 0.7 fusion.11
  7.8 1.6 %scatter_custom_fusion = bf16[144,1024]{1,0:T(8,128)(2,1)S(1)} fusion(s32[128]{0:T(128)S(1)} %get-tuple-element.5, bf16[128,1024]{1,0:T(8,128)(2,1)} %param.6, bf16[]{:T(256)} %constant.0.clone.1), kind=kCustom, calls=%fused_computation.23 | custom fusion | bytes 295424 | tf_op jit(solution)/shard_map/scatter | solution.py:40
  9.5 0.1 reshape.40
  9.6 1.0 broadcast_in_dim.43
  10.6 8.3 %all-to-all-start = ((bf16[16,18,1024]{2,1,0:T(8,128)(2,1)}), bf16[16,18,1024]{2,1,0:T(8,128)(2,1)S(1)}, u32[]{:S(2)}, u32[]{:S(2)}) async-start(bf16[16,18,1024]{2,1,0:T(8,128)(2,1)} %bitcast), calls=%async_computation | async-start | bytes 1572864 | tf_op jit(solution)/shard_map/all_to_all | solution.py:52
  18.9 1.6 %scatter_custom_fusion.1 = bf16[144,1024]{1,0:T(8,128)(2,1)S(1)} fusion(s32[128]{0:T(128)S(1)} %get-tuple-element.5, bf16[128,1024]{1,0:T(8,128)(2,1)} %param.7, bf16[]{:T(256)} %constant.0.clone.1), kind=kCustom, calls=%fused_computation.21 | custom fusion | bytes 295424 | tf_op jit(solution)/shard_map/scatter | solution.py:40
  20.6 18.0 %all-to-all-done = bf16[16,18,1024]{2,1,0:T(8,128)(2,1)S(1)} async-done(((bf16[16,18,1024]{2,1,0:T(8,128)(2,1)}), bf16[16,18,1024]{2,1,0:T(8,128)(2,1)S(1)}, u32[]{:S(2)}, u32[]{:S(2)}) %all-to-all-start) | async-done | bytes 589856 | tf_op jit(solution)/shard_map/all_to_all | solution.py:52
  38.6 1.0 broadcast_in_dim.47
  39.6 4.9 %all-to-all-start.2 = ((bf16[16,18,1024]{2,1,0:T(8,128)(2,1)}), bf16[16,18,1024]{2,1,0:T(8,128)(2,1)S(1)}, u32[]{:S(2)}, u32[]{:S(2)}) async-start(bf16[16,18,1024]{2,1,0:T(8,128)(2,1)} %bitcast.2), calls=%async_computation.2 | async-start | bytes 1572864 | tf_op jit(solution)/shard_map/all_to_all | solution.py:68
  44.6 0.2 reshape.42
  44.8 5.0 %fusion.14 = f32[288,2048]{1,0:T(8,128)} fusion(bf16[288,1024]{1,0:T(8,128)(2,1)S(1)} %reshape.42, bf16[1024,2048]{1,0:T(8,128)(2,1)} %param.10), kind=kOutput, calls=%fused_computation.34 | convolution fusion | flops 1207959552 | bytes 7143424 | tf_op jit(solution)/shard_map/dot_general | solution.py:54
  49.8 13.4 %all-to-all-done.2 = bf16[16,18,1024]{2,1,0:T(8,128)(2,1)S(1)} async-done(((bf16[16,18,1024]{2,1,0:T(8,128)(2,1)}), bf16[16,18,1024]{2,1,0:T(8,128)(2,1)S(1)}, u32[]{:S(2)}, u32[]{:S(2)}) %all-to-all-start.2) | async-done | bytes 589856 | tf_op jit(solution)/shard_map/all_to_all | solution.py:68
  63.2 0.2 reshape.47
  63.3 7.3 %convolution_multiply_fusion = f32[1024,2048]{1,0:T(8,128)} fusion(bf16[288,1024]{1,0:T(8,128)(2,1)S(1)} %reshape.47, f32[288,2048]{1,0:T(8,128)} %fusion.14), kind=kOutput, calls=%fused_computation.4 | convolution fusion | flops 1213005824 | bytes 11337728 | tf_op jit(solution)/shard_map/dot_general | solution.py:75
  70.8 1.6 %copy-done = f32[288,2048]{1,0:T(8,128)S(1)} copy-done((f32[288,2048]{1,0:T(8,128)S(1)}, f32[288,2048]{1,0:T(8,128)}, u32[]{:S(2)}) %copy-start) | copy-done | bytes 2359320
  72.4 4.1 %fusion = bf16[288,2048]{1,0:T(8,128)(2,1)S(1)} fusion(bf16[288,1024]{1,0:T(8,128)(2,1)S(1)} %reshape.47, bf16[1024,2048]{1,0:T(8,128)(2,1)} %param.11, f32[288,2048]{1,0:T(8,128)S(1)} %copy-done), kind=kOutput, calls=%fused_computation.8 | convolution fusion | flops 1213857792 | bytes 8323072 | tf_op jit(solution)/shard_map/dot_general | solution.py:83
  76.5 1.0 copy-done.1
  77.5 7.3 %convolution_multiply_fusion.1 = f32[1024,2048]{1,0:T(8,128)} fusion(bf16[288,1024]{1,0:T(8,128)(2,1)S(1)} %reshape.42, bf16[288,2048]{1,0:T(8,128)(2,1)S(1)} %fusion), kind=kOutput, calls=%fused_computation.5 | convolution fusion | flops 1210056704 | bytes 10158080 | tf_op jit(solution)/shard_map/dot_general | solution.py:87
  84.8 3.9 %convolution_convert_fusion.1 = bf16[288,1024]{1,0:T(8,128)(2,1)S(1)} fusion(bf16[1024,2048]{1,0:T(8,128)(2,1)} %param.11, f32[288,2048]{1,0:T(8,128)S(1)} %copy-done), kind=kOutput, calls=%fused_computation.16 | convolution fusion | flops 1211203584 | bytes 7143424 | tf_op jit(solution)/shard_map/dot_general | solution.py:59
  88.7 1.1 reshape.43
  89.8 5.5 %all-to-all-start.1 = ((bf16[16,18,1024]{2,1,0:T(8,128)(2,1)}), bf16[16,18,1024]{2,1,0:T(8,128)(2,1)S(1)}, u32[]{:S(2)}, u32[]{:S(2)}) async-start(bf16[16,18,1024]{2,1,0:T(8,128)(2,1)} %reshape.43), calls=%async_computation.1 | async-start | bytes 1572864 | tf_op jit(solution)/shard_map/all_to_all | solution.py:65
  95.3 4.2 %convolution_convert_fusion = bf16[288,1024]{1,0:T(8,128)(2,1)S(1)} fusion(bf16[288,2048]{1,0:T(8,128)(2,1)S(1)} %copy-done.2, bf16[1024,2048]{1,0:T(8,128)(2,1)} %param.10), kind=kOutput, calls=%fused_computation.15 | convolution fusion | flops 1208254464 | bytes 5963776 | tf_op jit(solution)/shard_map/dot_general | solution.py:93
  99.5 1.1 reshape.48
  100.6 13.3 %all-to-all-done.1 = bf16[16,18,1024]{2,1,0:T(8,128)(2,1)S(1)} async-done(((bf16[16,18,1024]{2,1,0:T(8,128)(2,1)}), bf16[16,18,1024]{2,1,0:T(8,128)(2,1)S(1)}, u32[]{:S(2)}, u32[]{:S(2)}) %all-to-all-start.1) | async-done | bytes 589856 | tf_op jit(solution)/shard_map/all_to_all | solution.py:65
  113.9 4.9 %all-to-all-start.3 = ((bf16[16,18,1024]{2,1,0:T(8,128)(2,1)}), bf16[16,18,1024]{2,1,0:T(8,128)(2,1)S(1)}, u32[]{:S(2)}, u32[]{:S(2)}) async-start(bf16[16,18,1024]{2,1,0:T(8,128)(2,1)} %reshape.48), calls=%async_computation.3 | async-start | bytes 1572864 | tf_op jit(solution)/shard_map/all_to_all | solution.py:97
  118.8 0.6 copy.11
  119.4 18.0 %all-to-all-done.3 = bf16[16,18,1024]{2,1,0:T(8,128)(2,1)S(1)} async-done(((bf16[16,18,1024]{2,1,0:T(8,128)(2,1)}), bf16[16,18,1024]{2,1,0:T(8,128)(2,1)S(1)}, u32[]{:S(2)}, u32[]{:S(2)}) %all-to-all-start.3) | async-done | bytes 589856 | tf_op jit(solution)/shard_map/all_to_all | solution.py:97
  137.3 0.6 copy.13
  138.0 1.8 %gather_fusion = bf16[128,2,1024]{2,1,0:T(2,128)(2,1)S(1)} fusion(bf16[8,2,18,1024]{3,1,2,0:T(2,128)(2,1)S(1)} %copy.11, s32[128]{0:T(128)S(1)} %get-tuple-element.4), kind=kCustom, calls=%fused_computation | custom fusion | bytes 1049600 | tf_op jit(solution)/shard_map/gather | solution.py:48
  139.7 1.8 %gather_fusion.1 = bf16[128,2,1024]{2,1,0:T(2,128)(2,1)S(1)} fusion(bf16[8,2,18,1024]{3,1,2,0:T(2,128)(2,1)S(1)} %copy.13, s32[128]{0:T(128)S(1)} %get-tuple-element.4), kind=kCustom, calls=%fused_computation.1 | custom fusion | bytes 1049600 | tf_op jit(solution)/shard_map/gather | solution.py:48
  141.5 2.8 %convert_reduce_fusion = (bf16[128,1024]{1,0:T(8,128)(2,1)S(1)}, bf16[128,1024]{1,0:T(8,128)(2,1)S(1)}) fusion(bf16[128,2,1024]{2,1,0:T(2,128)(2,1)S(1)} %gather_fusion.1, bf16[128,2,1024]{2,1,0:T(2,128)(2,1)S(1)} %gather_fusion), kind=kLoop, calls=%fused_computation.17 | loop fusion | flops 786432 | bytes 1572864 | tf_op jit(solution)/shard_map/reduce_sum | solution.py:49
  144.3 0.9 select_convert_fusion
  (14 shorter events, 0.2 us)
Async XLA Ops:
  10.6 28.1 %all-to-all-start = ((bf16[16,18,1024]{2,1,0:T(8,128)(2,1)}), bf16[16,18,1024]{2,1,0:T(8,128)(2,1)S(1)}, u32[]{:S(2)}, u32[]{:S(2)}) async-start(bf16[16,18,1024]{2,1,0:T(8,128)(2,1)} %bitcast), calls=%async_computation | async-start | bytes 1572864 | tf_op jit(solution)/shard_map/all_to_all | solution.py:52
  39.6 23.5 %all-to-all-start.2 = ((bf16[16,18,1024]{2,1,0:T(8,128)(2,1)}), bf16[16,18,1024]{2,1,0:T(8,128)(2,1)S(1)}, u32[]{:S(2)}, u32[]{:S(2)}) async-start(bf16[16,18,1024]{2,1,0:T(8,128)(2,1)} %bitcast.2), calls=%async_computation.2 | async-start | bytes 1572864 | tf_op jit(solution)/shard_map/all_to_all | solution.py:68
  44.5 100.7 %reduce-scatter.5.cloned.1.call-start = ((), (), s32[]{:S(2)}) async-start(), calls=%async_computation.7 | async-start | bytes 12582912 | tf_op jit(solution)/shard_map/reduce_scatter | solution.py:74
  70.7 1.7 %copy-start = (f32[288,2048]{1,0:T(8,128)S(1)}, f32[288,2048]{1,0:T(8,128)}, u32[]{:S(2)}) copy-start(f32[288,2048]{1,0:T(8,128)} %fusion.14) | copy-start | bytes 7077892
  70.7 74.5 %reduce-scatter.3.cloned.1.call-start = ((), (), s32[]{:S(2)}) async-start(), calls=%async_computation.6 | async-start | bytes 12582912 | tf_op jit(solution)/shard_map/reduce_scatter | solution.py:86
  76.4 1.0 copy-start.1
  88.7 6.6 %copy-start.2 = (bf16[288,2048]{1,0:T(8,128)(2,1)S(1)}, bf16[288,2048]{1,0:T(8,128)(2,1)}, u32[]{:S(2)}) copy-start(bf16[288,2048]{1,0:T(8,128)(2,1)} %copy-done.1) | copy-start | bytes 3538948
  89.8 24.1 %all-to-all-start.1 = ((bf16[16,18,1024]{2,1,0:T(8,128)(2,1)}), bf16[16,18,1024]{2,1,0:T(8,128)(2,1)S(1)}, u32[]{:S(2)}, u32[]{:S(2)}) async-start(bf16[16,18,1024]{2,1,0:T(8,128)(2,1)} %reshape.43), calls=%async_computation.1 | async-start | bytes 1572864 | tf_op jit(solution)/shard_map/all_to_all | solution.py:65
  99.5 19.2 %copy-start.3 = (s32[128]{0:T(128)S(1)}, s32[128]{0:T(128)}, u32[]{:S(2)}) copy-start(s32[128]{0:T(128)} %param.9) | copy-start | bytes 1540
  113.9 23.5 %all-to-all-start.3 = ((bf16[16,18,1024]{2,1,0:T(8,128)(2,1)}), bf16[16,18,1024]{2,1,0:T(8,128)(2,1)S(1)}, u32[]{:S(2)}, u32[]{:S(2)}) async-start(bf16[16,18,1024]{2,1,0:T(8,128)(2,1)} %reshape.48), calls=%async_computation.3 | async-start | bytes 1572864 | tf_op jit(solution)/shard_map/all_to_all | solution.py:97
Sparse Core Ops, SparseCore 0:
  70.8 16.0 reduce-scatter.4
  89.9 18.0 reduce-scatter.2
where the time goes:
time: 153 us; the launch traced here: 152 us
  waiting for transfers between devices  62.7 us (41%)
  matrix products  31.8 us (21%)
  starting transfers between devices  23.7 us (15%)
  local copies, waits for them, and re-layouts  15.3 us (10%)
  between operations  14.2 us (9%)
  other arithmetic  4.41 us (3%)
    all_to_all x1, waiting for transfers between devices, per_device(): lax.all_to_all(dispatch(tokens), 'lang', split_axis=0, concat_axis=0, til...  18 us
    all_to_all x1, waiting for transfers between devices, per_device(): lax.all_to_all(dx_part, 'lang', split_axis=0, concat_axis=0, tiled=True)  18 us
    all_to_all x1, waiting for transfers between devices, per_device(): lax.all_to_all(dispatch(grad_out), 'lang', split_axis=0, concat_axis=0, t...  13.4 us
    all_to_all x1, waiting for transfers between devices, per_device(): lax.all_to_all(partial_rows, 'lang', split_axis=0, concat_axis=0, tiled=T...  13.3 us
    all_to_all x1, starting transfers between devices, per_device(): lax.all_to_all(dispatch(tokens), 'lang', split_axis=0, concat_axis=0, til...  8.31 us
    dot_general x1, matrix products, per_device(): lax.dot_general(sliced, hidden_flat, (((0,), (0,)), ((), ())), preferred_...  7.35 us
    dot_general x1, matrix products, per_device(): lax.dot_general(sliced, d_pre, (((0,), (0,)), ((), ())), preferred_elemen...  7.28 us
    all_to_all x1, starting transfers between devices, per_device(): lax.all_to_all(partial_rows, 'lang', split_axis=0, concat_axis=0, tiled=T...  5.51 us
  transfers between devices with their start and end apart: 6, of which 4 were waited for; matrix products, arithmetic and copies ran while one was open for 24% of the time, Pallas kernels for 0%

commit v1 on v0

v1 whole, which is shorter than its diff:
```python
import jax
import jax.numpy as jnp
from jax import lax
from jax.sharding import PartitionSpec as P

MODULES = 8
TOK_DEV = 128
CAPACITY = 18
MAIN = 16
LANES = 128

INV_ROOT_TWO = 0.7071067811865476
INV_ROOT_TAU = 0.3989422804014327


def gelu_value(values):
    return 0.5 * values * (1.0 + lax.erf(values * INV_ROOT_TWO))


def gelu_slope(values):
    return (
        0.5 * (1.0 + lax.erf(values * INV_ROOT_TWO))
        + values * jnp.exp(-0.5 * values * values) * INV_ROOT_TAU
    )


def dot(a, b, contract):
    return lax.dot_general(a, b, (contract, ((), ())), preferred_element_type=jnp.float32)


def per_device(tokens, grad_out, lang_ids, slot_ids, w_up, w_down_t):
    n_lang = lax.axis_size("lang")
    n_rep = lax.axis_size("rep")
    groups = n_lang // MODULES
    count, width = tokens.shape
    pieces = width // LANES
    spare = CAPACITY - MAIN
    rows = MODULES * MAIN
    scale = 1.0 / TOK_DEV

    row = lax.broadcasted_iota(jnp.int32, (rows, count), 0)
    lang, place = row // MAIN, row % MAIN
    here = lang == lang_ids[None, :]
    slots = slot_ids[None, :]
    pick_main = (here & (slots == place)).astype(jnp.bfloat16)
    in_spare = here & (slots == MAIN + place // pieces)
    pick_spare = [(in_spare & (place % pieces == p)).astype(jnp.bfloat16) for p in range(pieces)]

    def pack(values):
        main = dot(pick_main, values, ((1,), (0,)))
        extra = sum(
            dot(pick_spare[p], values[:, p * LANES : (p + 1) * LANES], ((1,), (0,)))
            for p in range(pieces)
        )
        return jnp.concatenate([main, extra], axis=1).astype(jnp.bfloat16)

    def collect(packed):
        main = dot(pick_main, packed[:, :width], ((0,), (0,)))
        extra = jnp.concatenate(
            [dot(pick_spare[p], packed[:, width:], ((0,), (0,))) for p in range(pieces)], axis=1
        )
        return (main + extra).astype(jnp.bfloat16)

    def unpack(packed):
        extra = packed[:, width:].reshape(MODULES * spare, width)
        return jnp.concatenate([packed[:, :width], extra], axis=0)

    def repack(full):
        extra = full[rows:].reshape(rows, LANES)
        return jnp.concatenate([full[:rows], extra], axis=1)

    planes = [[g + groups * m for m in range(MODULES)] for g in range(groups)]

    def exchange(packed):
        cut = packed.reshape(MODULES, MAIN, packed.shape[1])
        got = lax.all_to_all(
            cut, "lang", split_axis=0, concat_axis=0, axis_index_groups=planes, tiled=True
        )
        return got.reshape(packed.shape)

    def shift_group(value, step):
        pairs = [
            (m * groups + g, m * groups + (g + step) % groups)
            for m in range(MODULES)
            for g in range(groups)
        ]
        return lax.ppermute(value, "lang", pairs)

    def shift_rep(value, step):
        return lax.ppermute(value, "rep", [(r, (r + step) % n_rep) for r in range(n_rep)])

    def spread(packed):
        return [packed] + [shift_group(packed, s) for s in range(1, groups)]

    def gather_rows(parts):
        return jnp.concatenate([unpack(p) for p in parts], axis=0)

    def reduce_group(partial):
        part_rows = rows + MODULES * spare
        parts = [partial[s * part_rows : (s + 1) * part_rows] for s in range(groups)]
        total = repack(parts[0]).astype(jnp.float32)
        for s in range(1, groups):
            total = total + shift_group(repack(parts[s]), -s).astype(jnp.float32)
        return total.astype(jnp.bfloat16)

    x_rows = gather_rows(spread(exchange(pack(tokens))))
    y_rows = gather_rows(spread(exchange(pack(grad_out))))

    pre = dot(x_rows, w_up, ((1,), (0,)))
    hidden = gelu_value(pre).astype(jnp.bfloat16)
    out_part = dot(hidden, w_down_t, ((1,), (1,))).astype(jnp.bfloat16)
    out_back = exchange(reduce_group(out_part))

    d_hidden = dot(y_rows, w_down_t, ((1,), (0,)))
    d_pre = (d_hidden * gelu_slope(pre)).astype(jnp.bfloat16)
    dx_part = dot(d_pre, w_up, ((1,), (1,))).astype(jnp.bfloat16)
    dx_back = exchange(reduce_group(dx_part))

    own = width // n_rep
    start = lax.axis_index("rep") * own

    def over_reps(value):
        return [value] + [shift_rep(value, s) for s in range(1, n_rep)]

    def weight_grad(left, right):
        lefts = jnp.concatenate(over_reps(left), axis=0)
        lefts = lax.dynamic_slice_in_dim(lefts, start, own, axis=1)
        rights = jnp.concatenate(over_reps(right), axis=0)
        return dot(lefts, rights, ((0,), (0,))) * scale

    grad_down = weight_grad(y_rows, hidden)
    grad_up = weight_grad(x_rows, d_pre)
    return collect(out_back), collect(dx_back), grad_up, grad_down


def solution(mesh):
    placed = (
        P(("lang", "rep"), None),
        P(("lang", "rep"), None),
        P(("lang", "rep")),
        P(("lang", "rep")),
        P(None, "lang"),
        P(None, "lang"),
    )
    return jax.shard_map(
        per_device,
        mesh=mesh,
        in_specs=placed,
        out_specs=(
            P(("lang", "rep"), None),
            P(("lang", "rep"), None),
            P("rep", "lang"),
            P("rep", "lang"),
        ),
        check_vma=False,
    )
```

time: 153 us -> 135 us (0.88)
  waiting for transfers between devices: 62.7 us -> 21.1 us
  matrix products: 31.8 us -> 54 us
  between operations: 14.2 us -> 1.01 us
  other arithmetic: 4.41 us -> 10.4 us
  starting transfers between devices: 23.7 us -> 27.4 us
  local copies, waits for them, and re-layouts: 15.3 us -> 18.9 us
    all_to_all x4, waiting for transfers between devices: 62.6 us -> 16.9 us  [exchange(): lax.all_to_all(cut, 'lang', split_axis=0, concat_axis=0, axis_index_group...]
    dot_general x6 -> x42, matrix products: 31.8 us -> 54 us  [dot(): lax.dot_general(a, b, (contract, ((), ())), preferred_element_type=jnp.fl...]
    ppermute x0 -> x8, starting transfers between devices: none -> 7.05 us  [the longest x4 6.03 us: shift_group(): return lax.ppermute(value, 'lang', pairs)]
    concatenate x1 -> x6, other arithmetic: 0.68 us -> 6.65 us  [the longest x2 3.47 us: repack(): return jnp.concatenate([full[:rows], extra], axis=1)]
    ppermute x0 -> x8, waiting for transfers between devices: none -> 4.22 us  [the longest x4 4.21 us: shift_group(): return lax.ppermute(value, 'lang', pairs)]
    concatenate x0 -> x2, local copies, waits for them, and re-layouts: none -> 3.85 us  [weight_grad(): lefts = jnp.concatenate(over_reps(left), axis=0)]
    unnamed x8 -> x50, local copies, waits for them, and re-layouts: 2.61 us -> 6.36 us
    gather x2 -> x0, local copies, waits for them, and re-layouts: 3.55 us -> none  [collect(): returned.reshape(MODULES, groups, capacity, feature_width)]
  transfers between devices with their start and end apart: 6 -> 12, of which waited for: 4 -> 5; matrix products, arithmetic and copies ran while one was open for 24% -> 43% of each run, Pallas kernels for 0% -> 0%
where the time goes in v1:
time: 135 us; the launch traced here: 133 us
  matrix products  54 us (40%)
  starting transfers between devices  27.4 us (20%)
  waiting for transfers between devices  21.1 us (16%)
  local copies, waits for them, and re-layouts  18.9 us (14%)
  other arithmetic  10.4 us (8%)
    dot_general x42, matrix products, dot(): lax.dot_general(a, b, (contract, ((), ())), preferred_element_type=jnp.fl...  54 us
    all_to_all x4, starting transfers between devices, exchange(): lax.all_to_all(cut, 'lang', split_axis=0, concat_axis=0, axis_index_group...  20.4 us
    all_to_all x4, waiting for transfers between devices, exchange(): lax.all_to_all(cut, 'lang', split_axis=0, concat_axis=0, axis_index_group...  16.9 us
    unnamed x50, local copies, waits for them, and re-layouts  6.36 us
    ppermute x4, starting transfers between devices, shift_group(): return lax.ppermute(value, 'lang', pairs)  6.03 us
    reshape x4, local copies, waits for them, and re-layouts, repack(): extra = full[rows:].reshape(rows, LANES)  5.58 us
    ppermute x4, waiting for transfers between devices, shift_group(): return lax.ppermute(value, 'lang', pairs)  4.21 us
    concatenate x2, local copies, waits for them, and re-layouts, weight_grad(): lefts = jnp.concatenate(over_reps(left), axis=0)  3.85 us
  transfers between devices with their start and end apart: 12, of which 5 were waited for; matrix products, arithmetic and copies ran while one was open for 43% of the time, Pallas kernels for 0%

profile of v1, /device:TPU:0, one launch (start us, length us, event | category | flops | bytes accessed | tf_op | source)
XLA Modules:
  0.0 132.8 jit_solution(14385134476144248223)
XLA Ops:
  6.0 7.3 %all-to-all-start = ((bf16[8,16,1152]{2,1,0:T(8,128)(2,1)}), bf16[8,16,1152]{2,1,0:T(8,128)(2,1)S(1)}, u32[]{:S(2)}, u32[]{:S(2)}) async-start(bf16[8,16,1152]{2,1,0:T(8,128)(2,1)} %pad_maximum_fusion.2), calls=%async_computation | async-start | bytes 589824 | tf_op jit(solution)/shard_map/all_to_all | solution.py:76
  16.7 6.2 %all-to-all-done = bf16[8,16,1152]{2,1,0:T(8,128)(2,1)S(1)} async-done(((bf16[8,16,1152]{2,1,0:T(8,128)(2,1)}), bf16[8,16,1152]{2,1,0:T(8,128)(2,1)S(1)}, u32[]{:S(2)}, u32[]{:S(2)}) %all-to-all-start) | async-done | bytes 294944 | tf_op jit(solution)/shard_map/all_to_all | solution.py:76
  22.9 3.6 %all-to-all-start.2 = ((bf16[8,16,1152]{2,1,0:T(8,128)(2,1)}), bf16[8,16,1152]{2,1,0:T(8,128)(2,1)S(1)}, u32[]{:S(2)}, u32[]{:S(2)}) async-start(bf16[8,16,1152]{2,1,0:T(8,128)(2,1)} %pad_maximum_fusion.4), calls=%async_computation.2 | async-start | bytes 589824 | tf_op jit(solution)/shard_map/all_to_all | solution.py:76
  26.5 1.6 %collective-permute-start = (bf16[128,1152]{1,0:T(8,128)(2,1)S(1)}, bf16[128,1152]{1,0:T(8,128)(2,1)S(1)}, u32[]{:S(2)}, u32[]{:S(2)}) collective-permute-start(bf16[128,1152]{1,0:T(8,128)(2,1)S(1)} %bitcast.19), channel_id=1, source_target_pairs={{0,2},{2,0},{4,6},{6,4},{8,10},{10,8},{12,14},{14,12},{16,18},{18,... | collective-permute-start | bytes 884744 | tf_op jit(solution)/shard_map/ppermute | solution.py:87
  28.0 7.6 %all-to-all-done.2 = bf16[8,16,1152]{2,1,0:T(8,128)(2,1)S(1)} async-done(((bf16[8,16,1152]{2,1,0:T(8,128)(2,1)}), bf16[8,16,1152]{2,1,0:T(8,128)(2,1)S(1)}, u32[]{:S(2)}, u32[]{:S(2)}) %all-to-all-start.2) | async-done | bytes 294944 | tf_op jit(solution)/shard_map/all_to_all | solution.py:76
  35.6 1.5 %collective-permute-start.2 = (bf16[128,1152]{1,0:T(8,128)(2,1)S(1)}, bf16[128,1152]{1,0:T(8,128)(2,1)S(1)}, u32[]{:S(2)}, u32[]{:S(2)}) collective-permute-start(bf16[128,1152]{1,0:T(8,128)(2,1)S(1)} %bitcast.22), channel_id=1, source_target_pairs={{0,2},{2,0},{4,6},{6,4},{8,10},{10,8},{12,14},{14,12},{16,18},{18,... | collective-permute-start | bytes 884744 | tf_op jit(solution)/shard_map/ppermute | solution.py:87
  40.0 2.4 %collective-permute-done.2 = bf16[128,1152]{1,0:T(8,128)(2,1)S(1)} collective-permute-done((bf16[128,1152]{1,0:T(8,128)(2,1)S(1)}, bf16[128,1152]{1,0:T(8,128)(2,1)S(1)}, u32[]{:S(2)}, u32[]{:S(2)}) %collective-permute-start.2) | collective-permute-done | bytes 294944 | tf_op jit(solution)/shard_map/ppermute | solution.py:87
  44.0 3.5 %multiply_convert_fusion = (bf16[288,2048]{1,0:T(8,128)(2,1)S(1)}, f32[288,2048]{1,0:T(8,128)S(1)}) fusion(bf16[1024,2048]{1,0:T(8,128)(2,1)} %param.10, bf16[16,1024]{1,0:T(8,128)(2,1)S(1)} %reshape.64, bf16[128,1024]{1,0:T(8,128)(2,1)S(1)} %get-tuple-element.17, bf16[16,1024]{1,0:T(8,128)(2,1)S(1)} %reshape.63, bf16[128,1024]{1,0:T(8,128)(2,1)S(1)} %get-tuple-element.19), kind=kOutput, calls=%fused_computation.15 | convolution fusion | flops 1213267968 | bytes 8323072 | tf_op jit(solution)/shard_map/dot_general | solution.py:28
  49.1 3.2 %fusion = bf16[288,2048]{1,0:T(8,128)(2,1)S(1)} fusion(bf16[1024,2048]{1,0:T(8,128)(2,1)S(1)} %copy-done.20, f32[288,2048]{1,0:T(8,128)S(1)} %get-tuple-element.21, bf16[16,1024]{1,0:T(8,128)(2,1)S(1)} %reshape.71, bf16[128,1024]{1,0:T(8,128)(2,1)S(1)} %get-tuple-element.13, bf16[16,1024]{1,0:T(8,128)(2,1)S(1)} %reshape.70, ...), kind=kOutput, calls=%fused_computation.4 | convolution fusion | flops 1216217088 | bytes 8323072 | tf_op jit(solution)/shard_map/dot_general | solution.py:28
  62.6 1.7 %pad_maximum_fusion.5 = bf16[128,1152]{1,0:T(8,128)(2,1)} fusion(bf16[128,128]{1,0:T(8,128)(2,1)} %reshape.73, bf16[128,1024]{1,0:T(8,128)(2,1)} %get-tuple-element.5), kind=kLoop, calls=%fused_computation.66 | loop fusion | flops 589824 | bytes 589824 | tf_op jit(solution)/shard_map/concatenate | solution.py:70
  64.3 1.5 %collective-permute-start.3 = (bf16[128,1152]{1,0:T(8,128)(2,1)}, bf16[128,1152]{1,0:T(8,128)(2,1)}, u32[]{:S(2)}, u32[]{:S(2)}) collective-permute-start(bf16[128,1152]{1,0:T(8,128)(2,1)} %pad_maximum_fusion.5), channel_id=1, source_target_pairs={{0,2},{2,0},{4,6},{6,4},{8,10},{10,8},{12,14},{14,12},{16,18},{18,... | collective-permute-start | bytes 884744 | tf_op jit(solution)/shard_map/ppermute | solution.py:87
  70.0 1.7 %pad_maximum_fusion.3 = bf16[128,1152]{1,0:T(8,128)(2,1)} fusion(bf16[128,128]{1,0:T(8,128)(2,1)} %reshape.66, bf16[128,1024]{1,0:T(8,128)(2,1)} %get-tuple-element.9), kind=kLoop, calls=%fused_computation.64 | loop fusion | flops 589824 | bytes 589824 | tf_op jit(solution)/shard_map/concatenate | solution.py:70
  71.7 1.8 %collective-permute-done.3 = bf16[128,1152]{1,0:T(8,128)(2,1)} collective-permute-done((bf16[128,1152]{1,0:T(8,128)(2,1)}, bf16[128,1152]{1,0:T(8,128)(2,1)}, u32[]{:S(2)}, u32[]{:S(2)}) %collective-permute-start.3) | collective-permute-done | bytes 294944 | tf_op jit(solution)/shard_map/ppermute | solution.py:87
  75.0 1.9 %add_convert_fusion = bf16[128,1152]{1,0:T(8,128)(2,1)} fusion(bf16[128,1152]{1,0:T(8,128)(2,1)} %collective-permute-done.3, bf16[128,128]{1,0:T(8,128)(2,1)} %reshape.72, bf16[128,1024]{1,0:T(8,128)(2,1)} %get-tuple-element.4), kind=kLoop, calls=%fused_computation.61 | loop fusion | flops 1032192 | bytes 884736 | tf_op jit(solution)/shard_map/convert_element_type | solution.py:104
  76.9 5.3 %all-to-all-start.3 = ((bf16[8,16,1152]{2,1,0:T(8,128)(2,1)}), bf16[8,16,1152]{2,1,0:T(8,128)(2,1)}, u32[]{:S(2)}, u32[]{:S(2)}) async-start(bf16[8,16,1152]{2,1,0:T(8,128)(2,1)} %bitcast.25), calls=%async_computation.3 | async-start | bytes 589824 | tf_op jit(solution)/shard_map/all_to_all | solution.py:76
  82.2 1.9 %add_convert_fusion.1 = bf16[128,1152]{1,0:T(8,128)(2,1)} fusion(bf16[128,1152]{1,0:T(8,128)(2,1)} %collective-permute-done.1, bf16[128,128]{1,0:T(8,128)(2,1)} %reshape.65, bf16[128,1024]{1,0:T(8,128)(2,1)} %get-tuple-element.8), kind=kLoop, calls=%fused_computation.62 | loop fusion | flops 1032192 | bytes 884736 | tf_op jit(solution)/shard_map/convert_element_type | solution.py:104
  84.0 1.9 %constant_dynamic-update-slice_fusion = bf16[576,1024]{1,0:T(8,128)(2,1)} fusion(bf16[576,1024]{1,0:T(8,128)(2,1)} %constant_dynamic-update-slice_fusion.1, bf16[288,1024]{1,0:T(8,128)(2,1)} %collective-permute-done.4), kind=kLoop, calls=%fused_computation.96 | loop fusion | bytes 1179648 | tf_op jit(solution)/shard_map/concatenate | solution.py:126
  86.0 1.9 %constant_dynamic-update-slice_fusion.5 = bf16[576,1024]{1,0:T(8,128)(2,1)} fusion(bf16[576,1024]{1,0:T(8,128)(2,1)} %constant_dynamic-update-slice_fusion.6, bf16[288,1024]{1,0:T(8,128)(2,1)} %collective-permute-done.6), kind=kLoop, calls=%fused_computation.101 | loop fusion | bytes 1179648 | tf_op jit(solution)/shard_map/concatenate | solution.py:126
  87.9 3.1 %all-to-all-done.3 = bf16[8,16,1152]{2,1,0:T(8,128)(2,1)} async-done(((bf16[8,16,1152]{2,1,0:T(8,128)(2,1)}), bf16[8,16,1152]{2,1,0:T(8,128)(2,1)}, u32[]{:S(2)}, u32[]{:S(2)}) %all-to-all-start.3) | async-done | bytes 294944 | tf_op jit(solution)/shard_map/all_to_all | solution.py:76
  91.0 4.2 %all-to-all-start.1 = ((bf16[8,16,1152]{2,1,0:T(8,128)(2,1)}), bf16[8,16,1152]{2,1,0:T(8,128)(2,1)}, u32[]{:S(2)}, u32[]{:S(2)}) async-start(bf16[8,16,1152]{2,1,0:T(8,128)(2,1)} %bitcast.24), calls=%async_computation.1 | async-start | bytes 589824 | tf_op jit(solution)/shard_map/all_to_all | solution.py:76
  95.3 1.8 %convolution_dynamic-update-slice_fusion.7 = f32[128,1024]{1,0:T(8,128)} fusion(bf16[128,1152]{1,0:T(8,128)(2,1)} %bitcast.9, s32[128]{0:T(128)} %copy-done.10, s32[128]{0:T(128)S(1)} %get-tuple-element.26, pred[128]{0:T(512)(128)(4,1)} %copy-done.13, s32[128]{0:T(128)S(1)} %copy-done.5, s32[128]{0:T(128)S(1)} %copy-done.6, s32[128]{0:T(128)} %copy-done.7, ...), kind=kOutput, calls=%fused_computation.32 | convolution fusion | flops 4636671 | bytes 102400 | tf_op jit(solution)/shard_map/dot_general | solution.py:28
  97.0 1.8 %convolution_dynamic-update-slice_fusion.6 = f32[128,1024]{1,0:T(8,128)} fusion(f32[128,1024]{1,0:T(8,128)} %convolution_dynamic-update-slice_fusion.7, bf16[128,1152]{1,0:T(8,128)(2,1)} %bitcast.9, s32[128]{0:T(128)} %copy-done.10, s32[128]{0:T(128)S(1)} %get-tuple-element.26, pred[128]{0:T(512)(128)(4,1)} %copy-done.13, s32[128]{0:T(128)S(1)} %copy-done.5, ...), kind=kOutput, calls=%fused_computation.31 | convolution fusion | flops 4636672 | bytes 102400 | tf_op jit(solution)/shard_map/dot_general | solution.py:28
  98.8 1.8 %convolution_dynamic-update-slice_fusion.5 = f32[128,1024]{1,0:T(8,128)} fusion(f32[128,1024]{1,0:T(8,128)} %convolution_dynamic-update-slice_fusion.6, bf16[128,1152]{1,0:T(8,128)(2,1)} %bitcast.9, s32[128]{0:T(128)} %copy-done.10, s32[128]{0:T(128)S(1)} %get-tuple-element.26, pred[128]{0:T(512)(128)(4,1)} %copy-done.13, s32[128]{0:T(128)S(1)} %copy-done.5, ...), kind=kOutput, calls=%fused_computation.30 | convolution fusion | flops 4636672 | bytes 102400 | tf_op jit(solution)/shard_map/dot_general | solution.py:28
  100.6 1.7 %convolution_dynamic-update-slice_fusion.4 = f32[128,1024]{1,0:T(8,128)} fusion(f32[128,1024]{1,0:T(8,128)} %convolution_dynamic-update-slice_fusion.5, bf16[128,1152]{1,0:T(8,128)(2,1)} %bitcast.9, s32[128]{0:T(128)S(1)} %copy-done.11, s32[128]{0:T(128)S(1)} %get-tuple-element.26, pred[128]{0:T(512)(128)(4,1)S(1)} %copy-done.14, s32[128]{0:T(128)S(1)} %copy-done.5, ...), kind=kOutput, calls=%fused_computation.29 | convolution fusion | flops 4636672 | bytes 101632 | tf_op jit(solution)/shard_map/dot_general | solution.py:28
  102.3 1.7 %convolution_dynamic-update-slice_fusion.3 = f32[128,1024]{1,0:T(8,128)} fusion(f32[128,1024]{1,0:T(8,128)} %convolution_dynamic-update-slice_fusion.4, bf16[128,1152]{1,0:T(8,128)(2,1)} %bitcast.9, s32[128]{0:T(128)S(1)} %copy-done.11, s32[128]{0:T(128)S(1)} %get-tuple-element.26, pred[128]{0:T(512)(128)(4,1)S(1)} %copy-done.14, s32[128]{0:T(128)S(1)} %copy-done.5, ...), kind=kOutput, calls=%fused_computation.28 | convolution fusion | flops 4636672 | bytes 101632 | tf_op jit(solution)/shard_map/dot_general | solution.py:28
  104.0 1.7 %convolution_dynamic-update-slice_fusion.2 = f32[128,1024]{1,0:T(8,128)} fusion(f32[128,1024]{1,0:T(8,128)} %convolution_dynamic-update-slice_fusion.3, bf16[128,1152]{1,0:T(8,128)(2,1)} %bitcast.9, s32[128]{0:T(128)S(1)} %copy-done.11, s32[128]{0:T(128)S(1)} %get-tuple-element.26, pred[128]{0:T(512)(128)(4,1)S(1)} %copy-done.14, s32[128]{0:T(128)S(1)} %copy-done.5, ...), kind=kOutput, calls=%fused_computation.27 | convolution fusion | flops 4636672 | bytes 101632 | tf_op jit(solution)/shard_map/dot_general | solution.py:28
  105.8 1.7 %convolution_dynamic-update-slice_fusion.1 = f32[128,1024]{1,0:T(8,128)} fusion(f32[128,1024]{1,0:T(8,128)} %convolution_dynamic-update-slice_fusion.2, bf16[128,1152]{1,0:T(8,128)(2,1)} %bitcast.9, s32[128]{0:T(128)S(1)} %copy-done.11, s32[128]{0:T(128)S(1)} %get-tuple-element.26, pred[128]{0:T(512)(128)(4,1)S(1)} %copy-done.14, s32[128]{0:T(128)S(1)} %copy-done.5, ...), kind=kOutput, calls=%fused_computation.26 | convolution fusion | flops 4636672 | bytes 101632 | tf_op jit(solution)/shard_map/dot_general | solution.py:28
  107.5 1.7 %convolution_dynamic-update-slice_fusion = f32[128,1024]{1,0:T(8,128)} fusion(f32[128,1024]{1,0:T(8,128)} %convolution_dynamic-update-slice_fusion.1, bf16[128,1152]{1,0:T(8,128)(2,1)} %bitcast.9, s32[128]{0:T(128)S(1)} %copy-done.11, s32[128]{0:T(128)S(1)} %get-tuple-element.26, pred[128]{0:T(512)(128)(4,1)S(1)} %copy-done.14, s32[128]{0:T(128)S(1)} %copy-done.5, ...), kind=kOutput, calls=%fused_computation.25 | convolution fusion | flops 4636672 | bytes 101632 | tf_op jit(solution)/shard_map/dot_general | solution.py:28
  118.3 2.2 %fusion.12 = bf16[128,1024]{1,0:T(8,128)(2,1)} fusion(f32[128,1024]{1,0:T(8,128)} %convolution_dynamic-update-slice_fusion, bf16[128,1152]{1,0:T(8,128)(2,1)} %bitcast.9, s32[128]{0:T(128)S(1)} %copy-done.12, s32[128]{0:T(128)S(1)} %get-tuple-element.26, s32[128]{0:T(128)S(1)} %copy-done.5, s32[128]{0:T(128)S(1)} %copy-done.6, s32[128]{0:T(128)S(1)} %copy-done.9, ...), kind=kOutput, calls=%fused_computation.22 | convolution fusion | flops 33898496 | bytes 1051904 | tf_op jit(solution)/shard_map/dot_general | solution.py:28
  120.5 2.1 %fusion.11 = bf16[128,1024]{1,0:T(8,128)(2,1)} fusion(f32[128,1024]{1,0:T(8,128)S(1)} %convolution_dynamic-update-slice_fusion.8, bf16[128,1152]{1,0:T(8,128)(2,1)} %bitcast.4, s32[128]{0:T(128)S(1)} %copy-done.12, s32[128]{0:T(128)S(1)} %get-tuple-element.26, s32[128]{0:T(128)S(1)} %copy-done.5, s32[128]{0:T(128)S(1)} %copy-done.6, s32[128]{0:T(128)S(1)} %copy-done.9, ...), kind=kOutput, calls=%fused_computation.21 | convolution fusion | flops 33898496 | bytes 1051904 | tf_op jit(solution)/shard_map/dot_general | solution.py:28
  122.6 5.3 %convolution_multiply_fusion.1 = f32[512,2048]{1,0:T(8,128)} fusion(bf16[288,2048]{1,0:T(8,128)(2,1)} %collective-permute-done.5, bf16[288,2048]{1,0:T(8,128)(2,1)S(1)} %fusion, bf16[576,1024]{1,0:T(8,128)(2,1)} %constant_dynamic-update-slice_fusion, s32[]{:T(128)S(6)} %select_n.73), kind=kOutput, calls=%fused_computation.2 | convolution fusion | flops 1213726720 | bytes 7143428 | tf_op jit(solution)/shard_map/dot_general | solution.py:28
  127.9 4.9 %convolution_multiply_fusion = f32[512,2048]{1,0:T(8,128)} fusion(bf16[288,2048]{1,0:T(8,128)(2,1)S(1)} %collective-permute-done.7, bf16[288,2048]{1,0:T(8,128)(2,1)S(1)} %get-tuple-element.20, bf16[576,1024]{1,0:T(8,128)(2,1)} %constant_dynamic-update-slice_fusion.5, s32[]{:T(128)S(6)} %select_n.73), kind=kOutput, calls=%fused_computation.1 | convolution fusion | flops 1213726720 | bytes 7143428 | tf_op jit(solution)/shard_map/dot_general | solution.py:28
  (113 shorter events, 39.6 us)
Async XLA Ops:
  0.6 2.5 %copy-start.5 = (s32[128]{0:T(128)S(1)}, s32[128]{0:T(128)}, u32[]{:S(2)}) copy-start(s32[128]{0:T(128)} %param.9) | copy-start | bytes 1540
  0.6 2.5 %copy-start.6 = (s32[128]{0:T(128)S(1)}, s32[128]{0:T(128)}, u32[]{:S(2)}) copy-start(s32[128]{0:T(128)} %param.8) | copy-start | bytes 1540
  0.7 2.5 %copy-start.3 = (bf16[128,1024]{1,0:T(8,128)(2,1)S(1)}, bf16[128,1024]{1,0:T(8,128)(2,1)}, u32[]{:S(2)}) copy-start(bf16[128,1024]{1,0:T(8,128)(2,1)} %param.6) | copy-start | bytes 786436
  0.7 14.9 %copy-start.7 = (s32[128]{0:T(128)}, s32[128]{0:T(128)S(1)}, u32[]{:S(2)}) copy-start(s32[128]{0:T(128)S(1)} %get-tuple-element.24) | copy-start | bytes 1540
  0.7 14.9 %copy-start.10 = (s32[128]{0:T(128)}, s32[128]{0:T(128)S(1)}, u32[]{:S(2)}) copy-start(s32[128]{0:T(128)S(1)} %get-tuple-element.25) | copy-start | bytes 1540
  0.7 14.8 %copy-start.13 = (pred[128]{0:T(512)(128)(4,1)}, pred[128]{0:T(512)(128)(4,1)S(1)}, u32[]{:S(2)}) copy-start(pred[128]{0:T(512)(128)(4,1)S(1)} %get-tuple-element.22) | copy-start | bytes 388
  0.7 14.8 %copy-start.16 = (pred[128]{0:T(512)(128)(4,1)}, pred[128]{0:T(512)(128)(4,1)S(1)}, u32[]{:S(2)}) copy-start(pred[128]{0:T(512)(128)(4,1)S(1)} %get-tuple-element.23) | copy-start | bytes 388
  4.6 8.6 %copy-start.4 = (bf16[128,1024]{1,0:T(8,128)(2,1)S(1)}, bf16[128,1024]{1,0:T(8,128)(2,1)}, u32[]{:S(2)}) copy-start(bf16[128,1024]{1,0:T(8,128)(2,1)} %param.7) | copy-start | bytes 786436
  6.0 16.9 %all-to-all-start = ((bf16[8,16,1152]{2,1,0:T(8,128)(2,1)}), bf16[8,16,1152]{2,1,0:T(8,128)(2,1)S(1)}, u32[]{:S(2)}, u32[]{:S(2)}) async-start(bf16[8,16,1152]{2,1,0:T(8,128)(2,1)} %pad_maximum_fusion.2), calls=%async_computation | async-start | bytes 589824 | tf_op jit(solution)/shard_map/all_to_all | solution.py:76
  22.9 12.8 %all-to-all-start.2 = ((bf16[8,16,1152]{2,1,0:T(8,128)(2,1)}), bf16[8,16,1152]{2,1,0:T(8,128)(2,1)S(1)}, u32[]{:S(2)}, u32[]{:S(2)}) async-start(bf16[8,16,1152]{2,1,0:T(8,128)(2,1)} %pad_maximum_fusion.4), calls=%async_computation.2 | async-start | bytes 589824 | tf_op jit(solution)/shard_map/all_to_all | solution.py:76
  26.5 13.5 %collective-permute-start = (bf16[128,1152]{1,0:T(8,128)(2,1)S(1)}, bf16[128,1152]{1,0:T(8,128)(2,1)S(1)}, u32[]{:S(2)}, u32[]{:S(2)}) collective-permute-start(bf16[128,1152]{1,0:T(8,128)(2,1)S(1)} %bitcast.19), channel_id=1, source_target_pairs={{0,2},{2,0},{4,6},{6,4},{8,10},{10,8},{12,14},{14,12},{16,18},{18,... | collective-permute-start | bytes 884744 | tf_op jit(solution)/shard_map/ppermute | solution.py:87
  35.6 6.7 %collective-permute-start.2 = (bf16[128,1152]{1,0:T(8,128)(2,1)S(1)}, bf16[128,1152]{1,0:T(8,128)(2,1)S(1)}, u32[]{:S(2)}, u32[]{:S(2)}) collective-permute-start(bf16[128,1152]{1,0:T(8,128)(2,1)S(1)} %bitcast.22), channel_id=1, source_target_pairs={{0,2},{2,0},{4,6},{6,4},{8,10},{10,8},{12,14},{14,12},{16,18},{18,... | collective-permute-start | bytes 884744 | tf_op jit(solution)/shard_map/ppermute | solution.py:87
  40.0 7.5 %copy-start.1 = (bf16[16,1024]{1,0:T(8,128)(2,1)}, bf16[16,1024]{1,0:T(8,128)(2,1)S(1)}, u32[]{:S(2)}) copy-start(bf16[16,1024]{1,0:T(8,128)(2,1)S(1)} %reshape.64) | copy-start | bytes 98308
  42.4 6.7 %copy-start = (bf16[16,1024]{1,0:T(8,128)(2,1)}, bf16[16,1024]{1,0:T(8,128)(2,1)S(1)}, u32[]{:S(2)}) copy-start(bf16[16,1024]{1,0:T(8,128)(2,1)S(1)} %reshape.71) | copy-start | bytes 98308
  44.0 5.1 %copy-start.20 = (bf16[1024,2048]{1,0:T(8,128)(2,1)S(1)}, bf16[1024,2048]{1,0:T(8,128)(2,1)}, u32[]{:S(2)}) copy-start(bf16[1024,2048]{1,0:T(8,128)(2,1)} %param.11) | copy-start | bytes 12582916
  49.1 3.2 %copy-start.19 = (bf16[1024,2048]{1,0:T(8,128)(2,1)S(1)}, bf16[1024,2048]{1,0:T(8,128)(2,1)}, u32[]{:S(2)}) copy-start(bf16[1024,2048]{1,0:T(8,128)(2,1)} %param.10) | copy-start | bytes 12582916
  58.1 64.4 %collective-permute-start.5 = (bf16[288,2048]{1,0:T(8,128)(2,1)S(1)}, bf16[288,2048]{1,0:T(8,128)(2,1)}, u32[]{:S(2)}, u32[]{:S(2)}) collective-permute-start(bf16[288,2048]{1,0:T(8,128)(2,1)S(1)} %fusion), channel_id=1, source_target_pairs={{0,1},{1,0},{2,3},{3,2},{4,5},{5,4},{6,7},{7,6},{8,9},{9,8},{10,11... | collective-permute-start | bytes 3538952 | tf_op jit(solution)/shard_map/ppermute | solution.py:90
  58.1 69.7 %collective-permute-start.7 = (bf16[288,2048]{1,0:T(8,128)(2,1)S(1)}, bf16[288,2048]{1,0:T(8,128)(2,1)S(1)}, u32[]{:S(2)}, u32[]{:S(2)}) collective-permute-start(bf16[288,2048]{1,0:T(8,128)(2,1)S(1)} %get-tuple-element.20), channel_id=1, source_target_pairs={{0,1},{1,0},{2,3},{3,2},{4,5},{5,4},{6,7},{7,6},{8,9},{9,8},{10,11... | collective-permute-start | bytes 3538952 | tf_op jit(solution)/shard_map/ppermute | solution.py:90
  59.3 24.8 %collective-permute-start.4 = (bf16[288,1024]{1,0:T(8,128)(2,1)}, bf16[288,1024]{1,0:T(8,128)(2,1)}, u32[]{:S(2)}, u32[]{:S(2)}) collective-permute-start(bf16[288,1024]{1,0:T(8,128)(2,1)} %pad_maximum_fusion), channel_id=1, source_target_pairs={{0,1},{1,0},{2,3},{3,2},{4,5},{5,4},{6,7},{7,6},{8,9},{9,8},{10,11... | collective-permute-start | bytes 1769480 | tf_op jit(solution)/shard_map/ppermute | solution.py:90
  59.3 26.7 %collective-permute-start.6 = (bf16[288,1024]{1,0:T(8,128)(2,1)}, bf16[288,1024]{1,0:T(8,128)(2,1)}, u32[]{:S(2)}, u32[]{:S(2)}) collective-permute-start(bf16[288,1024]{1,0:T(8,128)(2,1)} %pad_maximum_fusion.1), channel_id=1, source_target_pairs={{0,1},{1,0},{2,3},{3,2},{4,5},{5,4},{6,7},{7,6},{8,9},{9,8},{10,11... | collective-permute-start | bytes 1769480 | tf_op jit(solution)/shard_map/ppermute | solution.py:90
  64.3 9.2 %collective-permute-start.3 = (bf16[128,1152]{1,0:T(8,128)(2,1)}, bf16[128,1152]{1,0:T(8,128)(2,1)}, u32[]{:S(2)}, u32[]{:S(2)}) collective-permute-start(bf16[128,1152]{1,0:T(8,128)(2,1)} %pad_maximum_fusion.5), channel_id=1, source_target_pairs={{0,2},{2,0},{4,6},{6,4},{8,10},{10,8},{12,14},{14,12},{16,18},{18,... | collective-permute-start | bytes 884744 | tf_op jit(solution)/shard_map/ppermute | solution.py:87
  73.5 8.6 %collective-permute-start.1 = (bf16[128,1152]{1,0:T(8,128)(2,1)}, bf16[128,1152]{1,0:T(8,128)(2,1)}, u32[]{:S(2)}, u32[]{:S(2)}) collective-permute-start(bf16[128,1152]{1,0:T(8,128)(2,1)} %pad_maximum_fusion.3), channel_id=1, source_target_pairs={{0,2},{2,0},{4,6},{6,4},{8,10},{10,8},{12,14},{14,12},{16,18},{18,... | collective-permute-start | bytes 884744 | tf_op jit(solution)/shard_map/ppermute | solution.py:87
  76.9 14.1 %all-to-all-start.3 = ((bf16[8,16,1152]{2,1,0:T(8,128)(2,1)}), bf16[8,16,1152]{2,1,0:T(8,128)(2,1)}, u32[]{:S(2)}, u32[]{:S(2)}) async-start(bf16[8,16,1152]{2,1,0:T(8,128)(2,1)} %bitcast.25), calls=%async_computation.3 | async-start | bytes 589824 | tf_op jit(solution)/shard_map/all_to_all | solution.py:76
  91.0 18.3 %all-to-all-start.1 = ((bf16[8,16,1152]{2,1,0:T(8,128)(2,1)}), bf16[8,16,1152]{2,1,0:T(8,128)(2,1)}, u32[]{:S(2)}, u32[]{:S(2)}) async-start(bf16[8,16,1152]{2,1,0:T(8,128)(2,1)} %bitcast.24), calls=%async_computation.1 | async-start | bytes 589824 | tf_op jit(solution)/shard_map/all_to_all | solution.py:76
  95.2 5.3 %copy-start.8 = (s32[128]{0:T(128)S(1)}, s32[128]{0:T(128)}, u32[]{:S(2)}) copy-start(s32[128]{0:T(128)} %copy-done.7) | copy-start | bytes 1540
  95.2 5.3 %copy-start.11 = (s32[128]{0:T(128)S(1)}, s32[128]{0:T(128)}, u32[]{:S(2)}) copy-start(s32[128]{0:T(128)} %copy-done.10) | copy-start | bytes 1540
  95.2 5.3 %copy-start.14 = (pred[128]{0:T(512)(128)(4,1)S(1)}, pred[128]{0:T(512)(128)(4,1)}, u32[]{:S(2)}) copy-start(pred[128]{0:T(512)(128)(4,1)} %copy-done.13) | copy-start | bytes 388
  95.3 5.3 %copy-start.17 = (pred[128]{0:T(512)(128)(4,1)S(1)}, pred[128]{0:T(512)(128)(4,1)}, u32[]{:S(2)}) copy-start(pred[128]{0:T(512)(128)(4,1)} %copy-done.16) | copy-start | bytes 388
  109.3 4.5 %copy-start.9 = (s32[128]{0:T(128)S(1)}, s32[128]{0:T(128)}, u32[]{:S(2)}) copy-start(s32[128]{0:T(128)} %copy-done.7) | copy-start | bytes 1540
  109.3 4.5 %copy-start.12 = (s32[128]{0:T(128)S(1)}, s32[128]{0:T(128)}, u32[]{:S(2)}) copy-start(s32[128]{0:T(128)} %copy-done.10) | copy-start | bytes 1540
  109.3 4.5 %copy-start.15 = (pred[128]{0:T(512)(128)(4,1)S(1)}, pred[128]{0:T(512)(128)(4,1)}, u32[]{:S(2)}) copy-start(pred[128]{0:T(512)(128)(4,1)} %copy-done.13) | copy-start | bytes 388
  109.3 4.5 %copy-start.18 = (pred[128]{0:T(512)(128)(4,1)S(1)}, pred[128]{0:T(512)(128)(4,1)}, u32[]{:S(2)}) copy-start(pred[128]{0:T(512)(128)(4,1)} %copy-done.16) | copy-start | bytes 388
  (1 other events, 2.0 us)

commit v2 on v1

v2 whole, which is shorter than its diff:
```python
import functools

import jax
import jax.numpy as jnp
from jax import lax
from jax.experimental import pallas as pl
from jax.experimental.pallas import tpu as pltpu
from jax.sharding import PartitionSpec as P

MODULES = 8
TOK_DEV = 128
CAPACITY = 18
MAIN = 16
LANES = 128
SPARE = CAPACITY - MAIN
ROWS = MODULES * MAIN
PART = MODULES * CAPACITY

INV_ROOT_TWO = 0.7071067811865476
INV_ROOT_TAU = 0.3989422804014327


def gelu_value(values):
    return 0.5 * values * (1.0 + lax.erf(values * INV_ROOT_TWO))


def gelu_slope(values):
    return (
        0.5 * (1.0 + lax.erf(values * INV_ROOT_TWO))
        + values * jnp.exp(-0.5 * values * values) * INV_ROOT_TAU
    )


def dot(a, b, contract):
    return lax.dot_general(a, b, (contract, ((), ())), preferred_element_type=jnp.float32)


def piece_order():
    place = lax.broadcasted_iota(jnp.int32, (LANES, LANES), 0)
    column = lax.broadcasted_iota(jnp.int32, (LANES, LANES), 1)
    return ((place & 15) * 8 + (place >> 4) == column).astype(jnp.bfloat16)


def spare_rows(cut):
    ordered = dot(piece_order(), cut, ((1,), (0,))).astype(jnp.bfloat16)
    return jnp.concatenate([ordered[16 * p : 16 * (p + 1)] for p in range(8)], axis=1)


def spare_cut(rows):
    ordered = jnp.concatenate([rows[:, LANES * p : LANES * (p + 1)] for p in range(8)], axis=0)
    return dot(piece_order(), ordered, ((0,), (0,))).astype(jnp.bfloat16)


def slot_picks(lang_ref, slot_ref):
    count = lang_ref.shape[1]
    row = lax.broadcasted_iota(jnp.int32, (PART, count), 0)
    is_main = row < ROWS
    lang = jnp.where(is_main, row >> 4, (row - ROWS) >> 1)
    slot = jnp.where(is_main, row & 15, MAIN + (row & 1))
    hit = (lang == lang_ref[...]) & (slot == slot_ref[...])
    return hit.astype(jnp.bfloat16)


def pack_kernel(lang_ref, slot_ref, values_ref, packed_ref):
    width = values_ref.shape[1]
    rows = dot(slot_picks(lang_ref, slot_ref), values_ref[...], ((1,), (0,))).astype(jnp.bfloat16)
    packed_ref[:, :width] = rows[:ROWS]
    packed_ref[:, width:] = spare_cut(rows[ROWS:])


def unpack_kernel(packed_ref, rows_ref):
    width = rows_ref.shape[1]
    rows_ref[:ROWS] = packed_ref[:, :width]
    rows_ref[ROWS:] = spare_rows(packed_ref[:, width:])


def sum_pack_kernel(*refs):
    packed_ref = refs[-1]
    total = refs[0][...].astype(jnp.float32)
    for ref in refs[1:-1]:
        total = total + ref[...].astype(jnp.float32)
    total = total.astype(jnp.bfloat16)
    width = total.shape[1]
    packed_ref[:, :width] = total[:ROWS]
    packed_ref[:, width:] = spare_cut(total[ROWS:])


def collect_kernel(lang_ref, slot_ref, packed_ref, values_ref):
    width = values_ref.shape[1]
    rows = jnp.concatenate([packed_ref[:, :width], spare_rows(packed_ref[:, width:])], axis=0)
    picked = dot(slot_picks(lang_ref, slot_ref), rows, ((0,), (0,)))
    values_ref[...] = picked.astype(jnp.bfloat16)


def weight_grad_kernel(n_parts, start_ref, *refs):
    lefts, rights = refs[:n_parts], refs[n_parts : 2 * n_parts]
    out_ref, turned = refs[2 * n_parts :]
    own = out_ref.shape[0]

    @pl.when(pl.program_id(0) == 0)
    def _():
        columns = pl.ds(pl.multiple_of(start_ref[0], LANES), own)
        left = jnp.concatenate([ref[:, columns] for ref in lefts], axis=0)
        turned[...] = left.T

    right = jnp.concatenate([ref[...] for ref in rights], axis=0)
    out_ref[...] = dot(turned[...], right, ((1,), (0,))) * (1.0 / TOK_DEV)


def in_vmem(kernel, out_shape, cost=0):
    return pl.pallas_call(
        kernel,
        out_shape=out_shape,
        cost_estimate=pl.CostEstimate(flops=cost, bytes_accessed=1 << 20, transcendentals=0),
    )


def weight_grad(start, lefts, rights, own):
    n_parts = len(lefts)
    units = rights[0].shape[1]
    depth = sum(left.shape[0] for left in lefts)
    tile = min(512, units)
    if n_parts > 4:
        left = lax.dynamic_slice_in_dim(jnp.concatenate(lefts, axis=0), start, own, axis=1)
        return dot(left, jnp.concatenate(rights, axis=0), ((0,), (0,))) * (1.0 / TOK_DEV)
    return pl.pallas_call(
        functools.partial(weight_grad_kernel, n_parts),
        out_shape=jax.ShapeDtypeStruct((own, units), jnp.float32),
        grid=(units // tile,),
        in_specs=[pl.BlockSpec(memory_space=pltpu.SMEM)]
        + [pl.BlockSpec(left.shape, lambda i: (0, 0)) for left in lefts]
        + [pl.BlockSpec((right.shape[0], tile), lambda i: (0, i)) for right in rights],
        out_specs=pl.BlockSpec((own, tile), lambda i: (0, i)),
        scratch_shapes=[pltpu.VMEM((own, depth), jnp.bfloat16)],
        cost_estimate=pl.CostEstimate(
            flops=2 * own * depth * units, bytes_accessed=4 * own * units, transcendentals=0
        ),
        compiler_params=pltpu.CompilerParams(vmem_limit_bytes=24 << 20),
    )(start.reshape(1), *lefts, *rights)


def per_device(tokens, grad_out, lang_ids, slot_ids, w_up, w_down_t):
    n_lang = lax.axis_size("lang")
    n_rep = lax.axis_size("rep")
    groups = n_lang // MODULES
    count, width = tokens.shape
    lang_row, slot_row = lang_ids.reshape(1, count), slot_ids.reshape(1, count)
    packed_shape = jax.ShapeDtypeStruct((ROWS, width + LANES), jnp.bfloat16)
    rows_shape = jax.ShapeDtypeStruct((PART, width), jnp.bfloat16)
    values_shape = jax.ShapeDtypeStruct((count, width), jnp.bfloat16)
    planes = [[g + groups * m for m in range(MODULES)] for g in range(groups)]

    def pack(values):
        return in_vmem(pack_kernel, packed_shape)(lang_row, slot_row, values)

    def exchange(packed):
        cut = packed.reshape(MODULES, MAIN, packed.shape[1])
        got = lax.all_to_all(
            cut, "lang", split_axis=0, concat_axis=0, axis_index_groups=planes, tiled=True
        )
        return got.reshape(packed.shape)

    def shift_group(value, step):
        pairs = [
            (m * groups + g, m * groups + (g + step) % groups)
            for m in range(MODULES)
            for g in range(groups)
        ]
        return lax.ppermute(value, "lang", pairs)

    def shift_rep(value, step):
        return lax.ppermute(value, "rep", [(r, (r + step) % n_rep) for r in range(n_rep)])

    def spread(packed):
        rows = in_vmem(unpack_kernel, rows_shape)(packed)
        return [rows] + [shift_group(rows, s) for s in range(1, groups)]

    def send_back(parts):
        sums = [parts[0]] + [shift_group(parts[s], -s) for s in range(1, groups)]
        return exchange(in_vmem(sum_pack_kernel, packed_shape)(*sums))

    def collect(packed):
        return in_vmem(collect_kernel, values_shape)(lang_row, slot_row, packed)

    x_parts = spread(exchange(pack(tokens)))
    y_parts = spread(exchange(pack(grad_out)))

    pre = [dot(x, w_up, ((1,), (0,))) for x in x_parts]
    hidden = [gelu_value(v).astype(jnp.bfloat16) for v in pre]
    out_parts = [dot(h, w_down_t, ((1,), (1,))).astype(jnp.bfloat16) for h in hidden]
    out_back = send_back(out_parts)

    d_hidden = [dot(y, w_down_t, ((1,), (0,))) for y in y_parts]
    d_pre = [(d * gelu_slope(v)).astype(jnp.bfloat16) for d, v in zip(d_hidden, pre)]
    dx_parts = [dot(d, w_up, ((1,), (1,))).astype(jnp.bfloat16) for d in d_pre]
    dx_back = send_back(dx_parts)

    own = width // n_rep
    start = lax.axis_index("rep") * own

    def over_reps(parts):
        return [shift_rep(v, s) if s else v for s in range(n_rep) for v in parts]

    grad_down = weight_grad(start, over_reps(y_parts), over_reps(hidden), own)
    grad_up = weight_grad(start, over_reps(x_parts), over_reps(d_pre), own)
    return collect(out_back), collect(dx_back), grad_up, grad_down


def solution(mesh):
    placed = (
        P(("lang", "rep"), None),
        P(("lang", "rep"), None),
        P(("lang", "rep")),
        P(("lang", "rep")),
        P(None, "lang"),
        P(None, "lang"),
    )
    return jax.shard_map(
        per_device,
        mesh=mesh,
        in_specs=placed,
        out_specs=(
            P(("lang", "rep"), None),
            P(("lang", "rep"), None),
            P("rep", "lang"),
            P("rep", "lang"),
        ),
        check_vma=False,
    )
```

time: 135 us -> 99.7 us (0.74)
  matrix products: 54 us -> 17.4 us
  Pallas kernels: 0 us -> 27 us
  local copies, waits for them, and re-layouts: 18.9 us -> 0.73 us
  other arithmetic: 10.4 us -> 0 us
  waiting for transfers between devices: 21.1 us -> 23.7 us
  starting transfers between devices: 27.4 us -> 29.1 us
    dot_general x42 -> x8, matrix products: 54 us -> 17.4 us  [dot(): lax.dot_general(a, b, (contract, ((), ())), preferred_element_type=jnp.fl...]
    pallas_call x0 -> x10, Pallas kernels: none -> 27 us  [the longest x2 11.2 us: weight_grad(): pl.pallas_call(functools.partial(weight_grad_kernel, n_parts), out_shape=...]
    concatenate x6 -> x0, other arithmetic: 6.65 us -> none  [the longest x2 3.47 us: repack(): return jnp.concatenate([full[:rows], extra], axis=1)]
    reshape x8 -> x0, local copies, waits for them, and re-layouts: 5.66 us -> none  [the longest x4 5.58 us: repack(): extra = full[rows:].reshape(rows, LANES)]
    unnamed x50 -> x12, local copies, waits for them, and re-layouts: 6.36 us -> 0.73 us
    ppermute x4, waiting for transfers between devices: 4.21 us -> 9.22 us  [shift_group(): return lax.ppermute(value, 'lang', pairs)]
    concatenate x2 -> x0, local copies, waits for them, and re-layouts: 3.85 us -> none  [weight_grad(): lefts = jnp.concatenate(over_reps(left), axis=0)]
    convert_element_type x2 -> x0, other arithmetic: 3.74 us -> none  [reduce_group(): return total.astype(jnp.bfloat16)]
  transfers between devices with their start and end apart: 12 -> 16, of which waited for: 5 -> 5; matrix products, arithmetic and copies ran while one was open for 43% -> 18% of each run, Pallas kernels for 0% -> 23%
where the time goes in v2:
time: 99.7 us; the launch traced here: 98.7 us
  starting transfers between devices  29.1 us (29%)
  Pallas kernels  27 us (27%)
  waiting for transfers between devices  23.7 us (24%)
  matrix products  17.4 us (17%)
    all_to_all x4, starting transfers between devices, exchange(): lax.all_to_all(cut, 'lang', split_axis=0, concat_axis=0, axis_index_group...  22.4 us
    dot_general x8, matrix products, dot(): lax.dot_general(a, b, (contract, ((), ())), preferred_element_type=jnp.fl...  17.4 us
    all_to_all x4, waiting for transfers between devices, exchange(): lax.all_to_all(cut, 'lang', split_axis=0, concat_axis=0, axis_index_group...  14.4 us
    pallas_call x2, Pallas kernels, weight_grad(): pl.pallas_call(functools.partial(weight_grad_kernel, n_parts), out_shape=...  11.2 us
    ppermute x4, waiting for transfers between devices, shift_group(): return lax.ppermute(value, 'lang', pairs)  9.22 us
    ppermute x4, starting transfers between devices, shift_group(): return lax.ppermute(value, 'lang', pairs)  5.07 us
    pallas_call x2, Pallas kernels, pack(): return in_vmem(pack_kernel, packed_shape)(lang_row, slot_row, values)  4.1 us
    pallas_call x2, Pallas kernels, collect(): return in_vmem(collect_kernel, values_shape)(lang_row, slot_row, packed)  4.08 us
  transfers between devices with their start and end apart: 16, of which 5 were waited for; matrix products, arithmetic and copies ran while one was open for 18% of the time, Pallas kernels for 23%

profile of v2, /device:TPU:0, one launch (start us, length us, event | category | flops | bytes accessed | tf_op | source)
XLA Modules:
  0.0 98.7 jit_solution(13266495890013174468)
XLA Ops:
  0.6 2.1 %shard_map.97 = bf16[128,1152]{1,0:T(8,128)(2,1)} custom-call(s32[1,128]{1,0:T(1,128)} %bitcast.33, s32[1,128]{1,0:T(1,128)} %bitcast.37, bf16[128,1024]{1,0:T(8,128)(2,1)} %values_ref.3), custom_call_target="tpu_custom_call" | custom-call | bytes 1048576 | tf_op jit(solution)/shard_map/pallas_call | solution.py:154
  2.7 7.3 %all-to-all-start.2 = ((bf16[8,16,1152]{2,1,0:T(8,128)(2,1)}), bf16[8,16,1152]{2,1,0:T(8,128)(2,1)S(1)}, u32[]{:S(2)}, u32[]{:S(2)}) async-start(bf16[8,16,1152]{2,1,0:T(8,128)(2,1)} %bitcast.32), calls=%async_computation.2 | async-start | bytes 589824 | tf_op jit(solution)/shard_map/all_to_all | solution.py:158
  10.0 2.0 %shard_map.93 = bf16[128,1152]{1,0:T(8,128)(2,1)} custom-call(s32[1,128]{1,0:T(1,128)} %bitcast.34, s32[1,128]{1,0:T(1,128)} %bitcast.38, bf16[128,1024]{1,0:T(8,128)(2,1)} %values_ref.2), custom_call_target="tpu_custom_call" | custom-call | bytes 1048576 | tf_op jit(solution)/shard_map/pallas_call | solution.py:154
  12.0 7.6 %all-to-all-done.2 = bf16[8,16,1152]{2,1,0:T(8,128)(2,1)S(1)} async-done(((bf16[8,16,1152]{2,1,0:T(8,128)(2,1)}), bf16[8,16,1152]{2,1,0:T(8,128)(2,1)S(1)}, u32[]{:S(2)}, u32[]{:S(2)}) %all-to-all-start.2) | async-done | bytes 294944 | tf_op jit(solution)/shard_map/all_to_all | solution.py:158
  19.6 3.6 %all-to-all-start = ((bf16[8,16,1152]{2,1,0:T(8,128)(2,1)}), bf16[8,16,1152]{2,1,0:T(8,128)(2,1)S(1)}, u32[]{:S(2)}, u32[]{:S(2)}) async-start(bf16[8,16,1152]{2,1,0:T(8,128)(2,1)} %bitcast.29), calls=%async_computation | async-start | bytes 589824 | tf_op jit(solution)/shard_map/all_to_all | solution.py:158
  23.2 1.8 %shard_map.98.refs_0_ = bf16[144,1024]{1,0:T(8,128)(2,1)} custom-call(bf16[128,1152]{1,0:T(8,128)(2,1)} %bitcast.31), custom_call_target="tpu_custom_call" | custom-call | bytes 1048576 | tf_op jit(solution)/shard_map/pallas_call | solution.py:175
  25.0 1.5 %collective-permute-start.2 = (bf16[144,1024]{1,0:T(8,128)(2,1)}, bf16[144,1024]{1,0:T(8,128)(2,1)}, u32[]{:S(2)}, u32[]{:S(2)}) collective-permute-start(bf16[144,1024]{1,0:T(8,128)(2,1)} %shard_map.98.refs_0_), channel_id=1, source_target_pairs={{0,2},{2,0},{4,6},{6,4},{8,10},{10,8},{12,14},{14,12},{16,18},{18,... | collective-permute-start | bytes 884744 | tf_op jit(solution)/shard_map/ppermute | solution.py:169
  26.5 5.9 %all-to-all-done = bf16[8,16,1152]{2,1,0:T(8,128)(2,1)S(1)} async-done(((bf16[8,16,1152]{2,1,0:T(8,128)(2,1)}), bf16[8,16,1152]{2,1,0:T(8,128)(2,1)S(1)}, u32[]{:S(2)}, u32[]{:S(2)}) %all-to-all-start) | async-done | bytes 294944 | tf_op jit(solution)/shard_map/all_to_all | solution.py:158
  32.4 0.7 copy-done.4
  33.1 1.8 %shard_map.94.refs_0_ = bf16[144,1024]{1,0:T(8,128)(2,1)} custom-call(bf16[128,1152]{1,0:T(8,128)(2,1)} %bitcast.30), custom_call_target="tpu_custom_call" | custom-call | bytes 1048576 | tf_op jit(solution)/shard_map/pallas_call | solution.py:175
  34.9 1.5 %collective-permute-start = (bf16[144,1024]{1,0:T(8,128)(2,1)}, bf16[144,1024]{1,0:T(8,128)(2,1)S(1)}, u32[]{:S(2)}, u32[]{:S(2)}) collective-permute-start(bf16[144,1024]{1,0:T(8,128)(2,1)} %shard_map.94.refs_0_), channel_id=1, source_target_pairs={{0,2},{2,0},{4,6},{6,4},{8,10},{10,8},{12,14},{14,12},{16,18},{18,... | collective-permute-start | bytes 884744 | tf_op jit(solution)/shard_map/ppermute | solution.py:169
  36.4 3.2 %multiply_convert_fusion.1 = (bf16[144,2048]{1,0:T(8,128)(2,1)S(1)}, f32[144,2048]{1,0:T(8,128)S(1)}) fusion(bf16[144,1024]{1,0:T(8,128)(2,1)} %shard_map.94.refs_0_, bf16[1024,2048]{1,0:T(8,128)(2,1)} %param.10), kind=kOutput, calls=%fused_computation.20 | convolution fusion | flops 605454336 | bytes 6258688 | tf_op jit(solution)/shard_map/dot_general | solution.py:35
  39.6 1.3 %fusion.refs_4_ = bf16[144,2048]{1,0:T(8,128)(2,1)S(1)} fusion(bf16[144,1024]{1,0:T(8,128)(2,1)S(1)} %copy-done.1, bf16[1024,2048]{1,0:T(8,128)(2,1)S(1)} %copy-done.3, f32[144,2048]{1,0:T(8,128)S(1)} %get-tuple-element.5), kind=kOutput, calls=%fused_computation.2 | convolution fusion | flops 606928896 | bytes 6258688 | tf_op jit(solution)/shard_map/dot_general | solution.py:35
  40.9 0.9 collective-permute-done.refs_1_
  41.8 0.9 multiply_convert_fusion
  42.8 2.3 %fusion.1.refs_5_ = bf16[144,2048]{1,0:T(8,128)(2,1)S(1)} fusion(bf16[144,1024]{1,0:T(8,128)(2,1)} %collective-permute-done.2.refs_1_, bf16[1024,2048]{1,0:T(8,128)(2,1)S(1)} %copy-done.3, f32[144,2048]{1,0:T(8,128)S(1)} %get-tuple-element.7), kind=kOutput, calls=%fused_computation.3 | convolution fusion | flops 606928896 | bytes 6258688 | tf_op jit(solution)/shard_map/dot_general | solution.py:35
  45.1 1.5 %convolution_convert_fusion = bf16[144,1024]{1,0:T(8,128)(2,1)S(1)} fusion(bf16[144,2048]{1,0:T(8,128)(2,1)S(1)} %fusion.1.refs_5_, bf16[1024,2048]{1,0:T(8,128)(2,1)S(1)} %copy-done.2), kind=kOutput, calls=%fused_computation.6 | convolution fusion | flops 604127232 | bytes 5079040 | tf_op jit(solution)/shard_map/dot_general | solution.py:35
  46.6 1.5 %convolution_convert_fusion.2 = bf16[144,1024]{1,0:T(8,128)(2,1)S(1)} fusion(bf16[144,2048]{1,0:T(8,128)(2,1)S(1)} %get-tuple-element.6.refs_5_, bf16[1024,2048]{1,0:T(8,128)(2,1)S(1)} %copy-done.3), kind=kOutput, calls=%fused_computation.8 | convolution fusion | flops 604127232 | bytes 5079040 | tf_op jit(solution)/shard_map/dot_general | solution.py:35
  48.1 1.6 %collective-permute-start.1 = (bf16[144,1024]{1,0:T(8,128)(2,1)S(1)}, bf16[144,1024]{1,0:T(8,128)(2,1)}, u32[]{:S(2)}, u32[]{:S(2)}) collective-permute-start(bf16[144,1024]{1,0:T(8,128)(2,1)S(1)} %convolution_convert_fusion.2), channel_id=1, source_target_pairs={{0,2},{2,0},{4,6},{6,4},{8,10},{10,8},{12,14},{14,12},{16,18},{18,... | collective-permute-start | bytes 884744 | tf_op jit(solution)/shard_map/ppermute | solution.py:169
  49.7 0.5 collective-permute-start.3
  50.2 2.2 %convolution_convert_fusion.1.refs_0_ = bf16[144,1024]{1,0:T(8,128)(2,1)} fusion(bf16[144,2048]{1,0:T(8,128)(2,1)S(1)} %fusion.refs_4_, bf16[1024,2048]{1,0:T(8,128)(2,1)S(1)} %copy-done.2), kind=kOutput, calls=%fused_computation.7 | convolution fusion | flops 604127232 | bytes 5079040 | tf_op jit(solution)/shard_map/dot_general | solution.py:35
  52.5 8.3 %collective-permute-done.3.refs_1_ = bf16[144,1024]{1,0:T(8,128)(2,1)} collective-permute-done((bf16[144,1024]{1,0:T(8,128)(2,1)S(1)}, bf16[144,1024]{1,0:T(8,128)(2,1)}, u32[]{:S(2)}, u32[]{:S(2)}) %collective-permute-start.3) | collective-permute-done | bytes 294944 | tf_op jit(solution)/shard_map/ppermute | solution.py:169
  60.7 2.0 %shard_map.99 = bf16[128,1152]{1,0:T(8,128)(2,1)} custom-call(bf16[144,1024]{1,0:T(8,128)(2,1)} %convolution_convert_fusion.1.refs_0_, bf16[144,1024]{1,0:T(8,128)(2,1)} %collective-permute-done.3.refs_1_), custom_call_target="tpu_custom_call" | custom-call | bytes 1048576 | tf_op jit(solution)/shard_map/pallas_call | solution.py:180
  62.7 6.5 %all-to-all-start.3 = ((bf16[8,16,1152]{2,1,0:T(8,128)(2,1)}), bf16[8,16,1152]{2,1,0:T(8,128)(2,1)}, u32[]{:S(2)}, u32[]{:S(2)}) async-start(bf16[8,16,1152]{2,1,0:T(8,128)(2,1)} %bitcast.28), calls=%async_computation.3 | async-start | bytes 589824 | tf_op jit(solution)/shard_map/all_to_all | solution.py:158
  70.3 4.4 %convolution_convert_fusion.3.refs_0_ = bf16[144,1024]{1,0:T(8,128)(2,1)} fusion(bf16[144,2048]{1,0:T(8,128)(2,1)S(1)} %get-tuple-element.4.refs_4_, bf16[1024,2048]{1,0:T(8,128)(2,1)} %param.11), kind=kOutput, calls=%fused_computation.9 | convolution fusion | flops 604127232 | bytes 5079040 | tf_op jit(solution)/shard_map/dot_general | solution.py:35
  74.8 2.0 %shard_map.95 = bf16[128,1152]{1,0:T(8,128)(2,1)} custom-call(bf16[144,1024]{1,0:T(8,128)(2,1)} %convolution_convert_fusion.3.refs_0_, bf16[144,1024]{1,0:T(8,128)(2,1)} %collective-permute-done.1.refs_1_), custom_call_target="tpu_custom_call" | custom-call | bytes 1048576 | tf_op jit(solution)/shard_map/pallas_call | solution.py:180
  76.8 1.0 %all-to-all-done.3 = bf16[8,16,1152]{2,1,0:T(8,128)(2,1)} async-done(((bf16[8,16,1152]{2,1,0:T(8,128)(2,1)}), bf16[8,16,1152]{2,1,0:T(8,128)(2,1)}, u32[]{:S(2)}, u32[]{:S(2)}) %all-to-all-start.3) | async-done | bytes 294944 | tf_op jit(solution)/shard_map/all_to_all | solution.py:158
  77.8 5.0 %all-to-all-start.1 = ((bf16[8,16,1152]{2,1,0:T(8,128)(2,1)}), bf16[8,16,1152]{2,1,0:T(8,128)(2,1)}, u32[]{:S(2)}, u32[]{:S(2)}) async-start(bf16[8,16,1152]{2,1,0:T(8,128)(2,1)} %bitcast.27), calls=%async_computation.1 | async-start | bytes 589824 | tf_op jit(solution)/shard_map/all_to_all | solution.py:158
  83.4 5.6 %shard_map.102 = f32[512,2048]{1,0:T(8,128)} custom-call(s32[1]{0:T(128)} %bitcast.10.start_ref, bf16[144,1024]{1,0:T(8,128)(2,1)S(1)} %copy-done.1, bf16[144,1024]{1,0:T(8,128)(2,1)} %collective-permute-done.2.refs_1_, bf16[144,1024]{1,0:T(8,128)(2,1)S(1)} %collective-permute-done.8.refs_2_, bf16[144,1024]{1,0:T(8,128)(2,1)} %collective-permute-done.9.refs_3_, ...), custom_call_target="tpu_custom_call" | custom-call | flops 1207959552 | bytes 4194304 | tf_op jit(solution)/shard_map/pallas_call | solution.py:126
  89.0 5.6 %shard_map.101 = f32[512,2048]{1,0:T(8,128)} custom-call(s32[1]{0:T(128)} %bitcast.10.start_ref, bf16[144,1024]{1,0:T(8,128)(2,1)S(1)} %copy-done, bf16[144,1024]{1,0:T(8,128)(2,1)S(1)} %collective-permute-done.refs_1_, bf16[144,1024]{1,0:T(8,128)(2,1)} %collective-permute-done.4.refs_2_, bf16[144,1024]{1,0:T(8,128)(2,1)} %collective-permute-done.5.refs_3_, ...), custom_call_target="tpu_custom_call" | custom-call | flops 1207959552 | bytes 4194304 | tf_op jit(solution)/shard_map/pallas_call | solution.py:126
  94.6 2.0 %shard_map.100 = bf16[128,1024]{1,0:T(8,128)(2,1)} custom-call(s32[1,128]{1,0:T(1,128)} %bitcast.35, s32[1,128]{1,0:T(1,128)} %bitcast.39, bf16[128,1152]{1,0:T(8,128)(2,1)} %bitcast.9.packed_ref), custom_call_target="tpu_custom_call" | custom-call | bytes 1048576 | tf_op jit(solution)/shard_map/pallas_call | solution.py:183
  96.7 2.0 %shard_map.96 = bf16[128,1024]{1,0:T(8,128)(2,1)} custom-call(s32[1,128]{1,0:T(1,128)} %bitcast.36, s32[1,128]{1,0:T(1,128)} %bitcast.40, bf16[128,1152]{1,0:T(8,128)(2,1)} %bitcast.5.packed_ref), custom_call_target="tpu_custom_call" | custom-call | bytes 1048576 | tf_op jit(solution)/shard_map/pallas_call | solution.py:183
  (30 shorter events, 1.7 us)
Async XLA Ops:
  2.7 16.9 %all-to-all-start.2 = ((bf16[8,16,1152]{2,1,0:T(8,128)(2,1)}), bf16[8,16,1152]{2,1,0:T(8,128)(2,1)S(1)}, u32[]{:S(2)}, u32[]{:S(2)}) async-start(bf16[8,16,1152]{2,1,0:T(8,128)(2,1)} %bitcast.32), calls=%async_computation.2 | async-start | bytes 589824 | tf_op jit(solution)/shard_map/all_to_all | solution.py:158
  19.6 3.6 %copy-start.5 = (bf16[8,16,1152]{2,1,0:T(8,128)(2,1)}, bf16[8,16,1152]{2,1,0:T(8,128)(2,1)S(1)}, u32[]{:S(2)}) copy-start(bf16[8,16,1152]{2,1,0:T(8,128)(2,1)S(1)} %all-to-all-done.2) | copy-start | bytes 884740
  19.6 12.8 %all-to-all-start = ((bf16[8,16,1152]{2,1,0:T(8,128)(2,1)}), bf16[8,16,1152]{2,1,0:T(8,128)(2,1)S(1)}, u32[]{:S(2)}, u32[]{:S(2)}) async-start(bf16[8,16,1152]{2,1,0:T(8,128)(2,1)} %bitcast.29), calls=%async_computation | async-start | bytes 589824 | tf_op jit(solution)/shard_map/all_to_all | solution.py:158
  25.0 44.8 %collective-permute-start.8 = (bf16[144,1024]{1,0:T(8,128)(2,1)}, bf16[144,1024]{1,0:T(8,128)(2,1)S(1)}, u32[]{:S(2)}, u32[]{:S(2)}) collective-permute-start(bf16[144,1024]{1,0:T(8,128)(2,1)} %shard_map.98.refs_0_), channel_id=1, source_target_pairs={{0,1},{1,0},{2,3},{3,2},{4,5},{5,4},{6,7},{7,6},{8,9},{9,8},{10,11... | collective-permute-start | bytes 884744 | tf_op jit(solution)/shard_map/ppermute | solution.py:172
  25.0 17.8 %collective-permute-start.2 = (bf16[144,1024]{1,0:T(8,128)(2,1)}, bf16[144,1024]{1,0:T(8,128)(2,1)}, u32[]{:S(2)}, u32[]{:S(2)}) collective-permute-start(bf16[144,1024]{1,0:T(8,128)(2,1)} %shard_map.98.refs_0_), channel_id=1, source_target_pairs={{0,2},{2,0},{4,6},{6,4},{8,10},{10,8},{12,14},{14,12},{16,18},{18,... | collective-permute-start | bytes 884744 | tf_op jit(solution)/shard_map/ppermute | solution.py:169
  32.4 0.7 copy-start.4
  34.9 4.7 %copy-start.1 = (bf16[144,1024]{1,0:T(8,128)(2,1)S(1)}, bf16[144,1024]{1,0:T(8,128)(2,1)}, u32[]{:S(2)}) copy-start(bf16[144,1024]{1,0:T(8,128)(2,1)} %shard_map.98.refs_0_) | copy-start | bytes 884740
  34.9 4.7 %copy-start.3 = (bf16[1024,2048]{1,0:T(8,128)(2,1)S(1)}, bf16[1024,2048]{1,0:T(8,128)(2,1)}, u32[]{:S(2)}) copy-start(bf16[1024,2048]{1,0:T(8,128)(2,1)} %param.11) | copy-start | bytes 12582916
  34.9 6.9 %collective-permute-start = (bf16[144,1024]{1,0:T(8,128)(2,1)}, bf16[144,1024]{1,0:T(8,128)(2,1)S(1)}, u32[]{:S(2)}, u32[]{:S(2)}) collective-permute-start(bf16[144,1024]{1,0:T(8,128)(2,1)} %shard_map.94.refs_0_), channel_id=1, source_target_pairs={{0,2},{2,0},{4,6},{6,4},{8,10},{10,8},{12,14},{14,12},{16,18},{18,... | collective-permute-start | bytes 884744 | tf_op jit(solution)/shard_map/ppermute | solution.py:169
  39.6 2.3 %copy-start.2 = (bf16[1024,2048]{1,0:T(8,128)(2,1)S(1)}, bf16[1024,2048]{1,0:T(8,128)(2,1)}, u32[]{:S(2)}) copy-start(bf16[1024,2048]{1,0:T(8,128)(2,1)} %param.10) | copy-start | bytes 12582916
  48.1 22.1 %collective-permute-start.1 = (bf16[144,1024]{1,0:T(8,128)(2,1)S(1)}, bf16[144,1024]{1,0:T(8,128)(2,1)}, u32[]{:S(2)}, u32[]{:S(2)}) collective-permute-start(bf16[144,1024]{1,0:T(8,128)(2,1)S(1)} %convolution_convert_fusion.2), channel_id=1, source_target_pairs={{0,2},{2,0},{4,6},{6,4},{8,10},{10,8},{12,14},{14,12},{16,18},{18,... | collective-permute-start | bytes 884744 | tf_op jit(solution)/shard_map/ppermute | solution.py:169
  49.7 11.1 %collective-permute-start.3 = (bf16[144,1024]{1,0:T(8,128)(2,1)S(1)}, bf16[144,1024]{1,0:T(8,128)(2,1)}, u32[]{:S(2)}, u32[]{:S(2)}) collective-permute-start(bf16[144,1024]{1,0:T(8,128)(2,1)S(1)} %convolution_convert_fusion), channel_id=1, source_target_pairs={{0,2},{2,0},{4,6},{6,4},{8,10},{10,8},{12,14},{14,12},{16,18},{18,... | collective-permute-start | bytes 884744 | tf_op jit(solution)/shard_map/ppermute | solution.py:169
  62.7 15.1 %all-to-all-start.3 = ((bf16[8,16,1152]{2,1,0:T(8,128)(2,1)}), bf16[8,16,1152]{2,1,0:T(8,128)(2,1)}, u32[]{:S(2)}, u32[]{:S(2)}) async-start(bf16[8,16,1152]{2,1,0:T(8,128)(2,1)} %bitcast.28), calls=%async_computation.3 | async-start | bytes 589824 | tf_op jit(solution)/shard_map/all_to_all | solution.py:158
  69.2 13.8 %collective-permute-start.10 = (bf16[144,2048]{1,0:T(8,128)(2,1)S(1)}, bf16[144,2048]{1,0:T(8,128)(2,1)}, u32[]{:S(2)}, u32[]{:S(2)}) collective-permute-start(bf16[144,2048]{1,0:T(8,128)(2,1)S(1)} %get-tuple-element.4.refs_4_), channel_id=1, source_target_pairs={{0,1},{1,0},{2,3},{3,2},{4,5},{5,4},{6,7},{7,6},{8,9},{9,8},{10,11... | collective-permute-start | bytes 1769480 | tf_op jit(solution)/shard_map/ppermute | solution.py:172
  69.2 19.7 %collective-permute-start.6 = (bf16[144,2048]{1,0:T(8,128)(2,1)S(1)}, bf16[144,2048]{1,0:T(8,128)(2,1)}, u32[]{:S(2)}, u32[]{:S(2)}) collective-permute-start(bf16[144,2048]{1,0:T(8,128)(2,1)S(1)} %fusion.refs_4_), channel_id=1, source_target_pairs={{0,1},{1,0},{2,3},{3,2},{4,5},{5,4},{6,7},{7,6},{8,9},{9,8},{10,11... | collective-permute-start | bytes 1769480 | tf_op jit(solution)/shard_map/ppermute | solution.py:172
  69.7 19.2 %collective-permute-start.7 = (bf16[144,2048]{1,0:T(8,128)(2,1)S(1)}, bf16[144,2048]{1,0:T(8,128)(2,1)}, u32[]{:S(2)}, u32[]{:S(2)}) collective-permute-start(bf16[144,2048]{1,0:T(8,128)(2,1)S(1)} %fusion.1.refs_5_), channel_id=1, source_target_pairs={{0,1},{1,0},{2,3},{3,2},{4,5},{5,4},{6,7},{7,6},{8,9},{9,8},{10,11... | collective-permute-start | bytes 1769480 | tf_op jit(solution)/shard_map/ppermute | solution.py:172
  69.8 13.5 %collective-permute-start.11 = (bf16[144,2048]{1,0:T(8,128)(2,1)S(1)}, bf16[144,2048]{1,0:T(8,128)(2,1)}, u32[]{:S(2)}, u32[]{:S(2)}) collective-permute-start(bf16[144,2048]{1,0:T(8,128)(2,1)S(1)} %get-tuple-element.6.refs_5_), channel_id=1, source_target_pairs={{0,1},{1,0},{2,3},{3,2},{4,5},{5,4},{6,7},{7,6},{8,9},{9,8},{10,11... | collective-permute-start | bytes 1769480 | tf_op jit(solution)/shard_map/ppermute | solution.py:172
  70.3 12.5 %collective-permute-start.9 = (bf16[144,1024]{1,0:T(8,128)(2,1)}, bf16[144,1024]{1,0:T(8,128)(2,1)}, u32[]{:S(2)}, u32[]{:S(2)}) collective-permute-start(bf16[144,1024]{1,0:T(8,128)(2,1)} %collective-permute-done.2.refs_1_), channel_id=1, source_target_pairs={{0,1},{1,0},{2,3},{3,2},{4,5},{5,4},{6,7},{7,6},{8,9},{9,8},{10,11... | collective-permute-start | bytes 884744 | tf_op jit(solution)/shard_map/ppermute | solution.py:172
  74.8 8.0 %copy-start = (bf16[144,1024]{1,0:T(8,128)(2,1)S(1)}, bf16[144,1024]{1,0:T(8,128)(2,1)}, u32[]{:S(2)}) copy-start(bf16[144,1024]{1,0:T(8,128)(2,1)} %shard_map.94.refs_0_) | copy-start | bytes 884740
  77.8 18.9 %all-to-all-start.1 = ((bf16[8,16,1152]{2,1,0:T(8,128)(2,1)}), bf16[8,16,1152]{2,1,0:T(8,128)(2,1)}, u32[]{:S(2)}, u32[]{:S(2)}) async-start(bf16[8,16,1152]{2,1,0:T(8,128)(2,1)} %bitcast.27), calls=%async_computation.1 | async-start | bytes 589824 | tf_op jit(solution)/shard_map/all_to_all | solution.py:158
  82.8 6.2 %collective-permute-start.4 = (bf16[144,1024]{1,0:T(8,128)(2,1)S(1)}, bf16[144,1024]{1,0:T(8,128)(2,1)}, u32[]{:S(2)}, u32[]{:S(2)}) collective-permute-start(bf16[144,1024]{1,0:T(8,128)(2,1)S(1)} %copy-done), channel_id=1, source_target_pairs={{0,1},{1,0},{2,3},{3,2},{4,5},{5,4},{6,7},{7,6},{8,9},{9,8},{10,11... | collective-permute-start | bytes 884744 | tf_op jit(solution)/shard_map/ppermute | solution.py:172
  83.0 6.0 %collective-permute-start.5 = (bf16[144,1024]{1,0:T(8,128)(2,1)S(1)}, bf16[144,1024]{1,0:T(8,128)(2,1)}, u32[]{:S(2)}, u32[]{:S(2)}) collective-permute-start(bf16[144,1024]{1,0:T(8,128)(2,1)S(1)} %collective-permute-done.refs_1_), channel_id=1, source_target_pairs={{0,1},{1,0},{2,3},{3,2},{4,5},{5,4},{6,7},{7,6},{8,9},{9,8},{10,11... | collective-permute-start | bytes 884744 | tf_op jit(solution)/shard_map/ppermute | solution.py:172

commit v3 on v2

v3 whole, which is shorter than its diff:
```python
import functools

import jax
import jax.numpy as jnp
from jax import lax
from jax.experimental import pallas as pl
from jax.experimental.pallas import tpu as pltpu
from jax.sharding import PartitionSpec as P

MODULES = 8
TOK_DEV = 128
CAPACITY = 18
MAIN = 16
PACK_LIMIT = 60
LANES = 128
SPARE = CAPACITY - MAIN
ROWS = MODULES * MAIN
PART = MODULES * CAPACITY

INV_ROOT_TWO = 0.7071067811865476
INV_ROOT_TAU = 0.3989422804014327


def gelu_share(values):
    return 0.5 * (1.0 + lax.erf(values * INV_ROOT_TWO))


def dot(a, b, contract):
    return lax.dot_general(a, b, (contract, ((), ())), preferred_element_type=jnp.float32)


def piece_order():
    place = lax.broadcasted_iota(jnp.int32, (LANES, LANES), 0)
    column = lax.broadcasted_iota(jnp.int32, (LANES, LANES), 1)
    return ((place & 15) * 8 + (place >> 4) == column).astype(jnp.bfloat16)


def spare_rows(cut):
    ordered = dot(piece_order(), cut, ((1,), (0,))).astype(jnp.bfloat16)
    return jnp.concatenate([ordered[16 * p : 16 * (p + 1)] for p in range(8)], axis=1)


def spare_cut(rows):
    ordered = jnp.concatenate([rows[:, LANES * p : LANES * (p + 1)] for p in range(8)], axis=0)
    return dot(piece_order(), ordered, ((0,), (0,))).astype(jnp.bfloat16)


def slot_picks(lang, slot):
    row = lax.broadcasted_iota(jnp.int32, (PART, lang.shape[1]), 0)
    is_main = row < ROWS
    block = jnp.where(is_main, row >> 4, (row - ROWS) >> 1)
    place = jnp.where(is_main, row & 15, MAIN + (row & 1))
    return ((block == lang) & (place == slot)).astype(jnp.bfloat16)


def pack_kernel(me_ref, *refs):
    sources, outs, staged, arrived = refs[:4], refs[4:9], refs[9:13], refs[13]
    copies = [
        pltpu.make_async_copy(source, stage, arrived.at[i])
        for i, (source, stage) in enumerate(zip(sources, staged))
    ]
    for copy in copies:
        copy.start()
    for copy in copies[:3]:
        copy.wait()
    lang, slot = staged[0][...], staged[1][...]
    width = staged[2].shape[1]
    rows, cut = packed_rows(slot_picks(lang ^ me_ref[0], slot), staged[2][...])
    for z, out_ref in enumerate(outs[:4]):
        out_ref[:, :width] = rows[32 * z : 32 * (z + 1)]
        out_ref[:, width:] = cut[32 * z : 32 * (z + 1)]
    copies[3].wait()
    outs[4][:, :width], outs[4][:, width:] = packed_rows(slot_picks(lang, slot), staged[3][...])


def packed_rows(picks, values):
    rows = dot(picks, values, ((1,), (0,))).astype(jnp.bfloat16)
    return rows[:ROWS], spare_cut(rows[ROWS:])


def split_kernel(*refs):
    low_ref, high_ref = refs[-2:]
    for z, message_ref in enumerate(refs[:-2]):
        low_ref[16 * z : 16 * (z + 1)] = message_ref[:16]
        high_ref[16 * z : 16 * (z + 1)] = message_ref[16:]


def split_kernel(*refs):
    messages, outs = refs[:4], refs[4:]
    for z, message_ref in enumerate(messages):
        for place, out_ref in enumerate(outs):
            out_ref[16 * z : 16 * (z + 1)] = message_ref[16 * place : 16 * (place + 1)]


NEAR = (0, 2, 4, 6, 1, 3, 5, 7)


def put_rows(packed, rows_ref, first):
    width = rows_ref.shape[1]
    rows_ref[first : first + ROWS] = packed[:, :width]
    rows_ref[first + ROWS : first + PART] = spare_rows(packed[:, width:])


def unpack_near_kernel(groups, *refs):
    for g in range(groups):
        packed = jnp.concatenate([refs[g][...], refs[groups + g][...]], axis=0)
        put_rows(packed, refs[-1], PART * g)


def unpack_kernel(me_ref, *refs):
    for g, packed_ref in enumerate(refs[:-1]):
        blocks = [
            packed_ref[pl.ds(pl.multiple_of((me_ref[0] ^ near) * MAIN, MAIN), MAIN)] for near in NEAR
        ]
        put_rows(jnp.concatenate(blocks, axis=0), refs[-1], PART * g)


def put_packed(rows, packed_ref, place_of):
    width = rows.shape[1]
    cut = spare_cut(rows[ROWS:])
    for j, near in enumerate(NEAR):
        at = pl.ds(pl.multiple_of(place_of(near) * MAIN, MAIN), MAIN)
        packed_ref[at, :width] = rows[MAIN * j : MAIN * (j + 1)]
        packed_ref[at, width:] = cut[MAIN * j : MAIN * (j + 1)]


def sum_pack_kernel(me_ref, *refs):
    total = refs[0][...].astype(jnp.float32)
    for ref in refs[1:-1]:
        total = total + ref[...].astype(jnp.float32)
    put_packed(total.astype(jnp.bfloat16), refs[-1], lambda near: me_ref[0] ^ near)


def pack_all_kernel(groups, me_ref, member_ref, rows_ref, packed_ref):
    for s in range(groups):
        member = lax.rem(member_ref[0] + groups - s, groups)
        put_packed(
            rows_ref[PART * s : PART * (s + 1)],
            packed_ref,
            lambda near, member=member: (me_ref[0] ^ near) * groups + member,
        )


def collect_kernel(terms, lang_ref, slot_ref, packed_ref, values_ref):
    width = values_ref.shape[1]
    picks = slot_picks(lang_ref[...], slot_ref[...])
    packed = packed_ref[...]
    if terms > 1:
        total = packed.astype(jnp.float32).reshape(MODULES, terms, MAIN, width + LANES)
        packed = sum(total[:, g] for g in range(terms)).reshape(ROWS, width + LANES)
        packed = packed.astype(jnp.bfloat16)
    rows = jnp.concatenate([packed[:, :width], spare_rows(packed[:, width:])], axis=0)
    values_ref[...] = dot(picks, rows, ((0,), (0,))).astype(jnp.bfloat16)


def weight_grad_kernel(n_parts, start_ref, *refs):
    lefts, rights = refs[:n_parts], refs[n_parts : 2 * n_parts]
    out_ref, turned = refs[2 * n_parts :]
    own, tile = out_ref.shape
    step = pl.program_id(0)

    @pl.when(step == 0)
    def _():
        columns = pl.ds(pl.multiple_of(start_ref[0], LANES), own)
        turned[...] = jnp.concatenate([ref[:, columns] for ref in lefts], axis=0).T

    units = pl.ds(pl.multiple_of(step * tile, LANES), tile)
    right = jnp.concatenate([ref[:, units] for ref in rights], axis=0)
    out_ref[...] = dot(turned[...], right, ((1,), (0,))) * (1.0 / TOK_DEV)


VMEM_SPEC = pl.BlockSpec(memory_space=pltpu.VMEM)
SMEM_SPEC = pl.BlockSpec(memory_space=pltpu.SMEM)
FREE = pl.CostEstimate(flops=0, bytes_accessed=0, transcendentals=0)


def shapes_of(shapes):
    return [jax.ShapeDtypeStruct(shape, jnp.bfloat16) for shape in shapes]


def local(kernel, shapes, *operands, scalars=0):
    return pl.pallas_call(
        kernel,
        out_shape=shapes_of(shapes),
        in_specs=[SMEM_SPEC] * scalars + [VMEM_SPEC] * (len(operands) - scalars),
        out_specs=[VMEM_SPEC] * len(shapes),
        cost_estimate=FREE,
        compiler_params=pltpu.CompilerParams(vmem_limit_bytes=4 << 20),
    )(*operands)


def pack(me, lang_row, slot_row, tokens, grad_out):
    sources = (lang_row, slot_row, tokens, grad_out)
    packed_width = tokens.shape[1] + LANES
    return pl.pallas_call(
        pack_kernel,
        out_shape=shapes_of([(32, packed_width)] * 4 + [(ROWS, packed_width)]),
        in_specs=[SMEM_SPEC] + [pl.BlockSpec(memory_space=pltpu.HBM)] * 4,
        out_specs=[VMEM_SPEC] * 5,
        scratch_shapes=[pltpu.VMEM(v.shape, v.dtype) for v in sources]
        + [pltpu.SemaphoreType.DMA((4,))],
        cost_estimate=FREE,
        compiler_params=pltpu.CompilerParams(vmem_limit_bytes=PACK_LIMIT << 20),
    )(me, *sources)


def after(values, *earlier):
    return lax.optimization_barrier((*values, *earlier))[: len(values)]


def weight_grad(start, lefts, rights, own):
    n_parts = len(lefts)
    units = rights[0].shape[1]
    depth = sum(left.shape[0] for left in lefts)
    tile = min(512, units)
    if n_parts > 4:
        left = lax.dynamic_slice_in_dim(jnp.concatenate(lefts, axis=0), start, own, axis=1)
        return dot(left, jnp.concatenate(rights, axis=0), ((0,), (0,))) * (1.0 / TOK_DEV)
    return pl.pallas_call(
        functools.partial(weight_grad_kernel, n_parts),
        out_shape=jax.ShapeDtypeStruct((own, units), jnp.float32),
        grid=(units // tile,),
        in_specs=[SMEM_SPEC] + [VMEM_SPEC] * (2 * n_parts),
        out_specs=pl.BlockSpec((own, tile), lambda i: (0, i)),
        scratch_shapes=[pltpu.VMEM((own, depth), jnp.bfloat16)],
        cost_estimate=pl.CostEstimate(
            flops=2 * own * depth * units, bytes_accessed=4 * own * units, transcendentals=0
        ),
        compiler_params=pltpu.CompilerParams(vmem_limit_bytes=12 << 20),
    )(start.reshape(1), *lefts, *rights)


def per_device(tokens, grad_out, lang_ids, slot_ids, w_up, w_down_t):
    n_lang = lax.axis_size("lang")
    n_rep = lax.axis_size("rep")
    groups = n_lang // MODULES
    count, width = tokens.shape
    lang_index = lax.axis_index("lang")
    me = (lang_index // groups).astype(jnp.int32).reshape(1)
    member = lax.rem(lang_index, groups).astype(jnp.int32).reshape(1)
    lang_row, slot_row = lang_ids.reshape(1, count), slot_ids.reshape(1, count)
    packed_width = width + LANES

    def shift_near(value, bits):
        pairs = [
            (m * groups + g, (m ^ bits) * groups + g) for m in range(MODULES) for g in range(groups)
        ]
        return lax.ppermute(value, "lang", pairs)

    def shift_group(value, step):
        pairs = [
            (m * groups + g, m * groups + (g + step) % groups)
            for m in range(MODULES)
            for g in range(groups)
        ]
        return lax.ppermute(value, "lang", pairs)

    def shift_rep(value, step):
        return lax.ppermute(value, "rep", [(r, (r + step) % n_rep) for r in range(n_rep)])

    def over_groups(value):
        return [value] + [shift_group(value, s) for s in range(1, groups)]

    def exchange(packed):
        planes = [[g + groups * m for m in range(MODULES)] for g in range(groups)]
        cut = packed.reshape(MODULES, MAIN, packed_width)
        got = lax.all_to_all(
            cut, "lang", split_axis=0, concat_axis=0, axis_index_groups=planes, tiled=True
        )
        return got.reshape(ROWS, packed_width)

    def exchange_all(packed):
        cut = packed.reshape(n_lang, MAIN, packed_width)
        got = lax.all_to_all(cut, "lang", split_axis=0, concat_axis=0, tiled=True)
        return got.reshape(packed.shape)

    def collect(packed, terms):
        kernel = functools.partial(collect_kernel, terms)
        return local(kernel, [(count, width)], lang_row, slot_row, packed)[0]

    *x_messages, y_packed = pack(me, lang_row, slot_row, tokens, grad_out)

    got = [x_messages[0]] + [shift_near(x_messages[z], 2 * z) for z in (1, 2, 3)]
    x_low, x_send = local(split_kernel, [(64, packed_width)] * 2, *got)
    x_high = shift_near(x_send, 1)
    x_rows = local(
        functools.partial(unpack_near_kernel, groups),
        [(groups * PART, width)],
        *over_groups(x_low),
        *over_groups(x_high),
    )[0]
    y_rows = local(
        unpack_kernel, [(groups * PART, width)], me, *over_groups(exchange(y_packed)), scalars=1
    )[0]

    pre = dot(x_rows, w_up, ((1,), (0,)))
    share = gelu_share(pre)
    hidden = (pre * share).astype(jnp.bfloat16)
    slope = share + pre * jnp.exp(-0.5 * pre * pre) * INV_ROOT_TAU
    hidden, slope = lax.optimization_barrier((hidden, slope))
    out = dot(hidden, w_down_t, ((1,), (1,))).astype(jnp.bfloat16)
    out_packed = local(
        functools.partial(pack_all_kernel, groups),
        [(groups * ROWS, packed_width)],
        me,
        member,
        out,
        scalars=2,
    )[0]
    out_back = exchange_all(out_packed)
    ffn_out = collect(out_back, groups)

    (y_rows,) = after((y_rows,), out_packed)
    d_pre = (dot(y_rows, w_down_t, ((1,), (0,))) * slope).astype(jnp.bfloat16)
    dx = dot(d_pre, w_up, ((1,), (1,))).astype(jnp.bfloat16)
    dx_parts = [dx[PART * g : PART * (g + 1)] for g in range(groups)]
    dx_sums = [dx_parts[0]] + [shift_group(dx_parts[s], -s) for s in range(1, groups)]
    dx_packed = local(sum_pack_kernel, [(ROWS, packed_width)], me, *dx_sums, scalars=1)[0]
    (dx_packed,) = after((dx_packed,), out_back)
    dx_back = exchange(dx_packed)

    own = width // n_rep
    start = (lax.axis_index("rep") * own).astype(jnp.int32)

    def over_reps(value):
        return [value] + [shift_rep(value, s) for s in range(1, n_rep)]

    grad_down = weight_grad(start, over_reps(y_rows), over_reps(hidden), own)
    d_pre, x_rows = after((d_pre, x_rows), dx_packed)
    grad_up = weight_grad(start, over_reps(x_rows), over_reps(d_pre), own)
    (dx_back,) = after((dx_back,), grad_up, grad_down)
    return ffn_out, collect(dx_back, 1), grad_up, grad_down


def solution(mesh):
    placed = (
        P(("lang", "rep"), None),
        P(("lang", "rep"), None),
        P(("lang", "rep")),
        P(("lang", "rep")),
        P(None, "lang"),
        P(None, "lang"),
    )
    return jax.shard_map(
        per_device,
        mesh=mesh,
        in_specs=placed,
        out_specs=(
            P(("lang", "rep"), None),
            P(("lang", "rep"), None),
            P("rep", "lang"),
            P("rep", "lang"),
        ),
        check_vma=False,
    )
```

time: 99.7 us -> 80.8 us (0.81)
  Pallas kernels: 27 us -> 18.1 us
  waiting for transfers between devices: 23.7 us -> 17.5 us
  starting transfers between devices: 29.1 us -> 27.2 us
  matrix products: 17.4 us -> 15.8 us
    all_to_all x4 -> x2, starting transfers between devices: 22.4 us -> 9.31 us  [exchange(): lax.all_to_all(cut, 'lang', split_axis=0, concat_axis=0, axis_index_group...]
    all_to_all x4 -> x2, waiting for transfers between devices: 14.4 us -> 2.4 us  [exchange(): lax.all_to_all(cut, 'lang', split_axis=0, concat_axis=0, axis_index_group...]
    pallas_call x8, Pallas kernels: 15.7 us -> 6.92 us  [the longest x7 4.46 us: local(): pl.pallas_call(kernel, out_shape=shapes_of(shapes), in_specs=[SMEM_SPEC]...]
    ppermute x0 -> x4, waiting for transfers between devices: none -> 8.59 us  [shift_near(): return lax.ppermute(value, 'lang', pairs)]
    ppermute x0 -> x4, starting transfers between devices: none -> 7.26 us  [shift_near(): return lax.ppermute(value, 'lang', pairs)]
    all_to_all x0 -> x1, starting transfers between devices: none -> 4.62 us  [exchange_all(): got = lax.all_to_all(cut, 'lang', split_axis=0, concat_axis=0, tiled=True)]
    ppermute x4, waiting for transfers between devices: 9.22 us -> 6.45 us  [shift_group(): return lax.ppermute(value, 'lang', pairs)]
    dot_general x8 -> x4, matrix products: 17.4 us -> 15.8 us  [dot(): lax.dot_general(a, b, (contract, ((), ())), preferred_element_type=jnp.fl...]
  transfers between devices with their start and end apart: 16 -> 15, of which waited for: 5 -> 5; matrix products, arithmetic and copies ran while one was open for 18% -> 20% of each run, Pallas kernels for 23% -> 18%
where the time goes in v3:
time: 80.8 us; the launch traced here: 80.2 us
  starting transfers between devices  27.2 us (34%)
  Pallas kernels  18.1 us (22%)
  waiting for transfers between devices  17.5 us (22%)
  matrix products  15.8 us (20%)
  local copies, waits for them, and re-layouts  0.94 us (1%)
    dot_general x4, matrix products, dot(): lax.dot_general(a, b, (contract, ((), ())), preferred_element_type=jnp.fl...  15.8 us
    pallas_call x2, Pallas kernels, weight_grad(): pl.pallas_call(functools.partial(weight_grad_kernel, n_parts), out_shape=...  11.1 us
    all_to_all x2, starting transfers between devices, exchange(): lax.all_to_all(cut, 'lang', split_axis=0, concat_axis=0, axis_index_group...  9.31 us
    ppermute x4, waiting for transfers between devices, shift_near(): return lax.ppermute(value, 'lang', pairs)  8.59 us
    ppermute x4, starting transfers between devices, shift_near(): return lax.ppermute(value, 'lang', pairs)  7.26 us
    ppermute x4, waiting for transfers between devices, shift_group(): return lax.ppermute(value, 'lang', pairs)  6.45 us
    ppermute x4, starting transfers between devices, shift_group(): return lax.ppermute(value, 'lang', pairs)  5.5 us
    all_to_all x1, starting transfers between devices, exchange_all(): got = lax.all_to_all(cut, 'lang', split_axis=0, concat_axis=0, tiled=True)  4.62 us
  transfers between devices with their start and end apart: 15, of which 5 were waited for; matrix products, arithmetic and copies ran while one was open for 20% of the time, Pallas kernels for 18%

profile of v3, /device:TPU:0, one launch (start us, length us, event | category | flops | bytes accessed | tf_op | source)
XLA Modules:
  0.0 80.2 jit_solution(12884612953504407966)
XLA Ops:
  0.6 2.5 %shard_map.93 = (bf16[32,1152]{1,0:T(8,128)(2,1)}, bf16[32,1152]{1,0:T(8,128)(2,1)}, bf16[32,1152]{1,0:T(8,128)(2,1)}, bf16[32,1152]{1,0:T(8,128)(2,1)}, bf16[128,1152]{1,0:T(8,128)(2,1)}) custom-call(s32[1]{0:T(128)} %bitcast.2.me_ref, s32[1,128]{1,0:T(1,128)} %bitcast.23, s32[1,128]{1,0:T(1,128)} %bitcast.26, bf16[128,1024]{1,0:T(8,128)(2,1)} %refs_2_.1, ...), custom_call_target="tpu_custom_call" | custom-call | tf_op jit(solution)/shard_map/pallas_call | solution.py:195
  3.1 3.1 %collective-permute-start = (bf16[32,1152]{1,0:T(8,128)(2,1)}, bf16[32,1152]{1,0:T(8,128)(2,1)S(1)}, u32[]{:S(2)}, u32[]{:S(2)}) collective-permute-start(bf16[32,1152]{1,0:T(8,128)(2,1)} %get-tuple-element.19), channel_id=1, source_target_pairs={{0,8},{2,10},{4,12},{6,14},{8,0},{10,2},{12,4},{14,6},{16,24},{18,... | collective-permute-start | bytes 221192 | tf_op jit(solution)/shard_map/ppermute | solution.py:248
  6.2 2.6 %collective-permute-start.1 = (bf16[32,1152]{1,0:T(8,128)(2,1)}, bf16[32,1152]{1,0:T(8,128)(2,1)S(1)}, u32[]{:S(2)}, u32[]{:S(2)}) collective-permute-start(bf16[32,1152]{1,0:T(8,128)(2,1)} %get-tuple-element.20), channel_id=1, source_target_pairs={{0,16},{2,18},{4,20},{6,22},{8,24},{10,26},{12,28},{14,30},{16,0},... | collective-permute-start | bytes 221192 | tf_op jit(solution)/shard_map/ppermute | solution.py:248
  8.8 5.4 %collective-permute-done.1.refs_2_ = bf16[32,1152]{1,0:T(8,128)(2,1)S(1)} collective-permute-done((bf16[32,1152]{1,0:T(8,128)(2,1)}, bf16[32,1152]{1,0:T(8,128)(2,1)S(1)}, u32[]{:S(2)}, u32[]{:S(2)}) %collective-permute-start.1) | collective-permute-done | bytes 73760 | tf_op jit(solution)/shard_map/ppermute | solution.py:248
  14.2 1.1 %collective-permute-done.2.refs_3_ = bf16[32,1152]{1,0:T(8,128)(2,1)S(1)} collective-permute-done((bf16[32,1152]{1,0:T(8,128)(2,1)}, bf16[32,1152]{1,0:T(8,128)(2,1)S(1)}, u32[]{:S(2)}, u32[]{:S(2)}) %collective-permute-start.2) | collective-permute-done | bytes 73760 | tf_op jit(solution)/shard_map/ppermute | solution.py:248
  15.3 0.9 %copy-done = bf16[32,1152]{1,0:T(8,128)(2,1)S(1)} copy-done((bf16[32,1152]{1,0:T(8,128)(2,1)S(1)}, bf16[32,1152]{1,0:T(8,128)(2,1)}, u32[]{:S(2)}) %copy-start) | copy-done | bytes 73752
  16.2 1.6 %collective-permute-start.4 = (bf16[64,1152]{1,0:T(8,128)(2,1)S(1)}, bf16[64,1152]{1,0:T(8,128)(2,1)S(1)}, u32[]{:S(2)}, u32[]{:S(2)}) collective-permute-start(bf16[64,1152]{1,0:T(8,128)(2,1)S(1)} %get-tuple-element.23), channel_id=1, source_target_pairs={{0,4},{2,6},{4,0},{6,2},{8,12},{10,14},{12,8},{14,10},{16,20},{18,... | collective-permute-start | bytes 442376 | tf_op jit(solution)/shard_map/ppermute | solution.py:248
  17.7 1.5 %collective-permute-start.3 = (bf16[64,1152]{1,0:T(8,128)(2,1)S(1)}, bf16[64,1152]{1,0:T(8,128)(2,1)S(1)}, u32[]{:S(2)}, u32[]{:S(2)}) collective-permute-start(bf16[64,1152]{1,0:T(8,128)(2,1)S(1)} %get-tuple-element.22.refs_0_), channel_id=1, source_target_pairs={{0,2},{2,0},{4,6},{6,4},{8,10},{10,8},{12,14},{14,12},{16,18},{18,... | collective-permute-start | bytes 442376 | tf_op jit(solution)/shard_map/ppermute | solution.py:256
  19.2 2.1 %collective-permute-done.4.refs_2_ = bf16[64,1152]{1,0:T(8,128)(2,1)S(1)} collective-permute-done((bf16[64,1152]{1,0:T(8,128)(2,1)S(1)}, bf16[64,1152]{1,0:T(8,128)(2,1)S(1)}, u32[]{:S(2)}, u32[]{:S(2)}) %collective-permute-start.4) | collective-permute-done | bytes 147488 | tf_op jit(solution)/shard_map/ppermute | solution.py:248
  21.4 1.5 %collective-permute-start.5 = (bf16[64,1152]{1,0:T(8,128)(2,1)S(1)}, bf16[64,1152]{1,0:T(8,128)(2,1)S(1)}, u32[]{:S(2)}, u32[]{:S(2)}) collective-permute-start(bf16[64,1152]{1,0:T(8,128)(2,1)S(1)} %collective-permute-done.4.refs_2_), channel_id=1, source_target_pairs={{0,2},{2,0},{4,6},{6,4},{8,10},{10,8},{12,14},{14,12},{16,18},{18,... | collective-permute-start | bytes 442376 | tf_op jit(solution)/shard_map/ppermute | solution.py:256
  22.9 4.4 %all-to-all-start.1 = ((bf16[8,16,1152]{2,1,0:T(8,128)(2,1)}), bf16[8,16,1152]{2,1,0:T(8,128)(2,1)S(1)}, u32[]{:S(2)}, u32[]{:S(2)}) async-start(bf16[8,16,1152]{2,1,0:T(8,128)(2,1)} %bitcast.29), calls=%async_computation.1 | async-start | bytes 589824 | tf_op jit(solution)/shard_map/all_to_all | solution.py:267
  27.3 0.2 shard_map.95.refs_0_
  27.5 5.8 %fusion.4 = (f32[288,2048]{1,0:T(8,128)}, bf16[288,2048]{1,0:T(8,128)(2,1)}) fusion(bf16[288,1024]{1,0:T(8,128)(2,1)S(1)} %shard_map.95.refs_0_, bf16[1024,2048]{1,0:T(8,128)(2,1)} %param.10), kind=kOutput, calls=%fused_computation.6 | convolution fusion | flops 1213857792 | bytes 8323072 | tf_op jit(solution)/shard_map/dot_general | solution.py:29
  33.3 2.4 %all-to-all-done.1 = bf16[8,16,1152]{2,1,0:T(8,128)(2,1)S(1)} async-done(((bf16[8,16,1152]{2,1,0:T(8,128)(2,1)}), bf16[8,16,1152]{2,1,0:T(8,128)(2,1)S(1)}, u32[]{:S(2)}, u32[]{:S(2)}) %all-to-all-start.1) | async-done | bytes 294944 | tf_op jit(solution)/shard_map/all_to_all | solution.py:267
  35.7 0.5 collective-permute-start.6
  36.3 4.0 %convolution_convert_fusion.1.rows_ref = bf16[288,1024]{1,0:T(8,128)(2,1)S(1)} fusion(bf16[288,2048]{1,0:T(8,128)(2,1)} %get-tuple-element.24.refs_2_, bf16[1024,2048]{1,0:T(8,128)(2,1)} %param.11), kind=kOutput, calls=%fused_computation.10 | convolution fusion | flops 1208254464 | bytes 5963776 | tf_op jit(solution)/shard_map/dot_general | solution.py:29
  40.3 1.1 %shard_map.96 = bf16[256,1152]{1,0:T(8,128)(2,1)} custom-call(s32[1]{0:T(128)} %bitcast.2.me_ref, s32[1]{0:T(128)} %bitcast.3.member_ref, bf16[288,1024]{1,0:T(8,128)(2,1)S(1)} %convolution_convert_fusion.1.rows_ref), custom_call_target="tpu_custom_call" | custom-call | tf_op jit(solution)/shard_map/pallas_call | solution.py:182
  41.3 4.6 %all-to-all-start = ((bf16[16,16,1152]{2,1,0:T(8,128)(2,1)}), bf16[16,16,1152]{2,1,0:T(8,128)(2,1)S(1)}, u32[]{:S(2)}, u32[]{:S(2)}) async-start(bf16[16,16,1152]{2,1,0:T(8,128)(2,1)} %bitcast.4), calls=%async_computation | async-start | bytes 1179648 | tf_op jit(solution)/shard_map/all_to_all | solution.py:274
  46.0 0.2 shard_map.98.refs_0_
  46.1 4.5 %fusion.refs_2_ = bf16[288,2048]{1,0:T(8,128)(2,1)S(1)} fusion(f32[288,2048]{1,0:T(8,128)} %get-tuple-element.27, bf16[288,1024]{1,0:T(8,128)(2,1)S(1)} %shard_map.98.refs_0_, bf16[1024,2048]{1,0:T(8,128)(2,1)} %param.11), kind=kOutput, calls=%fused_computation.2 | convolution fusion | flops 1209139200 | bytes 8323072 | tf_op jit(solution)/shard_map/dot_general | solution.py:29
  50.6 1.5 %convolution_convert_fusion = bf16[288,1024]{1,0:T(8,128)(2,1)S(1)} fusion(bf16[288,2048]{1,0:T(8,128)(2,1)S(1)} %fusion.refs_2_, bf16[1024,2048]{1,0:T(8,128)(2,1)S(1)} %copy-done.3), kind=kOutput, calls=%fused_computation.9 | convolution fusion | flops 1208254464 | bytes 5963776 | tf_op jit(solution)/shard_map/dot_general | solution.py:29
  52.1 0.0 copy-start.1
  52.2 0.0 copy-start.2
  52.2 2.0 %collective-permute-start.7 = (bf16[144,1024]{1,0:T(8,128)(2,1)S(1)}, bf16[144,1024]{1,0:T(8,128)(2,1)S(1)}, u32[]{:S(2)}, u32[]{:S(2)}) collective-permute-start(bf16[144,1024]{1,0:T(8,128)(2,1)S(1)} %get-tuple-element.34), channel_id=1, source_target_pairs={{0,2},{2,0},{4,6},{6,4},{8,10},{10,8},{12,14},{14,12},{16,18},{18,... | collective-permute-start | bytes 884744 | tf_op jit(solution)/shard_map/ppermute | solution.py:256
  54.2 6.4 %collective-permute-done.7.refs_1_ = bf16[144,1024]{1,0:T(8,128)(2,1)S(1)} collective-permute-done((bf16[144,1024]{1,0:T(8,128)(2,1)S(1)}, bf16[144,1024]{1,0:T(8,128)(2,1)S(1)}, u32[]{:S(2)}, u32[]{:S(2)}) %collective-permute-start.7) | collective-permute-done | bytes 294944 | tf_op jit(solution)/shard_map/ppermute | solution.py:256
  60.6 0.9 %shard_map.99 = bf16[128,1152]{1,0:T(8,128)(2,1)} custom-call(s32[1]{0:T(128)} %bitcast.2.me_ref, bf16[144,1024]{1,0:T(8,128)(2,1)S(1)} %get-tuple-element.35.refs_0_, bf16[144,1024]{1,0:T(8,128)(2,1)S(1)} %collective-permute-done.7.refs_1_), custom_call_target="tpu_custom_call" | custom-call | tf_op jit(solution)/shard_map/pallas_call | solution.py:182
  61.6 0.5 collective-permute-start.10
  62.1 4.9 %all-to-all-start.2 = ((bf16[8,16,1152]{2,1,0:T(8,128)(2,1)}), bf16[8,16,1152]{2,1,0:T(8,128)(2,1)S(1)}, u32[]{:S(2)}, u32[]{:S(2)}) async-start(bf16[8,16,1152]{2,1,0:T(8,128)(2,1)} %bitcast.8), calls=%async_computation.2 | async-start | bytes 589824 | tf_op jit(solution)/shard_map/all_to_all | solution.py:267
  67.0 1.1 %shard_map.97 = bf16[128,1024]{1,0:T(8,128)(2,1)} custom-call(s32[1,128]{1,0:T(1,128)S(1)} %bitcast.24, s32[1,128]{1,0:T(1,128)S(1)} %bitcast.27, bf16[256,1152]{1,0:T(8,128)(2,1)S(1)} %bitcast.19), custom_call_target="tpu_custom_call" | custom-call | tf_op jit(solution)/shard_map/pallas_call | solution.py:182
  68.0 5.7 %shard_map.101 = f32[512,2048]{1,0:T(8,128)} custom-call(s32[1]{0:T(128)} %bitcast.10.start_ref, bf16[288,1024]{1,0:T(8,128)(2,1)S(1)} %shard_map.98.refs_0_, bf16[288,1024]{1,0:T(8,128)(2,1)} %collective-permute-done.10.refs_1_, bf16[288,2048]{1,0:T(8,128)(2,1)} %get-tuple-element.24.refs_2_, bf16[288,2048]{1,0:T(8,128)(2,1)} %collective-permute-done.11.refs_3_), custom_call_target="tpu_custom_call" | custom-call | flops 1207959552 | bytes 4194304 | tf_op jit(solution)/shard_map/pallas_call | solution.py:219
  73.8 5.4 %shard_map.100 = f32[512,2048]{1,0:T(8,128)} custom-call(s32[1]{0:T(128)} %bitcast.10.start_ref, bf16[288,1024]{1,0:T(8,128)(2,1)S(1)} %shard_map.95.refs_0_, bf16[288,1024]{1,0:T(8,128)(2,1)} %collective-permute-done.8.refs_1_, bf16[288,2048]{1,0:T(8,128)(2,1)S(1)} %fusion.refs_2_, bf16[288,2048]{1,0:T(8,128)(2,1)} %collective-permute-done.9.refs_3_), custom_call_target="tpu_custom_call" | custom-call | flops 1207959552 | bytes 4194304 | tf_op jit(solution)/shard_map/pallas_call | solution.py:219
  79.2 1.0 %shard_map.102 = bf16[128,1024]{1,0:T(8,128)(2,1)} custom-call(s32[1,128]{1,0:T(1,128)S(1)} %bitcast.25, s32[1,128]{1,0:T(1,128)S(1)} %bitcast.28, bf16[128,1152]{1,0:T(8,128)(2,1)S(1)} %bitcast.20), custom_call_target="tpu_custom_call" | custom-call | tf_op jit(solution)/shard_map/pallas_call | solution.py:182
  (21 shorter events, 0.1 us)
Async XLA Ops:
  3.1 5.7 %collective-permute-start = (bf16[32,1152]{1,0:T(8,128)(2,1)}, bf16[32,1152]{1,0:T(8,128)(2,1)S(1)}, u32[]{:S(2)}, u32[]{:S(2)}) collective-permute-start(bf16[32,1152]{1,0:T(8,128)(2,1)} %get-tuple-element.19), channel_id=1, source_target_pairs={{0,8},{2,10},{4,12},{6,14},{8,0},{10,2},{12,4},{14,6},{16,24},{18,... | collective-permute-start | bytes 221192 | tf_op jit(solution)/shard_map/ppermute | solution.py:248
  6.2 8.0 %collective-permute-start.1 = (bf16[32,1152]{1,0:T(8,128)(2,1)}, bf16[32,1152]{1,0:T(8,128)(2,1)S(1)}, u32[]{:S(2)}, u32[]{:S(2)}) collective-permute-start(bf16[32,1152]{1,0:T(8,128)(2,1)} %get-tuple-element.20), channel_id=1, source_target_pairs={{0,16},{2,18},{4,20},{6,22},{8,24},{10,26},{12,28},{14,30},{16,0},... | collective-permute-start | bytes 221192 | tf_op jit(solution)/shard_map/ppermute | solution.py:248
  8.8 6.5 %collective-permute-start.2 = (bf16[32,1152]{1,0:T(8,128)(2,1)}, bf16[32,1152]{1,0:T(8,128)(2,1)S(1)}, u32[]{:S(2)}, u32[]{:S(2)}) collective-permute-start(bf16[32,1152]{1,0:T(8,128)(2,1)} %get-tuple-element.21), channel_id=1, source_target_pairs={{0,24},{2,26},{4,28},{6,30},{8,16},{10,18},{12,20},{14,22},{16,8},... | collective-permute-start | bytes 221192 | tf_op jit(solution)/shard_map/ppermute | solution.py:248
  15.2 0.9 %copy-start = (bf16[32,1152]{1,0:T(8,128)(2,1)S(1)}, bf16[32,1152]{1,0:T(8,128)(2,1)}, u32[]{:S(2)}) copy-start(bf16[32,1152]{1,0:T(8,128)(2,1)} %get-tuple-element.18.refs_0_) | copy-start | bytes 221188
  16.2 5.2 %collective-permute-start.4 = (bf16[64,1152]{1,0:T(8,128)(2,1)S(1)}, bf16[64,1152]{1,0:T(8,128)(2,1)S(1)}, u32[]{:S(2)}, u32[]{:S(2)}) collective-permute-start(bf16[64,1152]{1,0:T(8,128)(2,1)S(1)} %get-tuple-element.23), channel_id=1, source_target_pairs={{0,4},{2,6},{4,0},{6,2},{8,12},{10,14},{12,8},{14,10},{16,20},{18,... | collective-permute-start | bytes 442376 | tf_op jit(solution)/shard_map/ppermute | solution.py:248
  17.7 9.6 %collective-permute-start.3 = (bf16[64,1152]{1,0:T(8,128)(2,1)S(1)}, bf16[64,1152]{1,0:T(8,128)(2,1)S(1)}, u32[]{:S(2)}, u32[]{:S(2)}) collective-permute-start(bf16[64,1152]{1,0:T(8,128)(2,1)S(1)} %get-tuple-element.22.refs_0_), channel_id=1, source_target_pairs={{0,2},{2,0},{4,6},{6,4},{8,10},{10,8},{12,14},{14,12},{16,18},{18,... | collective-permute-start | bytes 442376 | tf_op jit(solution)/shard_map/ppermute | solution.py:256
  21.4 5.9 %collective-permute-start.5 = (bf16[64,1152]{1,0:T(8,128)(2,1)S(1)}, bf16[64,1152]{1,0:T(8,128)(2,1)S(1)}, u32[]{:S(2)}, u32[]{:S(2)}) collective-permute-start(bf16[64,1152]{1,0:T(8,128)(2,1)S(1)} %collective-permute-done.4.refs_2_), channel_id=1, source_target_pairs={{0,2},{2,0},{4,6},{6,4},{8,10},{10,8},{12,14},{14,12},{16,18},{18,... | collective-permute-start | bytes 442376 | tf_op jit(solution)/shard_map/ppermute | solution.py:256
  22.9 12.9 %all-to-all-start.1 = ((bf16[8,16,1152]{2,1,0:T(8,128)(2,1)}), bf16[8,16,1152]{2,1,0:T(8,128)(2,1)S(1)}, u32[]{:S(2)}, u32[]{:S(2)}) async-start(bf16[8,16,1152]{2,1,0:T(8,128)(2,1)} %bitcast.29), calls=%async_computation.1 | async-start | bytes 589824 | tf_op jit(solution)/shard_map/all_to_all | solution.py:267
  35.7 10.2 %collective-permute-start.6 = (bf16[128,1152]{1,0:T(8,128)(2,1)S(1)}, bf16[128,1152]{1,0:T(8,128)(2,1)S(1)}, u32[]{:S(2)}, u32[]{:S(2)}) collective-permute-start(bf16[128,1152]{1,0:T(8,128)(2,1)S(1)} %bitcast.21), channel_id=1, source_target_pairs={{0,2},{2,0},{4,6},{6,4},{8,10},{10,8},{12,14},{14,12},{16,18},{18,... | collective-permute-start | bytes 884744 | tf_op jit(solution)/shard_map/ppermute | solution.py:256
  41.3 20.3 %all-to-all-start = ((bf16[16,16,1152]{2,1,0:T(8,128)(2,1)}), bf16[16,16,1152]{2,1,0:T(8,128)(2,1)S(1)}, u32[]{:S(2)}, u32[]{:S(2)}) async-start(bf16[16,16,1152]{2,1,0:T(8,128)(2,1)} %bitcast.4), calls=%async_computation | async-start | bytes 1179648 | tf_op jit(solution)/shard_map/all_to_all | solution.py:274
  46.1 4.5 %copy-start.3 = (bf16[1024,2048]{1,0:T(8,128)(2,1)S(1)}, bf16[1024,2048]{1,0:T(8,128)(2,1)}, u32[]{:S(2)}) copy-start(bf16[1024,2048]{1,0:T(8,128)(2,1)} %param.10) | copy-start | bytes 12582916
  52.1 14.8 %copy-start.1 = (s32[128]{0:T(128)S(1)}, s32[128]{0:T(128)}, u32[]{:S(2)}) copy-start(s32[128]{0:T(128)} %param.8) | copy-start | bytes 1540
  52.2 14.8 %copy-start.2 = (s32[128]{0:T(128)S(1)}, s32[128]{0:T(128)}, u32[]{:S(2)}) copy-start(s32[128]{0:T(128)} %param.9) | copy-start | bytes 1540
  52.2 8.4 %collective-permute-start.7 = (bf16[144,1024]{1,0:T(8,128)(2,1)S(1)}, bf16[144,1024]{1,0:T(8,128)(2,1)S(1)}, u32[]{:S(2)}, u32[]{:S(2)}) collective-permute-start(bf16[144,1024]{1,0:T(8,128)(2,1)S(1)} %get-tuple-element.34), channel_id=1, source_target_pairs={{0,2},{2,0},{4,6},{6,4},{8,10},{10,8},{12,14},{14,12},{16,18},{18,... | collective-permute-start | bytes 884744 | tf_op jit(solution)/shard_map/ppermute | solution.py:256
  54.2 13.8 %collective-permute-start.11 = (bf16[288,2048]{1,0:T(8,128)(2,1)}, bf16[288,2048]{1,0:T(8,128)(2,1)}, u32[]{:S(2)}, u32[]{:S(2)}) collective-permute-start(bf16[288,2048]{1,0:T(8,128)(2,1)} %get-tuple-element.24.refs_2_), channel_id=1, source_target_pairs={{0,1},{1,0},{2,3},{3,2},{4,5},{5,4},{6,7},{7,6},{8,9},{9,8},{10,11... | collective-permute-start | bytes 3538952 | tf_op jit(solution)/shard_map/ppermute | solution.py:259
  61.6 12.2 %collective-permute-start.9 = (bf16[288,2048]{1,0:T(8,128)(2,1)S(1)}, bf16[288,2048]{1,0:T(8,128)(2,1)}, u32[]{:S(2)}, u32[]{:S(2)}) collective-permute-start(bf16[288,2048]{1,0:T(8,128)(2,1)S(1)} %fusion.refs_2_), channel_id=1, source_target_pairs={{0,1},{1,0},{2,3},{3,2},{4,5},{5,4},{6,7},{7,6},{8,9},{9,8},{10,11... | collective-permute-start | bytes 3538952 | tf_op jit(solution)/shard_map/ppermute | solution.py:259
  61.6 6.4 %collective-permute-start.10 = (bf16[288,1024]{1,0:T(8,128)(2,1)S(1)}, bf16[288,1024]{1,0:T(8,128)(2,1)}, u32[]{:S(2)}, u32[]{:S(2)}) collective-permute-start(bf16[288,1024]{1,0:T(8,128)(2,1)S(1)} %shard_map.98.refs_0_), channel_id=1, source_target_pairs={{0,1},{1,0},{2,3},{3,2},{4,5},{5,4},{6,7},{7,6},{8,9},{9,8},{10,11... | collective-permute-start | bytes 1769480 | tf_op jit(solution)/shard_map/ppermute | solution.py:259
  62.1 11.7 %collective-permute-start.8 = (bf16[288,1024]{1,0:T(8,128)(2,1)S(1)}, bf16[288,1024]{1,0:T(8,128)(2,1)}, u32[]{:S(2)}, u32[]{:S(2)}) collective-permute-start(bf16[288,1024]{1,0:T(8,128)(2,1)S(1)} %shard_map.95.refs_0_), channel_id=1, source_target_pairs={{0,1},{1,0},{2,3},{3,2},{4,5},{5,4},{6,7},{7,6},{8,9},{9,8},{10,11... | collective-permute-start | bytes 1769480 | tf_op jit(solution)/shard_map/ppermute | solution.py:259
  62.1 17.1 %all-to-all-start.2 = ((bf16[8,16,1152]{2,1,0:T(8,128)(2,1)}), bf16[8,16,1152]{2,1,0:T(8,128)(2,1)S(1)}, u32[]{:S(2)}, u32[]{:S(2)}) async-start(bf16[8,16,1152]{2,1,0:T(8,128)(2,1)} %bitcast.8), calls=%async_computation.2 | async-start | bytes 589824 | tf_op jit(solution)/shard_map/all_to_all | solution.py:267

commit v4 on v3

v4 whole, which is shorter than its diff:
```python
import functools

import jax
import jax.numpy as jnp
from jax import lax
from jax.experimental import pallas as pl
from jax.experimental.pallas import tpu as pltpu
from jax.sharding import PartitionSpec as P

MODULES = 8
TOK_DEV = 128
CAPACITY = 18
MAIN = 16
SPLIT_COST = 6
VARIANT = "G"
UNPACK_COST = 2
LANES = 128
SPARE = CAPACITY - MAIN
ROWS = MODULES * MAIN
PART = MODULES * CAPACITY

INV_ROOT_TWO = 0.7071067811865476
INV_ROOT_TAU = 0.3989422804014327


def dot(a, b, contract):
    return lax.dot_general(a, b, (contract, ((), ())), preferred_element_type=jnp.float32)


def piece_order():
    place = lax.broadcasted_iota(jnp.int32, (LANES, LANES), 0)
    column = lax.broadcasted_iota(jnp.int32, (LANES, LANES), 1)
    return ((place & 15) * 8 + (place >> 4) == column).astype(jnp.bfloat16)


def spare_rows(cut):
    ordered = dot(piece_order(), cut, ((1,), (0,))).astype(jnp.bfloat16)
    return jnp.concatenate([ordered[16 * p : 16 * (p + 1)] for p in range(8)], axis=1)


def spare_cut(rows):
    ordered = jnp.concatenate([rows[:, LANES * p : LANES * (p + 1)] for p in range(8)], axis=0)
    return dot(piece_order(), ordered, ((0,), (0,))).astype(jnp.bfloat16)


def slot_picks(lang, slot):
    row = lax.broadcasted_iota(jnp.int32, (PART, lang.shape[1]), 0)
    is_main = row < ROWS
    block = jnp.where(is_main, row >> 4, (row - ROWS) >> 1)
    place = jnp.where(is_main, row & 15, MAIN + (row & 1))
    return ((block == lang) & (place == slot)).astype(jnp.bfloat16)


def pack_kernel(me_ref, *refs):
    sources, outs, staged, arrived = refs[:4], refs[4:12], refs[12:16], refs[16]
    copies = [
        pltpu.make_async_copy(source, stage, arrived.at[i])
        for i, (source, stage) in enumerate(zip(sources, staged))
    ]
    for copy in copies:
        copy.start()
    copies[0].wait()
    copies[1].wait()
    picks = slot_picks(staged[0][...] ^ me_ref[0], staged[1][...])
    for array in range(2):
        copies[2 + array].wait()
        width = staged[2].shape[1]
        rows, cut = packed_rows(picks, staged[2 + array][...])
        for z, out_ref in enumerate(outs[4 * array : 4 * (array + 1)]):
            out_ref[:, :width] = rows[32 * z : 32 * (z + 1)]
            out_ref[:, width:] = cut[32 * z : 32 * (z + 1)]


def packed_rows(picks, values):
    rows = dot(picks, values, ((1,), (0,))).astype(jnp.bfloat16)
    return rows[:ROWS], spare_cut(rows[ROWS:])


def split_kernel(*refs):
    messages, outs = refs[:4], refs[4:]
    for z, message_ref in enumerate(messages):
        for place, out_ref in enumerate(outs):
            out_ref[16 * z : 16 * (z + 1)] = message_ref[16 * place : 16 * (place + 1)]


def by_tiles(count):
    tile = min(512, count)
    return [slice(first, first + tile) for first in range(0, count, tile)]


def put_shares(left_ref, right_ref, outs):
    for part in by_tiles(right_ref.shape[0]):
        share = dot(left_ref[...], right_ref[part], ((1,), (1,))).astype(jnp.bfloat16)
        for g, out_ref in enumerate(outs):
            out_ref[:, part] = share[PART * g : PART * (g + 1)]


def forward_kernel(rows_ref, up_ref, down_ref, hidden_ref, slope_ref, *outs):
    for units in by_tiles(up_ref.shape[1]):
        pre = dot(rows_ref[...], up_ref[:, units], ((1,), (0,)))
        share = 0.5 * (1.0 + lax.erf(pre * INV_ROOT_TWO))
        hidden_ref[:, units] = (pre * share).astype(jnp.bfloat16)
        slope_ref[:, units] = share + pre * jnp.exp(-0.5 * pre * pre) * INV_ROOT_TAU
    put_shares(hidden_ref, down_ref, outs)


def backward_kernel(rows_ref, slope_ref, up_ref, down_ref, d_pre_ref, *outs):
    for units in by_tiles(up_ref.shape[1]):
        d_hidden = dot(rows_ref[...], down_ref[:, units], ((1,), (0,)))
        d_pre_ref[:, units] = (d_hidden * slope_ref[:, units]).astype(jnp.bfloat16)
    put_shares(d_pre_ref, up_ref, outs)


NEAR = (0, 2, 4, 6, 1, 3, 5, 7)


def put_rows(packed, rows_ref, first):
    width = rows_ref.shape[1]
    rows_ref[first : first + ROWS] = packed[:, :width]
    rows_ref[first + ROWS : first + PART] = spare_rows(packed[:, width:])


def unpack_near_kernel(groups, *refs):
    for g in range(groups):
        packed = jnp.concatenate([refs[g][...], refs[groups + g][...]], axis=0)
        put_rows(packed, refs[-1], PART * g)


def send_kernel(groups, me_ref, member_ref, *refs):
    packed_ref = refs[-1]
    for i, rows_ref in enumerate(refs[:-1]):
        array, s = divmod(i, groups)
        member = lax.rem(member_ref[0] + groups - s, groups)
        rows = rows_ref[...]
        width = rows.shape[1]
        cut = spare_cut(rows[ROWS:])
        for j, near in enumerate(NEAR):
            device = (me_ref[0] ^ near) * groups + member
            at = pl.ds(pl.multiple_of((device * 2 + array) * MAIN, MAIN), MAIN)
            packed_ref[at, :width] = rows[MAIN * j : MAIN * (j + 1)]
            packed_ref[at, width:] = cut[MAIN * j : MAIN * (j + 1)]


def collect_kernel(groups, lang_ref, slot_ref, packed_ref, *outs):
    picks = slot_picks(lang_ref[...], slot_ref[...])
    for array, values_ref in enumerate(outs):
        width = values_ref.shape[1]
        blocks = []
        for m in range(MODULES):
            total = 0.0
            for g in range(groups):
                first = ((m * groups + g) * 2 + array) * MAIN
                total = total + packed_ref[first : first + MAIN].astype(jnp.float32)
            blocks.append(total.astype(jnp.bfloat16))
        packed = jnp.concatenate(blocks, axis=0)
        rows = jnp.concatenate([packed[:, :width], spare_rows(packed[:, width:])], axis=0)
        values_ref[...] = dot(picks, rows, ((0,), (0,))).astype(jnp.bfloat16)


def weight_grad_kernel(n_parts, start_ref, *refs):
    lefts, rights = refs[:n_parts], refs[n_parts : 2 * n_parts]
    out_ref, turned = refs[2 * n_parts :]
    own, tile = out_ref.shape
    step = pl.program_id(0)

    @pl.when(step == 0)
    def _():
        columns = pl.ds(pl.multiple_of(start_ref[0], LANES), own)
        turned[...] = jnp.concatenate([ref[:, columns] for ref in lefts], axis=0).T

    units = pl.ds(pl.multiple_of(step * tile, LANES), tile)
    right = jnp.concatenate([ref[:, units] for ref in rights], axis=0)
    out_ref[...] = dot(turned[...], right, ((1,), (0,))) * (1.0 / TOK_DEV)


VMEM_SPEC = pl.BlockSpec(memory_space=pltpu.VMEM)
SMEM_SPEC = pl.BlockSpec(memory_space=pltpu.SMEM)


def cost(micros):
    return pl.CostEstimate(flops=int(micros * 1e9), bytes_accessed=0, transcendentals=0)


def shapes_of(shapes):
    return [jax.ShapeDtypeStruct(shape, jnp.bfloat16) for shape in shapes]


def in_hbm(value):
    return pltpu.with_memory_space_constraint(value, pltpu.HBM)


def local(kernel, shapes, *operands, scalars=0, micros=0, grant=4, kept=()):
    outs = [s if isinstance(s, jax.ShapeDtypeStruct) else shapes_of([s])[0] for s in shapes]
    return pl.pallas_call(
        kernel,
        out_shape=[pltpu.VMEM(s.shape, s.dtype) if i in kept else s for i, s in enumerate(outs)],
        in_specs=[SMEM_SPEC] * scalars + [VMEM_SPEC] * (len(operands) - scalars),
        out_specs=[VMEM_SPEC] * len(shapes),
        cost_estimate=cost(micros),
        compiler_params=pltpu.CompilerParams(vmem_limit_bytes=grant << 20),
    )(*operands)


def stage_kernel(*refs):
    sources, outs, arrived = refs[:2], refs[2:4], refs[4]
    copies = [
        pltpu.make_async_copy(source, out, arrived.at[i])
        for i, (source, out) in enumerate(zip(sources, outs))
    ]
    for copy in copies:
        copy.start()
    for copy in copies:
        copy.wait()


def stage(*weights):
    return pl.pallas_call(
        stage_kernel,
        out_shape=[pltpu.VMEM(w.shape, w.dtype) for w in weights],
        in_specs=[pl.BlockSpec(memory_space=pltpu.HBM)] * 2,
        out_specs=[VMEM_SPEC] * 2,
        scratch_shapes=[pltpu.SemaphoreType.DMA((2,))],
        cost_estimate=cost(4),
        compiler_params=pltpu.CompilerParams(vmem_limit_bytes=2 << 20),
    )(*[in_hbm(w) for w in weights])


def pack(me, lang_row, slot_row, tokens, grad_out):
    sources = (lang_row, slot_row, tokens, grad_out)
    packed_width = tokens.shape[1] + LANES
    return pl.pallas_call(
        pack_kernel,
        out_shape=shapes_of([(32, packed_width)] * 8),
        in_specs=[SMEM_SPEC] + [pl.BlockSpec(memory_space=pltpu.HBM)] * 4,
        out_specs=[VMEM_SPEC] * 8,
        scratch_shapes=[pltpu.VMEM(v.shape, v.dtype) for v in sources]
        + [pltpu.SemaphoreType.DMA((4,))],
        cost_estimate=cost(2),
        compiler_params=pltpu.CompilerParams(vmem_limit_bytes=4 << 20),
    )(me, *[in_hbm(v) for v in sources])


def after(values, *earlier):
    return lax.optimization_barrier((*values, *earlier))[: len(values)]


def weight_grad(start, lefts, rights, own):
    n_parts = len(lefts)
    units = rights[0].shape[1]
    depth = sum(left.shape[0] for left in lefts)
    tile = min(512, units)
    if n_parts > 4:
        left = lax.dynamic_slice_in_dim(jnp.concatenate(lefts, axis=0), start, own, axis=1)
        return dot(left, jnp.concatenate(rights, axis=0), ((0,), (0,))) * (1.0 / TOK_DEV)
    return pl.pallas_call(
        functools.partial(weight_grad_kernel, n_parts),
        out_shape=jax.ShapeDtypeStruct((own, units), jnp.float32),
        grid=(units // tile,),
        in_specs=[SMEM_SPEC] + [VMEM_SPEC] * (2 * n_parts),
        out_specs=pl.BlockSpec((own, tile), lambda i: (0, i)),
        scratch_shapes=[pltpu.VMEM((own, depth), jnp.bfloat16)],
        cost_estimate=pl.CostEstimate(
            flops=2 * own * depth * units, bytes_accessed=4 * own * units, transcendentals=0
        ),
        compiler_params=pltpu.CompilerParams(vmem_limit_bytes=12 << 20),
    )(start.reshape(1), *lefts, *rights)


def per_device(tokens, grad_out, lang_ids, slot_ids, w_up, w_down_t):
    n_lang = lax.axis_size("lang")
    n_rep = lax.axis_size("rep")
    groups = n_lang // MODULES
    count, width = tokens.shape
    lang_index = lax.axis_index("lang")
    me = (lang_index // groups).astype(jnp.int32).reshape(1)
    member = lax.rem(lang_index, groups).astype(jnp.int32).reshape(1)
    lang_row, slot_row = lang_ids.reshape(1, count), slot_ids.reshape(1, count)
    packed_width = width + LANES

    def shift_near(value, bits):
        pairs = [
            (m * groups + g, (m ^ bits) * groups + g) for m in range(MODULES) for g in range(groups)
        ]
        return lax.ppermute(value, "lang", pairs)

    def shift_group(value, step):
        pairs = [
            (m * groups + g, m * groups + (g + step) % groups)
            for m in range(MODULES)
            for g in range(groups)
        ]
        return lax.ppermute(value, "lang", pairs)

    def shift_rep(value, step):
        return lax.ppermute(value, "rep", [(r, (r + step) % n_rep) for r in range(n_rep)])

    def over_groups(value):
        return [value] + [shift_group(value, s) for s in range(1, groups)]

    def over_near(blocks, micros):
        got = [blocks[0]] + [shift_near(blocks[z], 2 * z) for z in (1, 2, 3)]
        return local(split_kernel, [(64, packed_width)] * 2, *got, micros=micros)

    def unpack(low, high, micros):
        return unpack_parts(over_groups(low), over_groups(high), micros)

    def unpack_parts(lows, highs, micros):
        return local(
            functools.partial(unpack_near_kernel, groups),
            [(groups * PART, width)],
            *lows,
            *highs,
            micros=micros,
            kept=(0,),
        )[0]

    messages = pack(me, lang_row, slot_row, tokens, grad_out)
    x_low, x_send = over_near(messages[:4], SPLIT_COST)
    y_low, y_send = over_near(messages[4:], 0)
    w_up, w_down_t = stage(w_up, w_down_t)
    x_send, w_up, w_down_t = lax.optimization_barrier((x_send, w_up, w_down_t))
    x_high, y_high = shift_near(x_send, 1), shift_near(y_send, 1)
    if VARIANT == "G":
        (x_high,) = after((x_high,), y_send)
    if VARIANT == "F":
        (x_send2,) = after((x_high,), y_send)
    x_rows = unpack(x_low, x_high, UNPACK_COST)
    y_lows, y_highs = over_groups(y_low), over_groups(y_high)
    if VARIANT == "G":
        (x_rows,) = after((x_rows,), y_high, y_lows[-1])
    y_rows = unpack_parts(y_lows, y_highs, 0)

    depth, units = groups * PART, w_up.shape[1]
    hidden, slope, *out_parts = local(
        forward_kernel,
        shapes_of([(depth, units)])
        + [jax.ShapeDtypeStruct((depth, units), jnp.float32)]
        + shapes_of([(PART, width)] * groups),
        x_rows,
        w_up,
        w_down_t,
        micros=4,
        grant=10,
        kept=(0, 1),
    )
    (y_rows,) = after((y_rows,), *out_parts)
    d_pre, *dx_parts = local(
        backward_kernel,
        [(depth, units)] + [(PART, width)] * groups,
        y_rows,
        slope,
        w_up,
        w_down_t,
        micros=3,
        grant=10,
        kept=(0,),
    )
    own = width // n_rep
    start = (lax.axis_index("rep") * own).astype(jnp.int32)

    def over_reps(value):
        return [value] + [shift_rep(value, s) for s in range(1, n_rep)]

    kernel = functools.partial(send_kernel, groups)
    shape = (n_lang * 2 * MAIN, packed_width)
    packed = local(kernel, [shape], me, member, *out_parts, *dx_parts, scalars=2, micros=1)[0]
    y_rows, hidden, x_rows, d_pre = after((y_rows, hidden, x_rows, d_pre), packed)
    grad_down = weight_grad(start, over_reps(y_rows), over_reps(hidden), own)
    grad_up = weight_grad(start, over_reps(x_rows), over_reps(d_pre), own)
    blocks = packed.reshape(n_lang, 2 * MAIN, packed_width)
    back = lax.all_to_all(blocks, "lang", split_axis=0, concat_axis=0, tiled=True).reshape(shape)
    (back,) = after((back,), grad_down, grad_up)
    kernel = functools.partial(collect_kernel, groups)
    ffn_out, grad_tokens = local(
        kernel, [(count, width)] * 2, lang_row, slot_row, back, micros=1, grant=8
    )
    return ffn_out, grad_tokens, grad_up, grad_down


def solution(mesh):
    placed = (
        P(("lang", "rep"), None),
        P(("lang", "rep"), None),
        P(("lang", "rep")),
        P(("lang", "rep")),
        P(None, "lang"),
        P(None, "lang"),
    )
    return jax.shard_map(
        per_device,
        mesh=mesh,
        in_specs=placed,
        out_specs=(
            P(("lang", "rep"), None),
            P(("lang", "rep"), None),
            P("rep", "lang"),
            P("rep", "lang"),
        ),
        check_vma=False,
    )
```

time: 80.8 us -> 72.3 us (0.89)
  matrix products: 15.8 us -> 0 us
  Pallas kernels: 18.1 us -> 24.8 us
  waiting for transfers between devices: 17.5 us -> 22.3 us
  starting transfers between devices: 27.2 us -> 23.2 us
    dot_general x4 -> x0, matrix products: 15.8 us -> none  [dot(): lax.dot_general(a, b, (contract, ((), ())), preferred_element_type=jnp.fl...]
    all_to_all x3 -> x1, starting transfers between devices: 13.9 us -> 4.88 us  [per_device(): lax.all_to_all(blocks, 'lang', split_axis=0, concat_axis=0, tiled=True)]
    pallas_call x8 -> x10, Pallas kernels: 6.92 us -> 13.9 us  [the longest x8 8.66 us: local(): pl.pallas_call(kernel, out_shape=[pltpu.VMEM(s.shape, s.dtype) if i in ke...]
    ppermute x4 -> x8, starting transfers between devices: 7.26 us -> 12.2 us  [shift_near(): return lax.ppermute(value, 'lang', pairs)]
    ppermute x4, waiting for transfers between devices: 0.01 us -> 4.5 us  [shift_rep(): lax.ppermute(value, 'rep', [(r, (r + step) % n_rep) for r in range(n_rep)])]
    all_to_all x3 -> x1, waiting for transfers between devices: 2.4 us -> 5.73 us  [per_device(): lax.all_to_all(blocks, 'lang', split_axis=0, concat_axis=0, tiled=True)]
    ppermute x4, waiting for transfers between devices: 6.45 us -> 3.69 us  [shift_group(): return lax.ppermute(value, 'lang', pairs)]
    ppermute x4 -> x8, waiting for transfers between devices: 8.59 us -> 8.41 us  [shift_near(): return lax.ppermute(value, 'lang', pairs)]
  transfers between devices with their start and end apart: 15 -> 17, of which waited for: 5 -> 10; matrix products, arithmetic and copies ran while one was open for 20% -> 0% of each run, Pallas kernels for 18% -> 24%
where the time goes in v4:
time: 72.3 us; the launch traced here: 72.1 us
  Pallas kernels  24.8 us (34%)
  starting transfers between devices  23.2 us (32%)
  waiting for transfers between devices  22.3 us (31%)
  local copies, waits for them, and re-layouts  1.02 us (1%)
  between operations  0.76 us (1%)
    ppermute x8, starting transfers between devices, shift_near(): return lax.ppermute(value, 'lang', pairs)  12.2 us
    pallas_call x2, Pallas kernels, weight_grad(): pl.pallas_call(functools.partial(weight_grad_kernel, n_parts), out_shape=...  10.9 us
    pallas_call x8, Pallas kernels, local(): pl.pallas_call(kernel, out_shape=[pltpu.VMEM(s.shape, s.dtype) if i in ke...  8.66 us
    ppermute x8, waiting for transfers between devices, shift_near(): return lax.ppermute(value, 'lang', pairs)  8.41 us
    all_to_all x1, waiting for transfers between devices, per_device(): lax.all_to_all(blocks, 'lang', split_axis=0, concat_axis=0, tiled=True)  5.73 us
    ppermute x4, starting transfers between devices, shift_group(): return lax.ppermute(value, 'lang', pairs)  5.01 us
    all_to_all x1, starting transfers between devices, per_device(): lax.all_to_all(blocks, 'lang', split_axis=0, concat_axis=0, tiled=True)  4.88 us
    ppermute x4, waiting for transfers between devices, shift_rep(): lax.ppermute(value, 'rep', [(r, (r + step) % n_rep) for r in range(n_rep)])  4.5 us
  transfers between devices with their start and end apart: 17, of which 10 were waited for; matrix products, arithmetic and copies ran while one was open for 0% of the time, Pallas kernels for 24%

profile of v4, /device:TPU:0, one launch (start us, length us, event | category | flops | bytes accessed | tf_op | source)
XLA Modules:
  0.0 72.1 jit_solution(1493625643017646515)
XLA Ops:
  0.6 1.7 %shard_map.93 = (bf16[32,1152]{1,0:T(8,128)(2,1)S(1)}, bf16[32,1152]{1,0:T(8,128)(2,1)S(1)}, bf16[32,1152]{1,0:T(8,128)(2,1)S(1)}, bf16[32,1152]{1,0:T(8,128)(2,...) custom-call(s32[1]{0:T(128)} %bitcast.2.me_ref, ...), custom_call_target="tpu_custom_call" | custom-call | flops 2000000000 | tf_op jit(solution)/shard_map/pallas_call | solution.py:231
  2.4 3.1 %collective-permute-start = (bf16[32,1152]{1,0:T(8,128)(2,1)S(1)}, bf16[32,1152]{1,0:T(8,128)(2,1)S(1)}, u32[]{:S(2)}, u32[]{:S(2)}) collective-permute-start(bf16[32,1152]{1,0:T(8,128)(2,1)S(1)} %get-tuple-element.39), channel_id=1, source_target_pairs={{0,8},{2,10},{4,12},{6,14},{8,0},{10,2},{12,4},{14,6},{16,24},{18,... | collective-permute-start | bytes 221192 | tf_op jit(solution)/shard_map/ppermute | solution.py:284
  5.5 2.6 %collective-permute-start.1 = (bf16[32,1152]{1,0:T(8,128)(2,1)S(1)}, bf16[32,1152]{1,0:T(8,128)(2,1)S(1)}, u32[]{:S(2)}, u32[]{:S(2)}) collective-permute-start(bf16[32,1152]{1,0:T(8,128)(2,1)S(1)} %get-tuple-element.40), channel_id=1, source_target_pairs={{0,16},{2,18},{4,20},{6,22},{8,24},{10,26},{12,28},{14,30},{16,0},... | collective-permute-start | bytes 221192 | tf_op jit(solution)/shard_map/ppermute | solution.py:284
  8.1 3.5 %shard_map.95 = (bf16[1024,2048]{1,0:T(8,128)(2,1)S(1)}, bf16[1024,2048]{1,0:T(8,128)(2,1)S(1)}) custom-call(bf16[1024,2048]{1,0:T(8,128)(2,1)} %refs_0_.1, bf16[1024,2048]{1,0:T(8,128)(2,1)} %refs_1_.1), custom_call_target="tpu_custom_call" | custom-call | flops 4000000000 | tf_op jit(solution)/shard_map/pallas_call | solution.py:217
  11.6 1.7 %collective-permute-done.1.refs_2_ = bf16[32,1152]{1,0:T(8,128)(2,1)S(1)} collective-permute-done((bf16[32,1152]{1,0:T(8,128)(2,1)S(1)}, bf16[32,1152]{1,0:T(8,128)(2,1)S(1)}, u32[]{:S(2)}, u32[]{:S(2)}) %collective-permute-start.1) | collective-permute-done | bytes 73760 | tf_op jit(solution)/shard_map/ppermute | solution.py:284
  13.3 1.1 %collective-permute-done.2.refs_3_ = bf16[32,1152]{1,0:T(8,128)(2,1)S(1)} collective-permute-done((bf16[32,1152]{1,0:T(8,128)(2,1)S(1)}, bf16[32,1152]{1,0:T(8,128)(2,1)S(1)}, u32[]{:S(2)}, u32[]{:S(2)}) %collective-permute-start.2) | collective-permute-done | bytes 73760 | tf_op jit(solution)/shard_map/ppermute | solution.py:284
  14.4 1.6 %collective-permute-start.4 = (bf16[64,1152]{1,0:T(8,128)(2,1)S(1)}, bf16[64,1152]{1,0:T(8,128)(2,1)S(1)}, u32[]{:S(2)}, u32[]{:S(2)}) collective-permute-start(bf16[64,1152]{1,0:T(8,128)(2,1)S(1)} %get-tuple-element.46), channel_id=1, source_target_pairs={{0,4},{2,6},{4,0},{6,2},{8,12},{10,14},{12,8},{14,10},{16,20},{18,... | collective-permute-start | bytes 442376 | tf_op jit(solution)/shard_map/ppermute | solution.py:284
  15.9 1.1 %collective-permute-start.5 = (bf16[32,1152]{1,0:T(8,128)(2,1)S(1)}, bf16[32,1152]{1,0:T(8,128)(2,1)S(1)}, u32[]{:S(2)}, u32[]{:S(2)}) collective-permute-start(bf16[32,1152]{1,0:T(8,128)(2,1)S(1)} %get-tuple-element.48), channel_id=1, source_target_pairs={{0,8},{2,10},{4,12},{6,14},{8,0},{10,2},{12,4},{14,6},{16,24},{18,... | collective-permute-start | bytes 221192 | tf_op jit(solution)/shard_map/ppermute | solution.py:284
  17.0 1.7 %collective-permute-start.6 = (bf16[32,1152]{1,0:T(8,128)(2,1)S(1)}, bf16[32,1152]{1,0:T(8,128)(2,1)S(1)}, u32[]{:S(2)}, u32[]{:S(2)}) collective-permute-start(bf16[32,1152]{1,0:T(8,128)(2,1)S(1)} %get-tuple-element.49), channel_id=1, source_target_pairs={{0,16},{2,18},{4,20},{6,22},{8,24},{10,26},{12,28},{14,30},{16,0},... | collective-permute-start | bytes 221192 | tf_op jit(solution)/shard_map/ppermute | solution.py:284
  18.7 1.6 %collective-permute-start.7 = (bf16[32,1152]{1,0:T(8,128)(2,1)S(1)}, bf16[32,1152]{1,0:T(8,128)(2,1)S(1)}, u32[]{:S(2)}, u32[]{:S(2)}) collective-permute-start(bf16[32,1152]{1,0:T(8,128)(2,1)S(1)} %get-tuple-element.50), channel_id=1, source_target_pairs={{0,24},{2,26},{4,28},{6,30},{8,16},{10,18},{12,20},{14,22},{16,8},... | collective-permute-start | bytes 221192 | tf_op jit(solution)/shard_map/ppermute | solution.py:284
  20.3 2.8 %collective-permute-done.6.refs_2_ = bf16[32,1152]{1,0:T(8,128)(2,1)S(1)} collective-permute-done((bf16[32,1152]{1,0:T(8,128)(2,1)S(1)}, bf16[32,1152]{1,0:T(8,128)(2,1)S(1)}, u32[]{:S(2)}, u32[]{:S(2)}) %collective-permute-start.6) | collective-permute-done | bytes 73760 | tf_op jit(solution)/shard_map/ppermute | solution.py:284
  23.2 1.7 %collective-permute-done.7.refs_3_ = bf16[32,1152]{1,0:T(8,128)(2,1)S(1)} collective-permute-done((bf16[32,1152]{1,0:T(8,128)(2,1)S(1)}, bf16[32,1152]{1,0:T(8,128)(2,1)S(1)}, u32[]{:S(2)}, u32[]{:S(2)}) %collective-permute-start.7) | collective-permute-done | bytes 73760 | tf_op jit(solution)/shard_map/ppermute | solution.py:284
  24.9 0.6 collective-permute-start.9
  25.5 1.5 %collective-permute-start.3 = (bf16[64,1152]{1,0:T(8,128)(2,1)S(1)}, bf16[64,1152]{1,0:T(8,128)(2,1)S(1)}, u32[]{:S(2)}, u32[]{:S(2)}) collective-permute-start(bf16[64,1152]{1,0:T(8,128)(2,1)S(1)} %get-tuple-element.42.refs_0_), channel_id=1, source_target_pairs={{0,2},{2,0},{4,6},{6,4},{8,10},{10,8},{12,14},{14,12},{16,18},{18,... | collective-permute-start | bytes 442376 | tf_op jit(solution)/shard_map/ppermute | solution.py:292
  27.0 0.5 collective-permute-start.8
  27.5 1.5 %collective-permute-start.10 = (bf16[64,1152]{1,0:T(8,128)(2,1)S(1)}, bf16[64,1152]{1,0:T(8,128)(2,1)S(1)}, u32[]{:S(2)}, u32[]{:S(2)}) collective-permute-start(bf16[64,1152]{1,0:T(8,128)(2,1)S(1)} %get-tuple-element.53.refs_0_), channel_id=1, source_target_pairs={{0,2},{2,0},{4,6},{6,4},{8,10},{10,8},{12,14},{14,12},{16,18},{18,... | collective-permute-start | bytes 442376 | tf_op jit(solution)/shard_map/ppermute | solution.py:292
  29.0 1.1 %collective-permute-done.9.refs_2_ = bf16[64,1152]{1,0:T(8,128)(2,1)S(1)} collective-permute-done((bf16[64,1152]{1,0:T(8,128)(2,1)S(1)}, bf16[64,1152]{1,0:T(8,128)(2,1)S(1)}, u32[]{:S(2)}, u32[]{:S(2)}) %collective-permute-start.9) | collective-permute-done | bytes 147488 | tf_op jit(solution)/shard_map/ppermute | solution.py:284
  30.1 1.5 %collective-permute-start.11 = (bf16[64,1152]{1,0:T(8,128)(2,1)S(1)}, bf16[64,1152]{1,0:T(8,128)(2,1)S(1)}, u32[]{:S(2)}, u32[]{:S(2)}) collective-permute-start(bf16[64,1152]{1,0:T(8,128)(2,1)S(1)} %collective-permute-done.9.refs_2_), channel_id=1, source_target_pairs={{0,2},{2,0},{4,6},{6,4},{8,10},{10,8},{12,14},{14,12},{16,18},{18,... | collective-permute-start | bytes 442376 | tf_op jit(solution)/shard_map/ppermute | solution.py:292
  31.6 0.7 collective-permute-done.3.refs_1_
  32.3 1.6 %collective-permute-done.8.refs_3_ = bf16[64,1152]{1,0:T(8,128)(2,1)S(1)} collective-permute-done((bf16[64,1152]{1,0:T(8,128)(2,1)S(1)}, bf16[64,1152]{1,0:T(8,128)(2,1)S(1)}, u32[]{:S(2)}, u32[]{:S(2)}) %collective-permute-start.8) | collective-permute-done | bytes 147488 | tf_op jit(solution)/shard_map/ppermute | solution.py:292
  34.1 1.4 %collective-permute-done.10.refs_1_ = bf16[64,1152]{1,0:T(8,128)(2,1)S(1)} collective-permute-done((bf16[64,1152]{1,0:T(8,128)(2,1)S(1)}, bf16[64,1152]{1,0:T(8,128)(2,1)S(1)}, u32[]{:S(2)}, u32[]{:S(2)}) %collective-permute-start.10) | collective-permute-done | bytes 147488 | tf_op jit(solution)/shard_map/ppermute | solution.py:292
  35.5 3.1 %shard_map.98 = (bf16[288,2048]{1,0:T(8,128)(2,1)S(1)}, f32[288,2048]{1,0:T(8,128)S(1)}, bf16[144,1024]{1,0:T(8,128)(2,1)S(1)}, bf16[144,1024]{1,0:T(8,128)(2,1)S(1)}) custom-call(bf16[288,1024]{1,0:T(8,128)(2,1)S(1)} %shard_map.97.rows_ref.refs_0_, bf16[1024,2048]{1,0:T(8,128)(2,1)S(1)} %get-tuple-element.55.up_ref, ...), custom_call_target="tpu_custom_call" | custom-call | flops 4000000000 | tf_op jit(solution)/shard_map/pallas_call | solution.py:194
  38.7 2.6 %shard_map.100 = (bf16[288,2048]{1,0:T(8,128)(2,1)S(1)}, bf16[144,1024]{1,0:T(8,128)(2,1)S(1)}, bf16[144,1024]{1,0:T(8,128)(2,1)S(1)}) custom-call(bf16[288,1024]{1,0:T(8,128)(2,1)S(1)} %shard_map.99.rows_ref.refs_0_, f32[288,2048]{1,0:T(8,128)S(1)} %get-tuple-element.60.slope_ref, bf16[1024,2048]{1,0:T(8,128)(2,1)S(1)} %get-tuple-element.55.up_ref, ...), custom_call_target="tpu_custom_call" | custom-call | flops 3000000000 | tf_op jit(solution)/shard_map/pallas_call | solution.py:194
  41.4 1.0 %copy-done = bf16[288,2048]{1,0:T(8,128)(2,1)} copy-done((bf16[288,2048]{1,0:T(8,128)(2,1)}, bf16[288,2048]{1,0:T(8,128)(2,1)S(1)}, u32[]{:S(2)}) %copy-start) | copy-done | bytes 1179672
  42.4 1.3 %shard_map.101 = bf16[512,1152]{1,0:T(8,128)(2,1)} custom-call(s32[1]{0:T(128)} %bitcast.2.me_ref, s32[1]{0:T(128)} %bitcast.3.member_ref, bf16[144,1024]{1,0:T(8,128)(2,1)S(1)} %get-tuple-element.57.refs_0_, bf16[144,1024]{1,0:T(8,128)(2,1)S(1)} %get-tuple-element.58.refs_1_, bf16[144,1024]{1,0:T(8,128)(2,1)S(1)} %get-tuple-element.61.refs_2_, ...), custom_call_target="tpu_custom_call" | custom-call | flops 1000000000 | tf_op jit(solution)/shard_map/pallas_call | solution.py:194
  43.7 4.9 %all-to-all-start = ((bf16[16,32,1152]{2,1,0:T(8,128)(2,1)}), bf16[16,32,1152]{2,1,0:T(8,128)(2,1)S(1)}, u32[]{:S(2)}, u32[]{:S(2)}) async-start(bf16[16,32,1152]{2,1,0:T(8,128)(2,1)} %bitcast.4), calls=%async_computation | async-start | bytes 2359296 | tf_op jit(solution)/shard_map/all_to_all | solution.py:371
  48.7 0.5 collective-permute-start.15
  49.7 4.5 %collective-permute-done.12.refs_1_ = bf16[288,1024]{1,0:T(8,128)(2,1)} collective-permute-done((bf16[288,1024]{1,0:T(8,128)(2,1)S(1)}, bf16[288,1024]{1,0:T(8,128)(2,1)}, u32[]{:S(2)}, u32[]{:S(2)}) %collective-permute-start.12) | collective-permute-done | bytes 589856 | tf_op jit(solution)/shard_map/ppermute | solution.py:295
  54.2 5.5 %shard_map.102 = f32[512,2048]{1,0:T(8,128)} custom-call(s32[1]{0:T(128)} %bitcast.6.start_ref, bf16[288,1024]{1,0:T(8,128)(2,1)S(1)} %shard_map.99.rows_ref.refs_0_, bf16[288,1024]{1,0:T(8,128)(2,1)} %collective-permute-done.12.refs_1_, bf16[288,2048]{1,0:T(8,128)(2,1)S(1)} %get-tuple-element.66.refs_2_, bf16[288,2048]{1,0:T(8,128)(2,1)} %collective-permute-done.13.refs_3_), custom_call_target="tpu_custom_call" | custom-call | flops 1207959552 | bytes 4194304 | tf_op jit(solution)/shard_map/pallas_call | solution.py:255
  59.7 5.4 %shard_map.103 = f32[512,2048]{1,0:T(8,128)} custom-call(s32[1]{0:T(128)} %bitcast.6.start_ref, bf16[288,1024]{1,0:T(8,128)(2,1)S(1)} %shard_map.97.rows_ref.refs_0_, bf16[288,1024]{1,0:T(8,128)(2,1)} %collective-permute-done.14.refs_1_, bf16[288,2048]{1,0:T(8,128)(2,1)S(1)} %copy-done.1, bf16[288,2048]{1,0:T(8,128)(2,1)} %collective-permute-done.15.refs_3_), custom_call_target="tpu_custom_call" | custom-call | flops 1207959552 | bytes 4194304 | tf_op jit(solution)/shard_map/pallas_call | solution.py:255
  65.1 5.7 %all-to-all-done = bf16[16,32,1152]{2,1,0:T(8,128)(2,1)S(1)} async-done(((bf16[16,32,1152]{2,1,0:T(8,128)(2,1)}), bf16[16,32,1152]{2,1,0:T(8,128)(2,1)S(1)}, u32[]{:S(2)}, u32[]{:S(2)}) %all-to-all-start) | async-done | bytes 1179680 | tf_op jit(solution)/shard_map/all_to_all | solution.py:371
  70.8 1.3 %shard_map.104 = (bf16[128,1024]{1,0:T(8,128)(2,1)}, bf16[128,1024]{1,0:T(8,128)(2,1)}) custom-call(s32[1,128]{1,0:T(1,128)S(1)} %bitcast.9, s32[1,128]{1,0:T(1,128)S(1)} %bitcast.11, bf16[512,1152]{1,0:T(8,128)(2,1)S(1)} %bitcast.7), custom_call_target="tpu_custom_call" | custom-call | flops 1000000000 | tf_op jit(solution)/shard_map/pallas_call | solution.py:194
  (22 shorter events, 1.0 us)
Async XLA Ops:
  2.4 9.2 %collective-permute-start = (bf16[32,1152]{1,0:T(8,128)(2,1)S(1)}, bf16[32,1152]{1,0:T(8,128)(2,1)S(1)}, u32[]{:S(2)}, u32[]{:S(2)}) collective-permute-start(bf16[32,1152]{1,0:T(8,128)(2,1)S(1)} %get-tuple-element.39), channel_id=1, source_target_pairs={{0,8},{2,10},{4,12},{6,14},{8,0},{10,2},{12,4},{14,6},{16,24},{18,... | collective-permute-start | bytes 221192 | tf_op jit(solution)/shard_map/ppermute | solution.py:284
  5.5 7.8 %collective-permute-start.1 = (bf16[32,1152]{1,0:T(8,128)(2,1)S(1)}, bf16[32,1152]{1,0:T(8,128)(2,1)S(1)}, u32[]{:S(2)}, u32[]{:S(2)}) collective-permute-start(bf16[32,1152]{1,0:T(8,128)(2,1)S(1)} %get-tuple-element.40), channel_id=1, source_target_pairs={{0,16},{2,18},{4,20},{6,22},{8,24},{10,26},{12,28},{14,30},{16,0},... | collective-permute-start | bytes 221192 | tf_op jit(solution)/shard_map/ppermute | solution.py:284
  8.1 6.3 %collective-permute-start.2 = (bf16[32,1152]{1,0:T(8,128)(2,1)S(1)}, bf16[32,1152]{1,0:T(8,128)(2,1)S(1)}, u32[]{:S(2)}, u32[]{:S(2)}) collective-permute-start(bf16[32,1152]{1,0:T(8,128)(2,1)S(1)} %get-tuple-element.41), channel_id=1, source_target_pairs={{0,24},{2,26},{4,28},{6,30},{8,16},{10,18},{12,20},{14,22},{16,8},... | collective-permute-start | bytes 221192 | tf_op jit(solution)/shard_map/ppermute | solution.py:284
  14.4 12.6 %collective-permute-start.4 = (bf16[64,1152]{1,0:T(8,128)(2,1)S(1)}, bf16[64,1152]{1,0:T(8,128)(2,1)S(1)}, u32[]{:S(2)}, u32[]{:S(2)}) collective-permute-start(bf16[64,1152]{1,0:T(8,128)(2,1)S(1)} %get-tuple-element.46), channel_id=1, source_target_pairs={{0,4},{2,6},{4,0},{6,2},{8,12},{10,14},{12,8},{14,10},{16,20},{18,... | collective-permute-start | bytes 442376 | tf_op jit(solution)/shard_map/ppermute | solution.py:284
  15.9 4.4 %collective-permute-start.5 = (bf16[32,1152]{1,0:T(8,128)(2,1)S(1)}, bf16[32,1152]{1,0:T(8,128)(2,1)S(1)}, u32[]{:S(2)}, u32[]{:S(2)}) collective-permute-start(bf16[32,1152]{1,0:T(8,128)(2,1)S(1)} %get-tuple-element.48), channel_id=1, source_target_pairs={{0,8},{2,10},{4,12},{6,14},{8,0},{10,2},{12,4},{14,6},{16,24},{18,... | collective-permute-start | bytes 221192 | tf_op jit(solution)/shard_map/ppermute | solution.py:284
  17.0 6.2 %collective-permute-start.6 = (bf16[32,1152]{1,0:T(8,128)(2,1)S(1)}, bf16[32,1152]{1,0:T(8,128)(2,1)S(1)}, u32[]{:S(2)}, u32[]{:S(2)}) collective-permute-start(bf16[32,1152]{1,0:T(8,128)(2,1)S(1)} %get-tuple-element.49), channel_id=1, source_target_pairs={{0,16},{2,18},{4,20},{6,22},{8,24},{10,26},{12,28},{14,30},{16,0},... | collective-permute-start | bytes 221192 | tf_op jit(solution)/shard_map/ppermute | solution.py:284
  18.7 6.2 %collective-permute-start.7 = (bf16[32,1152]{1,0:T(8,128)(2,1)S(1)}, bf16[32,1152]{1,0:T(8,128)(2,1)S(1)}, u32[]{:S(2)}, u32[]{:S(2)}) collective-permute-start(bf16[32,1152]{1,0:T(8,128)(2,1)S(1)} %get-tuple-element.50), channel_id=1, source_target_pairs={{0,24},{2,26},{4,28},{6,30},{8,16},{10,18},{12,20},{14,22},{16,8},... | collective-permute-start | bytes 221192 | tf_op jit(solution)/shard_map/ppermute | solution.py:284
  24.9 5.2 %collective-permute-start.9 = (bf16[64,1152]{1,0:T(8,128)(2,1)S(1)}, bf16[64,1152]{1,0:T(8,128)(2,1)S(1)}, u32[]{:S(2)}, u32[]{:S(2)}) collective-permute-start(bf16[64,1152]{1,0:T(8,128)(2,1)S(1)} %get-tuple-element.51), channel_id=1, source_target_pairs={{0,4},{2,6},{4,0},{6,2},{8,12},{10,14},{12,8},{14,10},{16,20},{18,... | collective-permute-start | bytes 442376 | tf_op jit(solution)/shard_map/ppermute | solution.py:284
  25.5 6.8 %collective-permute-start.3 = (bf16[64,1152]{1,0:T(8,128)(2,1)S(1)}, bf16[64,1152]{1,0:T(8,128)(2,1)S(1)}, u32[]{:S(2)}, u32[]{:S(2)}) collective-permute-start(bf16[64,1152]{1,0:T(8,128)(2,1)S(1)} %get-tuple-element.42.refs_0_), channel_id=1, source_target_pairs={{0,2},{2,0},{4,6},{6,4},{8,10},{10,8},{12,14},{14,12},{16,18},{18,... | collective-permute-start | bytes 442376 | tf_op jit(solution)/shard_map/ppermute | solution.py:292
  27.0 6.9 %collective-permute-start.8 = (bf16[64,1152]{1,0:T(8,128)(2,1)S(1)}, bf16[64,1152]{1,0:T(8,128)(2,1)S(1)}, u32[]{:S(2)}, u32[]{:S(2)}) collective-permute-start(bf16[64,1152]{1,0:T(8,128)(2,1)S(1)} %collective-permute-done.4.refs_2_), channel_id=1, source_target_pairs={{0,2},{2,0},{4,6},{6,4},{8,10},{10,8},{12,14},{14,12},{16,18},{18,... | collective-permute-start | bytes 442376 | tf_op jit(solution)/shard_map/ppermute | solution.py:292
  27.5 8.0 %collective-permute-start.10 = (bf16[64,1152]{1,0:T(8,128)(2,1)S(1)}, bf16[64,1152]{1,0:T(8,128)(2,1)S(1)}, u32[]{:S(2)}, u32[]{:S(2)}) collective-permute-start(bf16[64,1152]{1,0:T(8,128)(2,1)S(1)} %get-tuple-element.53.refs_0_), channel_id=1, source_target_pairs={{0,2},{2,0},{4,6},{6,4},{8,10},{10,8},{12,14},{14,12},{16,18},{18,... | collective-permute-start | bytes 442376 | tf_op jit(solution)/shard_map/ppermute | solution.py:292
  30.1 8.4 %collective-permute-start.11 = (bf16[64,1152]{1,0:T(8,128)(2,1)S(1)}, bf16[64,1152]{1,0:T(8,128)(2,1)S(1)}, u32[]{:S(2)}, u32[]{:S(2)}) collective-permute-start(bf16[64,1152]{1,0:T(8,128)(2,1)S(1)} %collective-permute-done.9.refs_2_), channel_id=1, source_target_pairs={{0,2},{2,0},{4,6},{6,4},{8,10},{10,8},{12,14},{14,12},{16,18},{18,... | collective-permute-start | bytes 442376 | tf_op jit(solution)/shard_map/ppermute | solution.py:292
  41.4 1.0 %copy-start = (bf16[288,2048]{1,0:T(8,128)(2,1)}, bf16[288,2048]{1,0:T(8,128)(2,1)S(1)}, u32[]{:S(2)}) copy-start(bf16[288,2048]{1,0:T(8,128)(2,1)S(1)} %get-tuple-element.68.refs_2_) | copy-start | bytes 3538948
  43.7 27.1 %all-to-all-start = ((bf16[16,32,1152]{2,1,0:T(8,128)(2,1)}), bf16[16,32,1152]{2,1,0:T(8,128)(2,1)S(1)}, u32[]{:S(2)}, u32[]{:S(2)}) async-start(bf16[16,32,1152]{2,1,0:T(8,128)(2,1)} %bitcast.4), calls=%async_computation | async-start | bytes 2359296 | tf_op jit(solution)/shard_map/all_to_all | solution.py:371
  48.6 5.6 %collective-permute-start.13 = (bf16[288,2048]{1,0:T(8,128)(2,1)S(1)}, bf16[288,2048]{1,0:T(8,128)(2,1)}, u32[]{:S(2)}, u32[]{:S(2)}) collective-permute-start(bf16[288,2048]{1,0:T(8,128)(2,1)S(1)} %get-tuple-element.66.refs_2_), channel_id=1, source_target_pairs={{0,1},{1,0},{2,3},{3,2},{4,5},{5,4},{6,7},{7,6},{8,9},{9,8},{10,11... | collective-permute-start | bytes 3538952 | tf_op jit(solution)/shard_map/ppermute | solution.py:295
  48.7 11.0 %collective-permute-start.15 = (bf16[288,2048]{1,0:T(8,128)(2,1)}, bf16[288,2048]{1,0:T(8,128)(2,1)}, u32[]{:S(2)}, u32[]{:S(2)}) collective-permute-start(bf16[288,2048]{1,0:T(8,128)(2,1)} %copy-done), channel_id=1, source_target_pairs={{0,1},{1,0},{2,3},{3,2},{4,5},{5,4},{6,7},{7,6},{8,9},{9,8},{10,11... | collective-permute-start | bytes 3538952 | tf_op jit(solution)/shard_map/ppermute | solution.py:295
  49.2 5.0 %collective-permute-start.12 = (bf16[288,1024]{1,0:T(8,128)(2,1)S(1)}, bf16[288,1024]{1,0:T(8,128)(2,1)}, u32[]{:S(2)}, u32[]{:S(2)}) collective-permute-start(bf16[288,1024]{1,0:T(8,128)(2,1)S(1)} %shard_map.99.rows_ref.refs_0_), channel_id=1, source_target_pairs={{0,1},{1,0},{2,3},{3,2},{4,5},{5,4},{6,7},{7,6},{8,9},{9,8},{10,11... | collective-permute-start | bytes 1769480 | tf_op jit(solution)/shard_map/ppermute | solution.py:295
  49.2 10.4 %collective-permute-start.14 = (bf16[288,1024]{1,0:T(8,128)(2,1)S(1)}, bf16[288,1024]{1,0:T(8,128)(2,1)}, u32[]{:S(2)}, u32[]{:S(2)}) collective-permute-start(bf16[288,1024]{1,0:T(8,128)(2,1)S(1)} %shard_map.97.rows_ref.refs_0_), channel_id=1, source_target_pairs={{0,1},{1,0},{2,3},{3,2},{4,5},{5,4},{6,7},{7,6},{8,9},{9,8},{10,11... | collective-permute-start | bytes 1769480 | tf_op jit(solution)/shard_map/ppermute | solution.py:295
  54.2 5.5 %copy-start.1 = (bf16[288,2048]{1,0:T(8,128)(2,1)S(1)}, bf16[288,2048]{1,0:T(8,128)(2,1)}, u32[]{:S(2)}) copy-start(bf16[288,2048]{1,0:T(8,128)(2,1)} %copy-done) | copy-start | bytes 3538948
  59.6 11.2 %copy-start.2 = (s32[128]{0:T(128)S(1)}, s32[128]{0:T(128)}, u32[]{:S(2)}) copy-start(s32[128]{0:T(128)} %param.8) | copy-start | bytes 1540
  59.6 11.2 %copy-start.3 = (s32[128]{0:T(128)S(1)}, s32[128]{0:T(128)}, u32[]{:S(2)}) copy-start(s32[128]{0:T(128)} %param.9) | copy-start | bytes 1540

commit v5 on v4

--- a/solution.py
+++ b/solution.py
@@ -11,7 +11,7 @@
 TOK_DEV = 128
 CAPACITY = 18
 MAIN = 16
-SPLIT_COST = 6
+SPLIT_COST = 8
 VARIANT = "G"
 UNPACK_COST = 2
 LANES = 128
@@ -27,20 +27,23 @@
     return lax.dot_general(a, b, (contract, ((), ())), preferred_element_type=jnp.float32)
 
 
-def piece_order():
-    place = lax.broadcasted_iota(jnp.int32, (LANES, LANES), 0)
-    column = lax.broadcasted_iota(jnp.int32, (LANES, LANES), 1)
-    return ((place & 15) * 8 + (place >> 4) == column).astype(jnp.bfloat16)
-
-
-def spare_rows(cut):
-    ordered = dot(piece_order(), cut, ((1,), (0,))).astype(jnp.bfloat16)
-    return jnp.concatenate([ordered[16 * p : 16 * (p + 1)] for p in range(8)], axis=1)
+def piece_order(pieces):
+    place = lax.broadcasted_iota(jnp.int32, (16 * pieces, LANES), 0)
+    column = lax.broadcasted_iota(jnp.int32, (16 * pieces, LANES), 1)
+    piece, row = place >> 4, place & 15
+    return (((row >> 1) * 16 + (row & 1) * pieces + piece) == column).astype(jnp.bfloat16)
+
+
+def spare_rows(cut, pieces):
+    ordered = dot(piece_order(pieces), cut, ((1,), (0,))).astype(jnp.bfloat16)
+    return jnp.concatenate([ordered[16 * p : 16 * (p + 1)] for p in range(pieces)], axis=1)
 
 
 def spare_cut(rows):
-    ordered = jnp.concatenate([rows[:, LANES * p : LANES * (p + 1)] for p in range(8)], axis=0)
-    return dot(piece_order(), ordered, ((0,), (0,))).astype(jnp.bfloat16)
+    pieces = rows.shape[1] // LANES
+    ordered = [rows[:, LANES * p : LANES * (p + 1)] for p in range(pieces)]
+    ordered = jnp.concatenate(ordered, axis=0)
+    return dot(piece_order(pieces), ordered, ((0,), (0,))).astype(jnp.bfloat16)
 
 
 def slot_picks(lang, slot):
@@ -88,27 +91,27 @@
     return [slice(first, first + tile) for first in range(0, count, tile)]
 
 
-def put_shares(left_ref, right_ref, outs):
-    for part in by_tiles(right_ref.shape[0]):
-        share = dot(left_ref[...], right_ref[part], ((1,), (1,))).astype(jnp.bfloat16)
-        for g, out_ref in enumerate(outs):
-            out_ref[:, part] = share[PART * g : PART * (g + 1)]
-
-
-def forward_kernel(rows_ref, up_ref, down_ref, hidden_ref, slope_ref, *outs):
+def forward_kernel(groups, member_ref, rows_ref, up_ref, down_ref, hidden_ref, slope_ref, *outs):
     for units in by_tiles(up_ref.shape[1]):
         pre = dot(rows_ref[...], up_ref[:, units], ((1,), (0,)))
         share = 0.5 * (1.0 + lax.erf(pre * INV_ROOT_TWO))
         hidden_ref[:, units] = (pre * share).astype(jnp.bfloat16)
         slope_ref[:, units] = share + pre * jnp.exp(-0.5 * pre * pre) * INV_ROOT_TAU
-    put_shares(hidden_ref, down_ref, outs)
+    for s, out_ref in enumerate(outs):
+        width = out_ref.shape[1]
+        first = pl.multiple_of(lax.rem(member_ref[0] + s, groups) * width, LANES)
+        weights = down_ref[pl.ds(first, width)]
+        out_ref[...] = dot(hidden_ref[...], weights, ((1,), (1,))).astype(jnp.bfloat16)
 
 
 def backward_kernel(rows_ref, slope_ref, up_ref, down_ref, d_pre_ref, *outs):
     for units in by_tiles(up_ref.shape[1]):
         d_hidden = dot(rows_ref[...], down_ref[:, units], ((1,), (0,)))
         d_pre_ref[:, units] = (d_hidden * slope_ref[:, units]).astype(jnp.bfloat16)
-    put_shares(d_pre_ref, up_ref, outs)
+    for part in by_tiles(up_ref.shape[0]):
+        share = dot(d_pre_ref[...], up_ref[part], ((1,), (1,))).astype(jnp.bfloat16)
+        for g, out_ref in enumerate(outs):
+            out_ref[:, part] = share[PART * g : PART * (g + 1)]
 
 
 NEAR = (0, 2, 4, 6, 1, 3, 5, 7)
@@ -117,7 +120,7 @@
 def put_rows(packed, rows_ref, first):
     width = rows_ref.shape[1]
     rows_ref[first : first + ROWS] = packed[:, :width]
-    rows_ref[first + ROWS : first + PART] = spare_rows(packed[:, width:])
+    rows_ref[first + ROWS : first + PART] = spare_rows(packed[:, width:], width // LANES)
 
 
 def unpack_near_kernel(groups, *refs):
@@ -127,34 +130,48 @@
 
 
 def send_kernel(groups, me_ref, member_ref, *refs):
-    packed_ref = refs[-1]
-    for i, rows_ref in enumerate(refs[:-1]):
-        array, s = divmod(i, groups)
+    sums, dx_refs, packed_ref = refs[:groups], refs[groups:-1], refs[-1]
+    for s in range(groups):
         member = lax.rem(member_ref[0] + groups - s, groups)
-        rows = rows_ref[...]
-        width = rows.shape[1]
-        cut = spare_cut(rows[ROWS:])
-        for j, near in enumerate(NEAR):
-            device = (me_ref[0] ^ near) * groups + member
-            at = pl.ds(pl.multiple_of((device * 2 + array) * MAIN, MAIN), MAIN)
-            packed_ref[at, :width] = rows[MAIN * j : MAIN * (j + 1)]
-            packed_ref[at, width:] = cut[MAIN * j : MAIN * (j + 1)]
-
-
-def collect_kernel(groups, lang_ref, slot_ref, packed_ref, *outs):
-    picks = slot_picks(lang_ref[...], slot_ref[...])
-    for array, values_ref in enumerate(outs):
-        width = values_ref.shape[1]
-        blocks = []
-        for m in range(MODULES):
-            total = 0.0
-            for g in range(groups):
-                first = ((m * groups + g) * 2 + array) * MAIN
-                total = total + packed_ref[first : first + MAIN].astype(jnp.float32)
-            blocks.append(total.astype(jnp.bfloat16))
-        packed = jnp.concatenate(blocks, axis=0)
-        rows = jnp.concatenate([packed[:, :width], spare_rows(packed[:, width:])], axis=0)
-        values_ref[...] = dot(picks, rows, ((0,), (0,))).astype(jnp.bfloat16)
+        total = 0.0
+        for t in range(groups):
+            part = PART * ((s - t) % groups)
+            total = total + sums[t][part : part + PART].astype(jnp.float32)
+        first = 0
+        for rows in (dx_refs[s][...], total.astype(jnp.bfloat16)):
+            width = rows.shape[1]
+            cut = spare_cut(rows[ROWS:])
+            for j, near in enumerate(NEAR):
+                device = (me_ref[0] ^ near) * groups + member
+                at = pl.ds(pl.multiple_of(device * MAIN, MAIN), MAIN)
+                main = slice(MAIN * j, MAIN * (j + 1))
+                packed_ref[at, first : first + width] = rows[main]
+                packed_ref[at, first + width : first + width + LANES] = cut[main]
+            first += width + LANES
+
+
+def collect_kernel(groups, lang_ref, slot_ref, packed_ref, out_ref, dx_ref):
+    picks = slot_picks(lang_ref[...], slot_ref[...]).T
+    width = dx_ref.shape[1]
+    share = width // groups
+    middle = width + LANES
+
+    def blocks(g, columns):
+        firsts = [MAIN * (m * groups + g) for m in range(MODULES)]
+        return jnp.concatenate([packed_ref[f : f + MAIN, columns] for f in firsts], axis=0)
+
+    def pick(main, cut):
+        rows = jnp.concatenate([main, spare_rows(cut, main.shape[1] // LANES)], axis=0)
+        return dot(picks, rows, ((1,), (0,))).astype(jnp.bfloat16)
+
+    total = 0.0
+    for g in range(groups):
+        total = total + blocks(g, slice(0, middle)).astype(jnp.float32)
+        main = blocks(g, slice(middle, middle + share))
+        cut = blocks(g, slice(middle + share, middle + share + LANES))
+        out_ref[:, share * g : share * (g + 1)] = pick(main, cut)
+    total = total.astype(jnp.bfloat16)
+    dx_ref[...] = pick(total[:, :width], total[:, width:])
 
 
 def weight_grad_kernel(n_parts, start_ref, *refs):
@@ -315,30 +332,29 @@
         )[0]
 
     messages = pack(me, lang_row, slot_row, tokens, grad_out)
-    x_low, x_send = over_near(messages[:4], SPLIT_COST)
-    y_low, y_send = over_near(messages[4:], 0)
+    x_low, x_send = over_near(messages[:4], 0)
+    y_low, y_send = over_near(messages[4:], SPLIT_COST)
     w_up, w_down_t = stage(w_up, w_down_t)
-    x_send, w_up, w_down_t = lax.optimization_barrier((x_send, w_up, w_down_t))
+    (x_send,) = after((x_send,), w_up)
     x_high, y_high = shift_near(x_send, 1), shift_near(y_send, 1)
-    if VARIANT == "G":
-        (x_high,) = after((x_high,), y_send)
-    if VARIANT == "F":
-        (x_send2,) = after((x_high,), y_send)
-    x_rows = unpack(x_low, x_high, UNPACK_COST)
+    x_lows = over_groups(x_low)
+    (x_high,) = after((x_high,), y_send, x_lows[-1])
+    x_rows = unpack_parts(x_lows, over_groups(x_high), UNPACK_COST)
     y_lows, y_highs = over_groups(y_low), over_groups(y_high)
-    if VARIANT == "G":
-        (x_rows,) = after((x_rows,), y_high, y_lows[-1])
+    (x_rows,) = after((x_rows,), y_high)
     y_rows = unpack_parts(y_lows, y_highs, 0)
 
     depth, units = groups * PART, w_up.shape[1]
     hidden, slope, *out_parts = local(
-        forward_kernel,
+        functools.partial(forward_kernel, groups),
         shapes_of([(depth, units)])
         + [jax.ShapeDtypeStruct((depth, units), jnp.float32)]
-        + shapes_of([(PART, width)] * groups),
+        + shapes_of([(depth, width // groups)] * groups),
+        member,
         x_rows,
         w_up,
         w_down_t,
+        scalars=1,
         micros=4,
         grant=10,
         kept=(0, 1),
@@ -361,13 +377,14 @@
     def over_reps(value):
         return [value] + [shift_rep(value, s) for s in range(1, n_rep)]
 
+    sums = [out_parts[0]] + [shift_group(out_parts[s], s) for s in range(1, groups)]
     kernel = functools.partial(send_kernel, groups)
-    shape = (n_lang * 2 * MAIN, packed_width)
-    packed = local(kernel, [shape], me, member, *out_parts, *dx_parts, scalars=2, micros=1)[0]
+    shape = (n_lang * MAIN, packed_width + width // groups + LANES)
+    packed = local(kernel, [shape], me, member, *sums, *dx_parts, scalars=2, micros=1)[0]
     y_rows, hidden, x_rows, d_pre = after((y_rows, hidden, x_rows, d_pre), packed)
     grad_down = weight_grad(start, over_reps(y_rows), over_reps(hidden), own)
     grad_up = weight_grad(start, over_reps(x_rows), over_reps(d_pre), own)
-    blocks = packed.reshape(n_lang, 2 * MAIN, packed_width)
+    blocks = packed.reshape(n_lang, MAIN, shape[1])
     back = lax.all_to_all(blocks, "lang", split_axis=0, concat_axis=0, tiled=True).reshape(shape)
     (back,) = after((back,), grad_down, grad_up)
     kernel = functools.partial(collect_kernel, groups)

time: 72.3 us -> 69.3 us (0.959)
  waiting for transfers between devices: 22.3 us -> 17.2 us
  starting transfers between devices: 23.2 us -> 25.2 us
    ppermute x8, waiting for transfers between devices: 8.41 us -> 3.46 us  [shift_near(): return lax.ppermute(value, 'lang', pairs)]
    all_to_all x1, waiting for transfers between devices: 5.73 us -> 2.77 us  [per_device(): lax.all_to_all(blocks, 'lang', split_axis=0, concat_axis=0, tiled=True)]
    ppermute x4 -> x5, waiting for transfers between devices: 3.69 us -> 6.46 us  [shift_group(): return lax.ppermute(value, 'lang', pairs)]
    ppermute x8, starting transfers between devices: 12.2 us -> 13.3 us  [shift_near(): return lax.ppermute(value, 'lang', pairs)]
    all_to_all x1, starting transfers between devices: 4.88 us -> 5.93 us  [per_device(): lax.all_to_all(blocks, 'lang', split_axis=0, concat_axis=0, tiled=True)]
    ppermute x4 -> x5, starting transfers between devices: 5.01 us -> 4.9 us  [shift_group(): return lax.ppermute(value, 'lang', pairs)]
  transfers between devices with their start and end apart: 17 -> 18, of which waited for: 10 -> 7; matrix products, arithmetic and copies ran while one was open for 0% -> 0% of each run, Pallas kernels for 24% -> 29%
where the time goes in v5:
time: 69.3 us; the launch traced here: 69 us
  starting transfers between devices  25.2 us (36%)
  Pallas kernels  24.9 us (36%)
  waiting for transfers between devices  17.2 us (25%)
  local copies, waits for them, and re-layouts  0.91 us (1%)
  between operations  0.77 us (1%)
    ppermute x8, starting transfers between devices, shift_near(): return lax.ppermute(value, 'lang', pairs)  13.3 us
    pallas_call x2, Pallas kernels, weight_grad(): pl.pallas_call(functools.partial(weight_grad_kernel, n_parts), out_shape=...  10.8 us
    pallas_call x8, Pallas kernels, local(): pl.pallas_call(kernel, out_shape=[pltpu.VMEM(s.shape, s.dtype) if i in ke...  8.93 us
    ppermute x5, waiting for transfers between devices, shift_group(): return lax.ppermute(value, 'lang', pairs)  6.46 us
    all_to_all x1, starting transfers between devices, per_device(): lax.all_to_all(blocks, 'lang', split_axis=0, concat_axis=0, tiled=True)  5.93 us
    ppermute x5, starting transfers between devices, shift_group(): return lax.ppermute(value, 'lang', pairs)  4.9 us
    ppermute x4, waiting for transfers between devices, shift_rep(): lax.ppermute(value, 'rep', [(r, (r + step) % n_rep) for r in range(n_rep)])  4.5 us
    pallas_call x1, Pallas kernels, stage(): pl.pallas_call(stage_kernel, out_shape=[pltpu.VMEM(w.shape, w.dtype) for...  3.48 us
  transfers between devices with their start and end apart: 18, of which 7 were waited for; matrix products, arithmetic and copies ran while one was open for 0% of the time, Pallas kernels for 29%

profile of v5, /device:TPU:0, one launch (start us, length us, event | category | flops | bytes accessed | tf_op | source)
XLA Modules:
  0.0 69.0 jit_solution(18075768053284579925)
XLA Ops:
  0.6 1.7 %shard_map.93 = (bf16[32,1152]{1,0:T(8,128)(2,1)S(1)}, bf16[32,1152]{1,0:T(8,128)(2,1)S(1)}, bf16[32,1152]{1,0:T(8,128)(2,1)S(1)}, bf16[32,1152]{1,0:T(8,128)(2,...) custom-call(s32[1]{0:T(128)} %bitcast.2.me_ref, ...), custom_call_target="tpu_custom_call" | custom-call | flops 2000000000 | tf_op jit(solution)/shard_map/pallas_call | solution.py:248
  2.4 3.1 %collective-permute-start = (bf16[32,1152]{1,0:T(8,128)(2,1)S(1)}, bf16[32,1152]{1,0:T(8,128)(2,1)S(1)}, u32[]{:S(2)}, u32[]{:S(2)}) collective-permute-start(bf16[32,1152]{1,0:T(8,128)(2,1)S(1)} %get-tuple-element.37), channel_id=1, source_target_pairs={{0,8},{2,10},{4,12},{6,14},{8,0},{10,2},{12,4},{14,6},{16,24},{18,... | collective-permute-start | bytes 221192 | tf_op jit(solution)/shard_map/ppermute | solution.py:301
  5.5 2.6 %collective-permute-start.1 = (bf16[32,1152]{1,0:T(8,128)(2,1)S(1)}, bf16[32,1152]{1,0:T(8,128)(2,1)S(1)}, u32[]{:S(2)}, u32[]{:S(2)}) collective-permute-start(bf16[32,1152]{1,0:T(8,128)(2,1)S(1)} %get-tuple-element.38), channel_id=1, source_target_pairs={{0,16},{2,18},{4,20},{6,22},{8,24},{10,26},{12,28},{14,30},{16,0},... | collective-permute-start | bytes 221192 | tf_op jit(solution)/shard_map/ppermute | solution.py:301
  8.1 0.9 %collective-permute-start.5 = (bf16[32,1152]{1,0:T(8,128)(2,1)S(1)}, bf16[32,1152]{1,0:T(8,128)(2,1)S(1)}, u32[]{:S(2)}, u32[]{:S(2)}) collective-permute-start(bf16[32,1152]{1,0:T(8,128)(2,1)S(1)} %get-tuple-element.45), channel_id=1, source_target_pairs={{0,8},{2,10},{4,12},{6,14},{8,0},{10,2},{12,4},{14,6},{16,24},{18,... | collective-permute-start | bytes 221192 | tf_op jit(solution)/shard_map/ppermute | solution.py:301
  9.0 3.5 %collective-permute-start.6 = (bf16[32,1152]{1,0:T(8,128)(2,1)S(1)}, bf16[32,1152]{1,0:T(8,128)(2,1)S(1)}, u32[]{:S(2)}, u32[]{:S(2)}) collective-permute-start(bf16[32,1152]{1,0:T(8,128)(2,1)S(1)} %get-tuple-element.46), channel_id=1, source_target_pairs={{0,16},{2,18},{4,20},{6,22},{8,24},{10,26},{12,28},{14,30},{16,0},... | collective-permute-start | bytes 221192 | tf_op jit(solution)/shard_map/ppermute | solution.py:301
  12.6 3.5 %shard_map.95 = (bf16[1024,2048]{1,0:T(8,128)(2,1)S(1)}, bf16[1024,2048]{1,0:T(8,128)(2,1)S(1)}) custom-call(bf16[1024,2048]{1,0:T(8,128)(2,1)} %refs_0_.1, bf16[1024,2048]{1,0:T(8,128)(2,1)} %refs_1_.1), custom_call_target="tpu_custom_call" | custom-call | flops 4000000000 | tf_op jit(solution)/shard_map/pallas_call | solution.py:234
  16.1 1.7 %collective-permute-start.3 = (bf16[64,1152]{1,0:T(8,128)(2,1)S(1)}, bf16[64,1152]{1,0:T(8,128)(2,1)S(1)}, u32[]{:S(2)}, u32[]{:S(2)}) collective-permute-start(bf16[64,1152]{1,0:T(8,128)(2,1)S(1)} %get-tuple-element.40.refs_0_), channel_id=1, source_target_pairs={{0,2},{2,0},{4,6},{6,4},{8,10},{10,8},{12,14},{14,12},{16,18},{18,... | collective-permute-start | bytes 442376 | tf_op jit(solution)/shard_map/ppermute | solution.py:309
  17.8 1.5 %collective-permute-start.4 = (bf16[64,1152]{1,0:T(8,128)(2,1)S(1)}, bf16[64,1152]{1,0:T(8,128)(2,1)S(1)}, u32[]{:S(2)}, u32[]{:S(2)}) collective-permute-start(bf16[64,1152]{1,0:T(8,128)(2,1)S(1)} %get-tuple-element.43), channel_id=1, source_target_pairs={{0,4},{2,6},{4,0},{6,2},{8,12},{10,14},{12,8},{14,10},{16,20},{18,... | collective-permute-start | bytes 442376 | tf_op jit(solution)/shard_map/ppermute | solution.py:301
  19.3 1.1 %collective-permute-done.6.refs_2_ = bf16[32,1152]{1,0:T(8,128)(2,1)S(1)} collective-permute-done((bf16[32,1152]{1,0:T(8,128)(2,1)S(1)}, bf16[32,1152]{1,0:T(8,128)(2,1)S(1)}, u32[]{:S(2)}, u32[]{:S(2)}) %collective-permute-start.6) | collective-permute-done | bytes 73760 | tf_op jit(solution)/shard_map/ppermute | solution.py:301
  20.4 1.6 %collective-permute-start.9 = (bf16[64,1152]{1,0:T(8,128)(2,1)S(1)}, bf16[64,1152]{1,0:T(8,128)(2,1)S(1)}, u32[]{:S(2)}, u32[]{:S(2)}) collective-permute-start(bf16[64,1152]{1,0:T(8,128)(2,1)S(1)} %get-tuple-element.48), channel_id=1, source_target_pairs={{0,4},{2,6},{4,0},{6,2},{8,12},{10,14},{12,8},{14,10},{16,20},{18,... | collective-permute-start | bytes 442376 | tf_op jit(solution)/shard_map/ppermute | solution.py:301
  22.0 2.4 %collective-permute-done.4.refs_2_ = bf16[64,1152]{1,0:T(8,128)(2,1)S(1)} collective-permute-done((bf16[64,1152]{1,0:T(8,128)(2,1)S(1)}, bf16[64,1152]{1,0:T(8,128)(2,1)S(1)}, u32[]{:S(2)}, u32[]{:S(2)}) %collective-permute-start.4) | collective-permute-done | bytes 147488 | tf_op jit(solution)/shard_map/ppermute | solution.py:301
  24.4 0.3 collective-permute-start.8
  24.6 1.8 %collective-permute-start.11 = (bf16[64,1152]{1,0:T(8,128)(2,1)S(1)}, bf16[64,1152]{1,0:T(8,128)(2,1)S(1)}, u32[]{:S(2)}, u32[]{:S(2)}) collective-permute-start(bf16[64,1152]{1,0:T(8,128)(2,1)S(1)} %get-tuple-element.54.refs_0_), channel_id=1, source_target_pairs={{0,2},{2,0},{4,6},{6,4},{8,10},{10,8},{12,14},{14,12},{16,18},{18,... | collective-permute-start | bytes 442376 | tf_op jit(solution)/shard_map/ppermute | solution.py:309
  26.4 0.7 %collective-permute-start.12 = (bf16[64,1152]{1,0:T(8,128)(2,1)S(1)}, bf16[64,1152]{1,0:T(8,128)(2,1)S(1)}, u32[]{:S(2)}, u32[]{:S(2)}) collective-permute-start(bf16[64,1152]{1,0:T(8,128)(2,1)S(1)} %collective-permute-done.9.refs_2_), channel_id=1, source_target_pairs={{0,2},{2,0},{4,6},{6,4},{8,10},{10,8},{12,14},{14,12},{16,18},{18,... | collective-permute-start | bytes 442376 | tf_op jit(solution)/shard_map/ppermute | solution.py:309
  27.1 3.0 %collective-permute-done.8.refs_3_ = bf16[64,1152]{1,0:T(8,128)(2,1)S(1)} collective-permute-done((bf16[64,1152]{1,0:T(8,128)(2,1)S(1)}, bf16[64,1152]{1,0:T(8,128)(2,1)S(1)}, u32[]{:S(2)}, u32[]{:S(2)}) %collective-permute-start.8) | collective-permute-done | bytes 147488 | tf_op jit(solution)/shard_map/ppermute | solution.py:309
  30.1 0.2 shard_map.97.rows_ref.refs_0_
  30.3 3.1 %shard_map.98 = (bf16[288,2048]{1,0:T(8,128)(2,1)S(1)}, f32[288,2048]{1,0:T(8,128)S(1)}, bf16[288,512]{1,0:T(8,128)(2,1)S(1)}, bf16[288,512]{1,0:T(8,128)(2,1)S(1)}) custom-call(s32[1]{0:T(128)} %bitcast.3.member_ref, bf16[288,1024]{1,0:T(8,128)(2,1)S(1)} %shard_map.97.rows_ref.refs_0_, bf16[1024,2048]{1,0:T(8,128)(2,1)S(1)} %get-tuple-element.42.up_ref, ...), custom_call_target="tpu_custom_call" | custom-call | flops 4000000000 | tf_op jit(solution)/shard_map/pallas_call | solution.py:211
  33.4 0.5 collective-permute-start.10
  33.9 2.1 %collective-permute-done.12.refs_3_ = bf16[64,1152]{1,0:T(8,128)(2,1)S(1)} collective-permute-done((bf16[64,1152]{1,0:T(8,128)(2,1)S(1)}, bf16[64,1152]{1,0:T(8,128)(2,1)S(1)}, u32[]{:S(2)}, u32[]{:S(2)}) %collective-permute-start.12) | collective-permute-done | bytes 147488 | tf_op jit(solution)/shard_map/ppermute | solution.py:309
  36.0 0.2 shard_map.99.rows_ref.refs_0_
  36.2 2.6 %shard_map.100 = (bf16[288,2048]{1,0:T(8,128)(2,1)S(1)}, bf16[144,1024]{1,0:T(8,128)(2,1)S(1)}, bf16[144,1024]{1,0:T(8,128)(2,1)S(1)}) custom-call(bf16[288,1024]{1,0:T(8,128)(2,1)S(1)} %shard_map.99.rows_ref.refs_0_, f32[288,2048]{1,0:T(8,128)S(1)} %get-tuple-element.56.slope_ref, bf16[1024,2048]{1,0:T(8,128)(2,1)S(1)} %get-tuple-element.42.up_ref, ...), custom_call_target="tpu_custom_call" | custom-call | flops 3000000000 | tf_op jit(solution)/shard_map/pallas_call | solution.py:211
  38.8 1.4 %collective-permute-done.10.refs_1_ = bf16[288,512]{1,0:T(8,128)(2,1)S(1)} collective-permute-done((bf16[288,512]{1,0:T(8,128)(2,1)S(1)}, bf16[288,512]{1,0:T(8,128)(2,1)S(1)}, u32[]{:S(2)}, u32[]{:S(2)}) %collective-permute-start.10) | collective-permute-done | bytes 294944 | tf_op jit(solution)/shard_map/ppermute | solution.py:309
  40.1 0.3 shard_map.101
  40.4 0.9 %copy-done = bf16[256,1792]{1,0:T(8,128)(2,1)} copy-done((bf16[256,1792]{1,0:T(8,128)(2,1)}, bf16[256,1792]{1,0:T(8,128)(2,1)S(1)}, u32[]{:S(2)}) %copy-start) | copy-done | bytes 917528
  41.3 5.9 %all-to-all-start = ((bf16[16,16,1792]{2,1,0:T(8,128)(2,1)}), bf16[16,16,1792]{2,1,0:T(8,128)(2,1)}, u32[]{:S(2)}, u32[]{:S(2)}) async-start(bf16[16,16,1792]{2,1,0:T(8,128)(2,1)} %bitcast.7), calls=%async_computation | async-start | bytes 1835008 | tf_op jit(solution)/shard_map/all_to_all | solution.py:388
  47.4 0.5 collective-permute-start.16
  47.9 0.4 collective-permute-start.15
  48.4 4.5 %collective-permute-done.13.refs_1_ = bf16[288,1024]{1,0:T(8,128)(2,1)} collective-permute-done((bf16[288,1024]{1,0:T(8,128)(2,1)S(1)}, bf16[288,1024]{1,0:T(8,128)(2,1)}, u32[]{:S(2)}, u32[]{:S(2)}) %collective-permute-start.13) | collective-permute-done | bytes 589856 | tf_op jit(solution)/shard_map/ppermute | solution.py:312
  52.9 5.4 %shard_map.102 = f32[512,2048]{1,0:T(8,128)} custom-call(s32[1]{0:T(128)} %bitcast.6.start_ref, bf16[288,1024]{1,0:T(8,128)(2,1)S(1)} %shard_map.99.rows_ref.refs_0_, bf16[288,1024]{1,0:T(8,128)(2,1)} %collective-permute-done.13.refs_1_, bf16[288,2048]{1,0:T(8,128)(2,1)S(1)} %get-tuple-element.62.refs_2_, bf16[288,2048]{1,0:T(8,128)(2,1)} %collective-permute-done.14.refs_3_), custom_call_target="tpu_custom_call" | custom-call | flops 1207959552 | bytes 4194304 | tf_op jit(solution)/shard_map/pallas_call | solution.py:272
  58.3 5.4 %shard_map.103 = f32[512,2048]{1,0:T(8,128)} custom-call(s32[1]{0:T(128)} %bitcast.6.start_ref, bf16[288,1024]{1,0:T(8,128)(2,1)S(1)} %shard_map.97.rows_ref.refs_0_, bf16[288,1024]{1,0:T(8,128)(2,1)} %collective-permute-done.15.refs_1_, bf16[288,2048]{1,0:T(8,128)(2,1)S(1)} %get-tuple-element.64.refs_2_, bf16[288,2048]{1,0:T(8,128)(2,1)} %collective-permute-done.16.refs_3_), custom_call_target="tpu_custom_call" | custom-call | flops 1207959552 | bytes 4194304 | tf_op jit(solution)/shard_map/pallas_call | solution.py:272
  63.7 2.8 %all-to-all-done = bf16[16,16,1792]{2,1,0:T(8,128)(2,1)} async-done(((bf16[16,16,1792]{2,1,0:T(8,128)(2,1)}), bf16[16,16,1792]{2,1,0:T(8,128)(2,1)}, u32[]{:S(2)}, u32[]{:S(2)}) %all-to-all-start) | async-done | bytes 917536 | tf_op jit(solution)/shard_map/all_to_all | solution.py:388
  66.4 2.6 %shard_map.104 = (bf16[128,1024]{1,0:T(8,128)(2,1)}, bf16[128,1024]{1,0:T(8,128)(2,1)}) custom-call(s32[1,128]{1,0:T(1,128)S(1)} %bitcast.9, s32[1,128]{1,0:T(1,128)S(1)} %bitcast.11, bf16[256,1792]{1,0:T(8,128)(2,1)} %bitcast.5.packed_ref), custom_call_target="tpu_custom_call" | custom-call | flops 1000000000 | tf_op jit(solution)/shard_map/pallas_call | solution.py:211
  (22 shorter events, 0.4 us)
Async XLA Ops:
  2.4 10.1 %collective-permute-start = (bf16[32,1152]{1,0:T(8,128)(2,1)S(1)}, bf16[32,1152]{1,0:T(8,128)(2,1)S(1)}, u32[]{:S(2)}, u32[]{:S(2)}) collective-permute-start(bf16[32,1152]{1,0:T(8,128)(2,1)S(1)} %get-tuple-element.37), channel_id=1, source_target_pairs={{0,8},{2,10},{4,12},{6,14},{8,0},{10,2},{12,4},{14,6},{16,24},{18,... | collective-permute-start | bytes 221192 | tf_op jit(solution)/shard_map/ppermute | solution.py:301
  5.5 10.6 %collective-permute-start.1 = (bf16[32,1152]{1,0:T(8,128)(2,1)S(1)}, bf16[32,1152]{1,0:T(8,128)(2,1)S(1)}, u32[]{:S(2)}, u32[]{:S(2)}) collective-permute-start(bf16[32,1152]{1,0:T(8,128)(2,1)S(1)} %get-tuple-element.38), channel_id=1, source_target_pairs={{0,16},{2,18},{4,20},{6,22},{8,24},{10,26},{12,28},{14,30},{16,0},... | collective-permute-start | bytes 221192 | tf_op jit(solution)/shard_map/ppermute | solution.py:301
  8.1 8.0 %collective-permute-start.2 = (bf16[32,1152]{1,0:T(8,128)(2,1)S(1)}, bf16[32,1152]{1,0:T(8,128)(2,1)S(1)}, u32[]{:S(2)}, u32[]{:S(2)}) collective-permute-start(bf16[32,1152]{1,0:T(8,128)(2,1)S(1)} %get-tuple-element.39), channel_id=1, source_target_pairs={{0,24},{2,26},{4,28},{6,30},{8,16},{10,18},{12,20},{14,22},{16,8},... | collective-permute-start | bytes 221192 | tf_op jit(solution)/shard_map/ppermute | solution.py:301
  8.1 11.2 %collective-permute-start.5 = (bf16[32,1152]{1,0:T(8,128)(2,1)S(1)}, bf16[32,1152]{1,0:T(8,128)(2,1)S(1)}, u32[]{:S(2)}, u32[]{:S(2)}) collective-permute-start(bf16[32,1152]{1,0:T(8,128)(2,1)S(1)} %get-tuple-element.45), channel_id=1, source_target_pairs={{0,8},{2,10},{4,12},{6,14},{8,0},{10,2},{12,4},{14,6},{16,24},{18,... | collective-permute-start | bytes 221192 | tf_op jit(solution)/shard_map/ppermute | solution.py:301
  9.0 11.4 %collective-permute-start.6 = (bf16[32,1152]{1,0:T(8,128)(2,1)S(1)}, bf16[32,1152]{1,0:T(8,128)(2,1)S(1)}, u32[]{:S(2)}, u32[]{:S(2)}) collective-permute-start(bf16[32,1152]{1,0:T(8,128)(2,1)S(1)} %get-tuple-element.46), channel_id=1, source_target_pairs={{0,16},{2,18},{4,20},{6,22},{8,24},{10,26},{12,28},{14,30},{16,0},... | collective-permute-start | bytes 221192 | tf_op jit(solution)/shard_map/ppermute | solution.py:301
  12.5 7.9 %collective-permute-start.7 = (bf16[32,1152]{1,0:T(8,128)(2,1)S(1)}, bf16[32,1152]{1,0:T(8,128)(2,1)S(1)}, u32[]{:S(2)}, u32[]{:S(2)}) collective-permute-start(bf16[32,1152]{1,0:T(8,128)(2,1)S(1)} %get-tuple-element.47), channel_id=1, source_target_pairs={{0,24},{2,26},{4,28},{6,30},{8,16},{10,18},{12,20},{14,22},{16,8},... | collective-permute-start | bytes 221192 | tf_op jit(solution)/shard_map/ppermute | solution.py:301
  16.1 5.9 %collective-permute-start.3 = (bf16[64,1152]{1,0:T(8,128)(2,1)S(1)}, bf16[64,1152]{1,0:T(8,128)(2,1)S(1)}, u32[]{:S(2)}, u32[]{:S(2)}) collective-permute-start(bf16[64,1152]{1,0:T(8,128)(2,1)S(1)} %get-tuple-element.40.refs_0_), channel_id=1, source_target_pairs={{0,2},{2,0},{4,6},{6,4},{8,10},{10,8},{12,14},{14,12},{16,18},{18,... | collective-permute-start | bytes 442376 | tf_op jit(solution)/shard_map/ppermute | solution.py:309
  17.8 6.6 %collective-permute-start.4 = (bf16[64,1152]{1,0:T(8,128)(2,1)S(1)}, bf16[64,1152]{1,0:T(8,128)(2,1)S(1)}, u32[]{:S(2)}, u32[]{:S(2)}) collective-permute-start(bf16[64,1152]{1,0:T(8,128)(2,1)S(1)} %get-tuple-element.43), channel_id=1, source_target_pairs={{0,4},{2,6},{4,0},{6,2},{8,12},{10,14},{12,8},{14,10},{16,20},{18,... | collective-permute-start | bytes 442376 | tf_op jit(solution)/shard_map/ppermute | solution.py:301
  20.4 6.0 %collective-permute-start.9 = (bf16[64,1152]{1,0:T(8,128)(2,1)S(1)}, bf16[64,1152]{1,0:T(8,128)(2,1)S(1)}, u32[]{:S(2)}, u32[]{:S(2)}) collective-permute-start(bf16[64,1152]{1,0:T(8,128)(2,1)S(1)} %get-tuple-element.48), channel_id=1, source_target_pairs={{0,4},{2,6},{4,0},{6,2},{8,12},{10,14},{12,8},{14,10},{16,20},{18,... | collective-permute-start | bytes 442376 | tf_op jit(solution)/shard_map/ppermute | solution.py:301
  24.4 5.7 %collective-permute-start.8 = (bf16[64,1152]{1,0:T(8,128)(2,1)S(1)}, bf16[64,1152]{1,0:T(8,128)(2,1)S(1)}, u32[]{:S(2)}, u32[]{:S(2)}) collective-permute-start(bf16[64,1152]{1,0:T(8,128)(2,1)S(1)} %collective-permute-done.4.refs_2_), channel_id=1, source_target_pairs={{0,2},{2,0},{4,6},{6,4},{8,10},{10,8},{12,14},{14,12},{16,18},{18,... | collective-permute-start | bytes 442376 | tf_op jit(solution)/shard_map/ppermute | solution.py:309
  24.6 9.2 %collective-permute-start.11 = (bf16[64,1152]{1,0:T(8,128)(2,1)S(1)}, bf16[64,1152]{1,0:T(8,128)(2,1)S(1)}, u32[]{:S(2)}, u32[]{:S(2)}) collective-permute-start(bf16[64,1152]{1,0:T(8,128)(2,1)S(1)} %get-tuple-element.54.refs_0_), channel_id=1, source_target_pairs={{0,2},{2,0},{4,6},{6,4},{8,10},{10,8},{12,14},{14,12},{16,18},{18,... | collective-permute-start | bytes 442376 | tf_op jit(solution)/shard_map/ppermute | solution.py:309
  26.4 9.6 %collective-permute-start.12 = (bf16[64,1152]{1,0:T(8,128)(2,1)S(1)}, bf16[64,1152]{1,0:T(8,128)(2,1)S(1)}, u32[]{:S(2)}, u32[]{:S(2)}) collective-permute-start(bf16[64,1152]{1,0:T(8,128)(2,1)S(1)} %collective-permute-done.9.refs_2_), channel_id=1, source_target_pairs={{0,2},{2,0},{4,6},{6,4},{8,10},{10,8},{12,14},{14,12},{16,18},{18,... | collective-permute-start | bytes 442376 | tf_op jit(solution)/shard_map/ppermute | solution.py:309
  33.4 6.8 %collective-permute-start.10 = (bf16[288,512]{1,0:T(8,128)(2,1)S(1)}, bf16[288,512]{1,0:T(8,128)(2,1)S(1)}, u32[]{:S(2)}, u32[]{:S(2)}) collective-permute-start(bf16[288,512]{1,0:T(8,128)(2,1)S(1)} %get-tuple-element.53), channel_id=1, source_target_pairs={{0,2},{2,0},{4,6},{6,4},{8,10},{10,8},{12,14},{14,12},{16,18},{18,... | collective-permute-start | bytes 884744 | tf_op jit(solution)/shard_map/ppermute | solution.py:309
  40.4 0.9 %copy-start = (bf16[256,1792]{1,0:T(8,128)(2,1)}, bf16[256,1792]{1,0:T(8,128)(2,1)S(1)}, u32[]{:S(2)}) copy-start(bf16[256,1792]{1,0:T(8,128)(2,1)S(1)} %shard_map.101) | copy-start | bytes 2752516
  41.3 25.1 %all-to-all-start = ((bf16[16,16,1792]{2,1,0:T(8,128)(2,1)}), bf16[16,16,1792]{2,1,0:T(8,128)(2,1)}, u32[]{:S(2)}, u32[]{:S(2)}) async-start(bf16[16,16,1792]{2,1,0:T(8,128)(2,1)} %bitcast.7), calls=%async_computation | async-start | bytes 1835008 | tf_op jit(solution)/shard_map/all_to_all | solution.py:388
  47.3 5.6 %collective-permute-start.14 = (bf16[288,2048]{1,0:T(8,128)(2,1)S(1)}, bf16[288,2048]{1,0:T(8,128)(2,1)}, u32[]{:S(2)}, u32[]{:S(2)}) collective-permute-start(bf16[288,2048]{1,0:T(8,128)(2,1)S(1)} %get-tuple-element.62.refs_2_), channel_id=1, source_target_pairs={{0,1},{1,0},{2,3},{3,2},{4,5},{5,4},{6,7},{7,6},{8,9},{9,8},{10,11... | collective-permute-start | bytes 3538952 | tf_op jit(solution)/shard_map/ppermute | solution.py:312
  47.4 10.9 %collective-permute-start.16 = (bf16[288,2048]{1,0:T(8,128)(2,1)S(1)}, bf16[288,2048]{1,0:T(8,128)(2,1)}, u32[]{:S(2)}, u32[]{:S(2)}) collective-permute-start(bf16[288,2048]{1,0:T(8,128)(2,1)S(1)} %get-tuple-element.64.refs_2_), channel_id=1, source_target_pairs={{0,1},{1,0},{2,3},{3,2},{4,5},{5,4},{6,7},{7,6},{8,9},{9,8},{10,11... | collective-permute-start | bytes 3538952 | tf_op jit(solution)/shard_map/ppermute | solution.py:312
  47.9 5.0 %collective-permute-start.13 = (bf16[288,1024]{1,0:T(8,128)(2,1)S(1)}, bf16[288,1024]{1,0:T(8,128)(2,1)}, u32[]{:S(2)}, u32[]{:S(2)}) collective-permute-start(bf16[288,1024]{1,0:T(8,128)(2,1)S(1)} %shard_map.99.rows_ref.refs_0_), channel_id=1, source_target_pairs={{0,1},{1,0},{2,3},{3,2},{4,5},{5,4},{6,7},{7,6},{8,9},{9,8},{10,11... | collective-permute-start | bytes 1769480 | tf_op jit(solution)/shard_map/ppermute | solution.py:312
  47.9 10.3 %collective-permute-start.15 = (bf16[288,1024]{1,0:T(8,128)(2,1)S(1)}, bf16[288,1024]{1,0:T(8,128)(2,1)}, u32[]{:S(2)}, u32[]{:S(2)}) collective-permute-start(bf16[288,1024]{1,0:T(8,128)(2,1)S(1)} %shard_map.97.rows_ref.refs_0_), channel_id=1, source_target_pairs={{0,1},{1,0},{2,3},{3,2},{4,5},{5,4},{6,7},{7,6},{8,9},{9,8},{10,11... | collective-permute-start | bytes 1769480 | tf_op jit(solution)/shard_map/ppermute | solution.py:312
  58.2 8.2 %copy-start.1 = (s32[128]{0:T(128)S(1)}, s32[128]{0:T(128)}, u32[]{:S(2)}) copy-start(s32[128]{0:T(128)} %param.8) | copy-start | bytes 1540
  58.2 8.2 %copy-start.2 = (s32[128]{0:T(128)S(1)}, s32[128]{0:T(128)}, u32[]{:S(2)}) copy-start(s32[128]{0:T(128)} %param.9) | copy-start | bytes 1540

commit v6 on v5

--- a/solution.py
+++ b/solution.py
@@ -12,6 +12,7 @@
 CAPACITY = 18
 MAIN = 16
 SPLIT_COST = 8
+FORWARD_COST = 4
 VARIANT = "G"
 UNPACK_COST = 2
 LANES = 128
@@ -55,23 +56,21 @@
 
 
 def pack_kernel(me_ref, *refs):
-    sources, outs, staged, arrived = refs[:4], refs[4:12], refs[12:16], refs[16]
+    sources, outs, staged, arrived = refs[:3], refs[3:7], refs[7:10], refs[10]
     copies = [
         pltpu.make_async_copy(source, stage, arrived.at[i])
         for i, (source, stage) in enumerate(zip(sources, staged))
     ]
     for copy in copies:
         copy.start()
-    copies[0].wait()
-    copies[1].wait()
+    for copy in copies:
+        copy.wait()
+    width = staged[2].shape[1]
     picks = slot_picks(staged[0][...] ^ me_ref[0], staged[1][...])
-    for array in range(2):
-        copies[2 + array].wait()
-        width = staged[2].shape[1]
-        rows, cut = packed_rows(picks, staged[2 + array][...])
-        for z, out_ref in enumerate(outs[4 * array : 4 * (array + 1)]):
-            out_ref[:, :width] = rows[32 * z : 32 * (z + 1)]
-            out_ref[:, width:] = cut[32 * z : 32 * (z + 1)]
+    rows, cut = packed_rows(picks, staged[2][...])
+    for z, out_ref in enumerate(outs):
+        out_ref[:, :width] = rows[32 * z : 32 * (z + 1)]
+        out_ref[:, width:] = cut[32 * z : 32 * (z + 1)]
 
 
 def packed_rows(picks, values):
@@ -91,17 +90,47 @@
     return [slice(first, first + tile) for first in range(0, count, tile)]
 
 
-def forward_kernel(groups, member_ref, rows_ref, up_ref, down_ref, hidden_ref, slope_ref, *outs):
-    for units in by_tiles(up_ref.shape[1]):
+def forward_kernel(groups, member_ref, rows_ref, up_hbm, down_hbm, *refs):
+    hidden_ref, slope_ref, up_ref, down_ref = refs[:4]
+    outs, arrived = refs[4:-1], refs[-1]
+    tiles, width = by_tiles(up_ref.shape[1]), outs[0].shape[1]
+    bands = [slice(first, first + width) for first in range(0, down_ref.shape[0], width)]
+    pairs = [(up_hbm.at[:, units], up_ref.at[:, units]) for units in tiles]
+    pairs += [(down_hbm.at[band], down_ref.at[band]) for band in bands]
+    copies = [pltpu.make_async_copy(*pair, arrived.at[i]) for i, pair in enumerate(pairs)]
+    for copy in copies:
+        copy.start()
+    for units, copy in zip(tiles, copies):
+        copy.wait()
         pre = dot(rows_ref[...], up_ref[:, units], ((1,), (0,)))
         share = 0.5 * (1.0 + lax.erf(pre * INV_ROOT_TWO))
         hidden_ref[:, units] = (pre * share).astype(jnp.bfloat16)
         slope_ref[:, units] = share + pre * jnp.exp(-0.5 * pre * pre) * INV_ROOT_TAU
+    for copy in copies[len(tiles) :]:
+        copy.wait()
     for s, out_ref in enumerate(outs):
-        width = out_ref.shape[1]
         first = pl.multiple_of(lax.rem(member_ref[0] + s, groups) * width, LANES)
         weights = down_ref[pl.ds(first, width)]
         out_ref[...] = dot(hidden_ref[...], weights, ((1,), (1,))).astype(jnp.bfloat16)
+
+
+def forward(groups, member, x_rows, w_up, w_down_t):
+    depth, (width, units) = x_rows.shape[0], w_up.shape
+    return pl.pallas_call(
+        functools.partial(forward_kernel, groups),
+        out_shape=[
+            pltpu.VMEM((depth, units), jnp.bfloat16),
+            pltpu.VMEM((depth, units), jnp.float32),
+            pltpu.VMEM(w_up.shape, w_up.dtype),
+            pltpu.VMEM(w_down_t.shape, w_down_t.dtype),
+        ]
+        + shapes_of([(depth, width // groups)] * groups),
+        in_specs=[SMEM_SPEC, VMEM_SPEC] + [pl.BlockSpec(memory_space=pltpu.HBM)] * 2,
+        out_specs=[VMEM_SPEC] * (4 + groups),
+        scratch_shapes=[pltpu.SemaphoreType.DMA((len(by_tiles(units)) + groups,))],
+        cost_estimate=cost(FORWARD_COST),
+        compiler_params=pltpu.CompilerParams(vmem_limit_bytes=10 << 20),
+    )(member, x_rows, in_hbm(w_up), in_hbm(w_down_t))
 
 
 def backward_kernel(rows_ref, slope_ref, up_ref, down_ref, d_pre_ref, *outs):
@@ -174,20 +203,26 @@
     dx_ref[...] = pick(total[:, :width], total[:, width:])
 
 
-def weight_grad_kernel(n_parts, start_ref, *refs):
-    lefts, rights = refs[:n_parts], refs[n_parts : 2 * n_parts]
-    out_ref, turned = refs[2 * n_parts :]
-    own, tile = out_ref.shape
-    step = pl.program_id(0)
-
-    @pl.when(step == 0)
-    def _():
-        columns = pl.ds(pl.multiple_of(start_ref[0], LANES), own)
-        turned[...] = jnp.concatenate([ref[:, columns] for ref in lefts], axis=0).T
-
-    units = pl.ds(pl.multiple_of(step * tile, LANES), tile)
-    right = jnp.concatenate([ref[:, units] for ref in rights], axis=0)
-    out_ref[...] = dot(turned[...], right, ((1,), (0,))) * (1.0 / TOK_DEV)
+def weight_grads_kernel(n_parts, start_ref, *refs):
+    operands, outs, turned = refs[: 4 * n_parts], refs[4 * n_parts : -1], refs[-1]
+    own, tile = outs[0].shape
+    tiles = pl.num_programs(0) // 2
+
+    for i, out_ref in enumerate(outs):
+        lefts = operands[2 * n_parts * i : 2 * n_parts * i + n_parts]
+        rights = operands[2 * n_parts * i + n_parts : 2 * n_parts * (i + 1)]
+
+        @pl.when(pl.program_id(0) == i * tiles)
+        def _(lefts=lefts):
+            columns = pl.ds(pl.multiple_of(start_ref[0], LANES), own)
+            turned[...] = jnp.concatenate([ref[:, columns] for ref in lefts], axis=0).T
+
+        @pl.when(pl.program_id(0) // tiles == i)
+        def _(i=i, rights=rights, out_ref=out_ref):
+            first = (pl.program_id(0) - i * tiles) * tile
+            units = pl.ds(pl.multiple_of(first, LANES), tile)
+            right = jnp.concatenate([ref[:, units] for ref in rights], axis=0)
+            out_ref[...] = dot(turned[...], right, ((1,), (0,))) * (1.0 / TOK_DEV)
 
 
 VMEM_SPEC = pl.BlockSpec(memory_space=pltpu.VMEM)
@@ -218,40 +253,15 @@
     )(*operands)
 
 
-def stage_kernel(*refs):
-    sources, outs, arrived = refs[:2], refs[2:4], refs[4]
-    copies = [
-        pltpu.make_async_copy(source, out, arrived.at[i])
-        for i, (source, out) in enumerate(zip(sources, outs))
-    ]
-    for copy in copies:
-        copy.start()
-    for copy in copies:
-        copy.wait()
-
-
-def stage(*weights):
-    return pl.pallas_call(
-        stage_kernel,
-        out_shape=[pltpu.VMEM(w.shape, w.dtype) for w in weights],
-        in_specs=[pl.BlockSpec(memory_space=pltpu.HBM)] * 2,
-        out_specs=[VMEM_SPEC] * 2,
-        scratch_shapes=[pltpu.SemaphoreType.DMA((2,))],
-        cost_estimate=cost(4),
-        compiler_params=pltpu.CompilerParams(vmem_limit_bytes=2 << 20),
-    )(*[in_hbm(w) for w in weights])
-
-
-def pack(me, lang_row, slot_row, tokens, grad_out):
-    sources = (lang_row, slot_row, tokens, grad_out)
-    packed_width = tokens.shape[1] + LANES
+def pack(me, *sources):
+    packed_width = sources[2].shape[1] + LANES
     return pl.pallas_call(
         pack_kernel,
-        out_shape=shapes_of([(32, packed_width)] * 8),
-        in_specs=[SMEM_SPEC] + [pl.BlockSpec(memory_space=pltpu.HBM)] * 4,
-        out_specs=[VMEM_SPEC] * 8,
+        out_shape=shapes_of([(32, packed_width)] * 4),
+        in_specs=[SMEM_SPEC] + [pl.BlockSpec(memory_space=pltpu.HBM)] * 3,
+        out_specs=[VMEM_SPEC] * 4,
         scratch_shapes=[pltpu.VMEM(v.shape, v.dtype) for v in sources]
-        + [pltpu.SemaphoreType.DMA((4,))],
+        + [pltpu.SemaphoreType.DMA((3,))],
         cost_estimate=cost(2),
         compiler_params=pltpu.CompilerParams(vmem_limit_bytes=4 << 20),
     )(me, *[in_hbm(v) for v in sources])
@@ -261,26 +271,32 @@
     return lax.optimization_barrier((*values, *earlier))[: len(values)]
 
 
-def weight_grad(start, lefts, rights, own):
-    n_parts = len(lefts)
-    units = rights[0].shape[1]
-    depth = sum(left.shape[0] for left in lefts)
+def weight_grads(start, pairs, own):
+    n_parts, units = len(pairs[0][0]), pairs[0][1][0].shape[1]
+    depth = sum(left.shape[0] for left in pairs[0][0])
     tile = min(512, units)
+    tiles = units // tile
     if n_parts > 4:
-        left = lax.dynamic_slice_in_dim(jnp.concatenate(lefts, axis=0), start, own, axis=1)
-        return dot(left, jnp.concatenate(rights, axis=0), ((0,), (0,))) * (1.0 / TOK_DEV)
+        grads = []
+        for lefts, rights in pairs:
+            left = lax.dynamic_slice_in_dim(jnp.concatenate(lefts, axis=0), start, own, axis=1)
+            right = jnp.concatenate(rights, axis=0)
+            grads.append(dot(left, right, ((0,), (0,))) * (1.0 / TOK_DEV))
+        return grads
+    operands = [v for lefts, rights in pairs for v in (*lefts, *rights)]
     return pl.pallas_call(
-        functools.partial(weight_grad_kernel, n_parts),
-        out_shape=jax.ShapeDtypeStruct((own, units), jnp.float32),
-        grid=(units // tile,),
-        in_specs=[SMEM_SPEC] + [VMEM_SPEC] * (2 * n_parts),
-        out_specs=pl.BlockSpec((own, tile), lambda i: (0, i)),
+        functools.partial(weight_grads_kernel, n_parts),
+        out_shape=[jax.ShapeDtypeStruct((own, units), jnp.float32)] * 2,
+        grid=(2 * tiles,),
+        in_specs=[SMEM_SPEC] + [VMEM_SPEC] * len(operands),
+        out_specs=[
+            pl.BlockSpec((own, tile), lambda i: (0, jnp.minimum(i, tiles - 1))),
+            pl.BlockSpec((own, tile), lambda i: (0, jnp.maximum(i - tiles, 0))),
+        ],
         scratch_shapes=[pltpu.VMEM((own, depth), jnp.bfloat16)],
-        cost_estimate=pl.CostEstimate(
-            flops=2 * own * depth * units, bytes_accessed=4 * own * units, transcendentals=0
-        ),
-        compiler_params=pltpu.CompilerParams(vmem_limit_bytes=12 << 20),
-    )(start.reshape(1), *lefts, *rights)
+        cost_estimate=cost(4),
+        compiler_params=pltpu.CompilerParams(vmem_limit_bytes=24 << 20),
+    )(start.reshape(1), *operands[: 3 * n_parts], *[in_hbm(v) for v in operands[3 * n_parts :]])
 
 
 def per_device(tokens, grad_out, lang_ids, slot_ids, w_up, w_down_t):
@@ -331,11 +347,9 @@
             kept=(0,),
         )[0]
 
-    messages = pack(me, lang_row, slot_row, tokens, grad_out)
+    messages = pack(me, lang_row, slot_row, tokens) + pack(me, lang_row, slot_row, grad_out)
     x_low, x_send = over_near(messages[:4], 0)
     y_low, y_send = over_near(messages[4:], SPLIT_COST)
-    w_up, w_down_t = stage(w_up, w_down_t)
-    (x_send,) = after((x_send,), w_up)
     x_high, y_high = shift_near(x_send, 1), shift_near(y_send, 1)
     x_lows = over_groups(x_low)
     (x_high,) = after((x_high,), y_send, x_lows[-1])
@@ -345,20 +359,7 @@
     y_rows = unpack_parts(y_lows, y_highs, 0)
 
     depth, units = groups * PART, w_up.shape[1]
-    hidden, slope, *out_parts = local(
-        functools.partial(forward_kernel, groups),
-        shapes_of([(depth, units)])
-        + [jax.ShapeDtypeStruct((depth, units), jnp.float32)]
-        + shapes_of([(depth, width // groups)] * groups),
-        member,
-        x_rows,
-        w_up,
-        w_down_t,
-        scalars=1,
-        micros=4,
-        grant=10,
-        kept=(0, 1),
-    )
+    hidden, slope, w_up, w_down_t, *out_parts = forward(groups, member, x_rows, w_up, w_down_t)
     (y_rows,) = after((y_rows,), *out_parts)
     d_pre, *dx_parts = local(
         backward_kernel,
@@ -382,8 +383,11 @@
     shape = (n_lang * MAIN, packed_width + width // groups + LANES)
     packed = local(kernel, [shape], me, member, *sums, *dx_parts, scalars=2, micros=1)[0]
     y_rows, hidden, x_rows, d_pre = after((y_rows, hidden, x_rows, d_pre), packed)
-    grad_down = weight_grad(start, over_reps(y_rows), over_reps(hidden), own)
-    grad_up = weight_grad(start, over_reps(x_rows), over_reps(d_pre), own)
+    pairs = [
+        (over_reps(y_rows), over_reps(hidden)),
+        (over_reps(x_rows), over_reps(d_pre)),
+    ]
+    grad_down, grad_up = weight_grads(start, pairs, own)
     blocks = packed.reshape(n_lang, MAIN, shape[1])
     back = lax.all_to_all(blocks, "lang", split_axis=0, concat_axis=0, tiled=True).reshape(shape)
     (back,) = after((back,), grad_down, grad_up)

time: 69.3 us -> 68.2 us (0.984)
  starting transfers between devices: 25.2 us -> 28.8 us
  waiting for transfers between devices: 17.2 us -> 13.6 us
  Pallas kernels: 24.9 us -> 23.7 us
    pallas_call x8 -> x7, Pallas kernels: 8.93 us -> 5.62 us  [local(): pl.pallas_call(kernel, out_shape=[pltpu.VMEM(s.shape, s.dtype) if i in ke...]
    ppermute x5, waiting for transfers between devices: 6.46 us -> 3.24 us  [shift_group(): return lax.ppermute(value, 'lang', pairs)]
    all_to_all x1, waiting for transfers between devices: 2.77 us -> 0.39 us  [per_device(): lax.all_to_all(blocks, 'lang', split_axis=0, concat_axis=0, tiled=True)]
    pallas_call x4, Pallas kernels: 16 us -> 18.1 us  [the longest x1 10 us: weight_grads(): pl.pallas_call(functools.partial(weight_grads_kernel, n_parts), out_shape...]
    all_to_all x1, starting transfers between devices: 5.93 us -> 7.87 us  [per_device(): lax.all_to_all(blocks, 'lang', split_axis=0, concat_axis=0, tiled=True)]
    ppermute x5, starting transfers between devices: 4.9 us -> 6.58 us  [shift_group(): return lax.ppermute(value, 'lang', pairs)]
    ppermute x8, waiting for transfers between devices: 3.46 us -> 4.64 us  [shift_near(): return lax.ppermute(value, 'lang', pairs)]
    ppermute x4, waiting for transfers between devices: 4.5 us -> 5.34 us  [shift_rep(): lax.ppermute(value, 'rep', [(r, (r + step) % n_rep) for r in range(n_rep)])]
  transfers between devices with their start and end apart: 18 -> 18, of which waited for: 7 -> 10; matrix products, arithmetic and copies ran while one was open for 0% -> 0% of each run, Pallas kernels for 29% -> 29%
where the time goes in v6:
time: 68.2 us; the launch traced here: 67.9 us
  starting transfers between devices  28.8 us (42%)
  Pallas kernels  23.7 us (35%)
  waiting for transfers between devices  13.6 us (20%)
  local copies, waits for them, and re-layouts  1.03 us (2%)
  between operations  0.75 us (1%)
    ppermute x8, starting transfers between devices, shift_near(): return lax.ppermute(value, 'lang', pairs)  13.3 us
    pallas_call x1, Pallas kernels, weight_grads(): pl.pallas_call(functools.partial(weight_grads_kernel, n_parts), out_shape...  10 us
    all_to_all x1, starting transfers between devices, per_device(): lax.all_to_all(blocks, 'lang', split_axis=0, concat_axis=0, tiled=True)  7.87 us
    ppermute x5, starting transfers between devices, shift_group(): return lax.ppermute(value, 'lang', pairs)  6.58 us
    pallas_call x7, Pallas kernels, local(): pl.pallas_call(kernel, out_shape=[pltpu.VMEM(s.shape, s.dtype) if i in ke...  5.62 us
    ppermute x4, waiting for transfers between devices, shift_rep(): lax.ppermute(value, 'rep', [(r, (r + step) % n_rep) for r in range(n_rep)])  5.34 us
    pallas_call x1, Pallas kernels, forward(): pl.pallas_call(functools.partial(forward_kernel, groups), out_shape=[pltp...  5.32 us
    ppermute x8, waiting for transfers between devices, shift_near(): return lax.ppermute(value, 'lang', pairs)  4.64 us
  transfers between devices with their start and end apart: 18, of which 10 were waited for; matrix products, arithmetic and copies ran while one was open for 0% of the time, Pallas kernels for 29%

profile of v6, /device:TPU:0, one launch (start us, length us, event | category | flops | bytes accessed | tf_op | source)
XLA Modules:
  0.0 67.9 jit_solution(12433830435741382585)
XLA Ops:
  0.6 1.4 %shard_map.93 = (bf16[32,1152]{1,0:T(8,128)(2,1)S(1)}, bf16[32,1152]{1,0:T(8,128)(2,1)S(1)}, bf16[32,1152]{1,0:T(8,128)(2,1)S(1)}, bf16[32,1152]{1,0:T(8,128)(2,1)S(1)}) custom-call(s32[1]{0:T(128)} %bitcast.2.me_ref, s32[1,128]{1,0:T(1,128)} %bitcast.8, s32[1,128]{1,0:T(1,128)} %bitcast.11, bf16[128,1024]{1,0:T(8,128)(2,1)} %refs_2_.2), custom_call_target="tpu_custom_call" | custom-call | flops 2000000000 | tf_op jit(solution)/shard_map/pallas_call | solution.py:258
  2.0 3.1 %collective-permute-start = (bf16[32,1152]{1,0:T(8,128)(2,1)S(1)}, bf16[32,1152]{1,0:T(8,128)(2,1)S(1)}, u32[]{:S(2)}, u32[]{:S(2)}) collective-permute-start(bf16[32,1152]{1,0:T(8,128)(2,1)S(1)} %get-tuple-element.38), channel_id=1, source_target_pairs={{0,8},{2,10},{4,12},{6,14},{8,0},{10,2},{12,4},{14,6},{16,24},{18,... | collective-permute-start | bytes 221192 | tf_op jit(solution)/shard_map/ppermute | solution.py:317
  5.1 2.6 %collective-permute-start.1 = (bf16[32,1152]{1,0:T(8,128)(2,1)S(1)}, bf16[32,1152]{1,0:T(8,128)(2,1)S(1)}, u32[]{:S(2)}, u32[]{:S(2)}) collective-permute-start(bf16[32,1152]{1,0:T(8,128)(2,1)S(1)} %get-tuple-element.39), channel_id=1, source_target_pairs={{0,16},{2,18},{4,20},{6,22},{8,24},{10,26},{12,28},{14,30},{16,0},... | collective-permute-start | bytes 221192 | tf_op jit(solution)/shard_map/ppermute | solution.py:317
  7.7 1.4 %shard_map.95 = (bf16[32,1152]{1,0:T(8,128)(2,1)S(1)}, bf16[32,1152]{1,0:T(8,128)(2,1)S(1)}, bf16[32,1152]{1,0:T(8,128)(2,1)S(1)}, bf16[32,1152]{1,0:T(8,128)(2,1)S(1)}) custom-call(s32[1]{0:T(128)} %bitcast.2.me_ref, s32[1,128]{1,0:T(1,128)} %bitcast.9, s32[1,128]{1,0:T(1,128)} %bitcast.12, bf16[128,1024]{1,0:T(8,128)(2,1)} %refs_2_.3), custom_call_target="tpu_custom_call" | custom-call | flops 2000000000 | tf_op jit(solution)/shard_map/pallas_call | solution.py:258
  9.1 1.0 %collective-permute-start.5 = (bf16[32,1152]{1,0:T(8,128)(2,1)S(1)}, bf16[32,1152]{1,0:T(8,128)(2,1)S(1)}, u32[]{:S(2)}, u32[]{:S(2)}) collective-permute-start(bf16[32,1152]{1,0:T(8,128)(2,1)S(1)} %get-tuple-element.44), channel_id=1, source_target_pairs={{0,8},{2,10},{4,12},{6,14},{8,0},{10,2},{12,4},{14,6},{16,24},{18,... | collective-permute-start | bytes 221192 | tf_op jit(solution)/shard_map/ppermute | solution.py:317
  10.0 3.5 %collective-permute-start.6 = (bf16[32,1152]{1,0:T(8,128)(2,1)S(1)}, bf16[32,1152]{1,0:T(8,128)(2,1)S(1)}, u32[]{:S(2)}, u32[]{:S(2)}) collective-permute-start(bf16[32,1152]{1,0:T(8,128)(2,1)S(1)} %get-tuple-element.45), channel_id=1, source_target_pairs={{0,16},{2,18},{4,20},{6,22},{8,24},{10,26},{12,28},{14,30},{16,0},... | collective-permute-start | bytes 221192 | tf_op jit(solution)/shard_map/ppermute | solution.py:317
  13.5 1.2 %collective-permute-done.2.refs_3_ = bf16[32,1152]{1,0:T(8,128)(2,1)S(1)} collective-permute-done((bf16[32,1152]{1,0:T(8,128)(2,1)S(1)}, bf16[32,1152]{1,0:T(8,128)(2,1)S(1)}, u32[]{:S(2)}, u32[]{:S(2)}) %collective-permute-start.2) | collective-permute-done | bytes 73760 | tf_op jit(solution)/shard_map/ppermute | solution.py:317
  14.8 1.6 %collective-permute-start.4 = (bf16[64,1152]{1,0:T(8,128)(2,1)S(1)}, bf16[64,1152]{1,0:T(8,128)(2,1)S(1)}, u32[]{:S(2)}, u32[]{:S(2)}) collective-permute-start(bf16[64,1152]{1,0:T(8,128)(2,1)S(1)} %get-tuple-element.42), channel_id=1, source_target_pairs={{0,4},{2,6},{4,0},{6,2},{8,12},{10,14},{12,8},{14,10},{16,20},{18,... | collective-permute-start | bytes 442376 | tf_op jit(solution)/shard_map/ppermute | solution.py:317
  16.4 1.5 %collective-permute-start.3 = (bf16[64,1152]{1,0:T(8,128)(2,1)S(1)}, bf16[64,1152]{1,0:T(8,128)(2,1)S(1)}, u32[]{:S(2)}, u32[]{:S(2)}) collective-permute-start(bf16[64,1152]{1,0:T(8,128)(2,1)S(1)} %get-tuple-element.41.refs_0_), channel_id=1, source_target_pairs={{0,2},{2,0},{4,6},{6,4},{8,10},{10,8},{12,14},{14,12},{16,18},{18,... | collective-permute-start | bytes 442376 | tf_op jit(solution)/shard_map/ppermute | solution.py:325
  17.9 1.1 %collective-permute-done.6.refs_2_ = bf16[32,1152]{1,0:T(8,128)(2,1)S(1)} collective-permute-done((bf16[32,1152]{1,0:T(8,128)(2,1)S(1)}, bf16[32,1152]{1,0:T(8,128)(2,1)S(1)}, u32[]{:S(2)}, u32[]{:S(2)}) %collective-permute-start.6) | collective-permute-done | bytes 73760 | tf_op jit(solution)/shard_map/ppermute | solution.py:317
  19.0 0.8 %collective-permute-done.7.refs_3_ = bf16[32,1152]{1,0:T(8,128)(2,1)S(1)} collective-permute-done((bf16[32,1152]{1,0:T(8,128)(2,1)S(1)}, bf16[32,1152]{1,0:T(8,128)(2,1)S(1)}, u32[]{:S(2)}, u32[]{:S(2)}) %collective-permute-start.7) | collective-permute-done | bytes 73760 | tf_op jit(solution)/shard_map/ppermute | solution.py:317
  19.8 1.6 %collective-permute-start.9 = (bf16[64,1152]{1,0:T(8,128)(2,1)S(1)}, bf16[64,1152]{1,0:T(8,128)(2,1)S(1)}, u32[]{:S(2)}, u32[]{:S(2)}) collective-permute-start(bf16[64,1152]{1,0:T(8,128)(2,1)S(1)} %get-tuple-element.47), channel_id=1, source_target_pairs={{0,4},{2,6},{4,0},{6,2},{8,12},{10,14},{12,8},{14,10},{16,20},{18,... | collective-permute-start | bytes 442376 | tf_op jit(solution)/shard_map/ppermute | solution.py:317
  21.5 1.5 %collective-permute-start.8 = (bf16[64,1152]{1,0:T(8,128)(2,1)S(1)}, bf16[64,1152]{1,0:T(8,128)(2,1)S(1)}, u32[]{:S(2)}, u32[]{:S(2)}) collective-permute-start(bf16[64,1152]{1,0:T(8,128)(2,1)S(1)} %collective-permute-done.4.refs_2_), channel_id=1, source_target_pairs={{0,2},{2,0},{4,6},{6,4},{8,10},{10,8},{12,14},{14,12},{16,18},{18,... | collective-permute-start | bytes 442376 | tf_op jit(solution)/shard_map/ppermute | solution.py:325
  23.0 0.5 collective-permute-start.11
  23.5 1.5 %collective-permute-done.9.refs_2_ = bf16[64,1152]{1,0:T(8,128)(2,1)S(1)} collective-permute-done((bf16[64,1152]{1,0:T(8,128)(2,1)S(1)}, bf16[64,1152]{1,0:T(8,128)(2,1)S(1)}, u32[]{:S(2)}, u32[]{:S(2)}) %collective-permute-start.9) | collective-permute-done | bytes 147488 | tf_op jit(solution)/shard_map/ppermute | solution.py:317
  25.0 1.5 %collective-permute-start.12 = (bf16[64,1152]{1,0:T(8,128)(2,1)S(1)}, bf16[64,1152]{1,0:T(8,128)(2,1)S(1)}, u32[]{:S(2)}, u32[]{:S(2)}) collective-permute-start(bf16[64,1152]{1,0:T(8,128)(2,1)S(1)} %collective-permute-done.9.refs_2_), channel_id=1, source_target_pairs={{0,2},{2,0},{4,6},{6,4},{8,10},{10,8},{12,14},{14,12},{16,18},{18,... | collective-permute-start | bytes 442376 | tf_op jit(solution)/shard_map/ppermute | solution.py:325
  26.5 1.7 %collective-permute-done.8.refs_3_ = bf16[64,1152]{1,0:T(8,128)(2,1)S(1)} collective-permute-done((bf16[64,1152]{1,0:T(8,128)(2,1)S(1)}, bf16[64,1152]{1,0:T(8,128)(2,1)S(1)}, u32[]{:S(2)}, u32[]{:S(2)}) %collective-permute-start.8) | collective-permute-done | bytes 147488 | tf_op jit(solution)/shard_map/ppermute | solution.py:325
  28.3 0.2 shard_map.97.rows_ref.refs_4_
  28.4 5.3 %shard_map.98 = (bf16[288,2048]{1,0:T(8,128)(2,1)S(1)}, f32[288,2048]{1,0:T(8,128)S(1)}, bf16[1024,2048]{1,0:T(8,128)(2,1)S(1)}, bf16[1024,2048]{1,0:T(8,128)(2,...) custom-call(s32[1]{0:T(128)} %bitcast.3.member_ref, ...), custom_call_target="tpu_custom_call" | custom-call | flops 4000000000 | tf_op jit(solution)/shard_map/pallas_call | solution.py:119
  33.8 1.6 %collective-permute-start.10 = (bf16[288,512]{1,0:T(8,128)(2,1)S(1)}, bf16[288,512]{1,0:T(8,128)(2,1)S(1)}, u32[]{:S(2)}, u32[]{:S(2)}) collective-permute-start(bf16[288,512]{1,0:T(8,128)(2,1)S(1)} %get-tuple-element.51), channel_id=1, source_target_pairs={{0,2},{2,0},{4,6},{6,4},{8,10},{10,8},{12,14},{14,12},{16,18},{18,... | collective-permute-start | bytes 884744 | tf_op jit(solution)/shard_map/ppermute | solution.py:325
  35.5 2.6 %shard_map.100 = (bf16[288,2048]{1,0:T(8,128)(2,1)S(1)}, bf16[144,1024]{1,0:T(8,128)(2,1)S(1)}, bf16[144,1024]{1,0:T(8,128)(2,1)S(1)}) custom-call(bf16[288,1024]{1,0:T(8,128)(2,1)S(1)} %shard_map.99.rows_ref.refs_0_, f32[288,2048]{1,0:T(8,128)S(1)} %get-tuple-element.54.slope_ref, bf16[1024,2048]{1,0:T(8,128)(2,1)S(1)} %get-tuple-element.55.up_ref, ...), custom_call_target="tpu_custom_call" | custom-call | flops 3000000000 | tf_op jit(solution)/shard_map/pallas_call | solution.py:246
  38.1 1.0 %copy-done = bf16[288,2048]{1,0:T(8,128)(2,1)} copy-done((bf16[288,2048]{1,0:T(8,128)(2,1)}, bf16[288,2048]{1,0:T(8,128)(2,1)S(1)}, u32[]{:S(2)}) %copy-start) | copy-done | bytes 1179672
  39.1 1.4 %collective-permute-done.10.refs_1_ = bf16[288,512]{1,0:T(8,128)(2,1)S(1)} collective-permute-done((bf16[288,512]{1,0:T(8,128)(2,1)S(1)}, bf16[288,512]{1,0:T(8,128)(2,1)S(1)}, u32[]{:S(2)}, u32[]{:S(2)}) %collective-permute-start.10) | collective-permute-done | bytes 294944 | tf_op jit(solution)/shard_map/ppermute | solution.py:325
  40.5 1.2 %shard_map.101 = bf16[256,1792]{1,0:T(8,128)(2,1)} custom-call(s32[1]{0:T(128)} %bitcast.2.me_ref, s32[1]{0:T(128)} %bitcast.3.member_ref, bf16[288,512]{1,0:T(8,128)(2,1)S(1)} %get-tuple-element.50.refs_0_, bf16[288,512]{1,0:T(8,128)(2,1)S(1)} %collective-permute-done.10.refs_1_, bf16[144,1024]{1,0:T(8,128)(2,1)S(1)} %get-tuple-element.57.refs_2_, ...), custom_call_target="tpu_custom_call" | custom-call | flops 1000000000 | tf_op jit(solution)/shard_map/pallas_call | solution.py:246
  41.8 7.9 %all-to-all-start = ((bf16[16,16,1792]{2,1,0:T(8,128)(2,1)}), bf16[16,16,1792]{2,1,0:T(8,128)(2,1)S(1)}, u32[]{:S(2)}, u32[]{:S(2)}) async-start(bf16[16,16,1792]{2,1,0:T(8,128)(2,1)} %bitcast.4), calls=%async_computation | async-start | bytes 1835008 | tf_op jit(solution)/shard_map/all_to_all | solution.py:392
  49.7 0.5 collective-permute-start.16
  50.3 0.4 collective-permute-start.15
  50.7 4.5 %collective-permute-done.13.refs_1_ = bf16[288,1024]{1,0:T(8,128)(2,1)} collective-permute-done((bf16[288,1024]{1,0:T(8,128)(2,1)S(1)}, bf16[288,1024]{1,0:T(8,128)(2,1)}, u32[]{:S(2)}, u32[]{:S(2)}) %collective-permute-start.13) | collective-permute-done | bytes 589856 | tf_op jit(solution)/shard_map/ppermute | solution.py:328
  55.2 0.8 %collective-permute-done.15.refs_5_ = bf16[288,1024]{1,0:T(8,128)(2,1)} collective-permute-done((bf16[288,1024]{1,0:T(8,128)(2,1)S(1)}, bf16[288,1024]{1,0:T(8,128)(2,1)}, u32[]{:S(2)}, u32[]{:S(2)}) %collective-permute-start.15) | collective-permute-done | bytes 589856 | tf_op jit(solution)/shard_map/ppermute | solution.py:328
  56.1 10.0 %shard_map.102 = (f32[512,2048]{1,0:T(8,128)}, f32[512,2048]{1,0:T(8,128)}) custom-call(s32[1]{0:T(128)} %bitcast.6.start_ref, bf16[288,1024]{1,0:T(8,128)(2,1)S(1)} %shard_map.99.rows_ref.refs_0_, bf16[288,1024]{1,0:T(8,128)(2,1)} %collective-permute-done.13.refs_1_, bf16[288,2048]{1,0:T(8,128)(2,1)S(1)} %get-tuple-element.62.refs_2_, ...), custom_call_target="tpu_custom_call" | custom-call | flops 4000000000 | tf_op jit(solution)/shard_map/pallas_call | solution.py:287
  66.1 0.4 all-to-all-done
  66.5 1.4 %shard_map.103 = (bf16[128,1024]{1,0:T(8,128)(2,1)}, bf16[128,1024]{1,0:T(8,128)(2,1)}) custom-call(s32[1,128]{1,0:T(1,128)S(1)} %bitcast.10, s32[1,128]{1,0:T(1,128)S(1)} %bitcast.13, bf16[256,1792]{1,0:T(8,128)(2,1)S(1)} %bitcast.7), custom_call_target="tpu_custom_call" | custom-call | flops 1000000000 | tf_op jit(solution)/shard_map/pallas_call | solution.py:246
  (21 shorter events, 0.5 us)
Async XLA Ops:
  2.0 11.5 %collective-permute-start = (bf16[32,1152]{1,0:T(8,128)(2,1)S(1)}, bf16[32,1152]{1,0:T(8,128)(2,1)S(1)}, u32[]{:S(2)}, u32[]{:S(2)}) collective-permute-start(bf16[32,1152]{1,0:T(8,128)(2,1)S(1)} %get-tuple-element.38), channel_id=1, source_target_pairs={{0,8},{2,10},{4,12},{6,14},{8,0},{10,2},{12,4},{14,6},{16,24},{18,... | collective-permute-start | bytes 221192 | tf_op jit(solution)/shard_map/ppermute | solution.py:317
  5.1 8.4 %collective-permute-start.1 = (bf16[32,1152]{1,0:T(8,128)(2,1)S(1)}, bf16[32,1152]{1,0:T(8,128)(2,1)S(1)}, u32[]{:S(2)}, u32[]{:S(2)}) collective-permute-start(bf16[32,1152]{1,0:T(8,128)(2,1)S(1)} %get-tuple-element.39), channel_id=1, source_target_pairs={{0,16},{2,18},{4,20},{6,22},{8,24},{10,26},{12,28},{14,30},{16,0},... | collective-permute-start | bytes 221192 | tf_op jit(solution)/shard_map/ppermute | solution.py:317
  7.7 7.0 %collective-permute-start.2 = (bf16[32,1152]{1,0:T(8,128)(2,1)S(1)}, bf16[32,1152]{1,0:T(8,128)(2,1)S(1)}, u32[]{:S(2)}, u32[]{:S(2)}) collective-permute-start(bf16[32,1152]{1,0:T(8,128)(2,1)S(1)} %get-tuple-element.40), channel_id=1, source_target_pairs={{0,24},{2,26},{4,28},{6,30},{8,16},{10,18},{12,20},{14,22},{16,8},... | collective-permute-start | bytes 221192 | tf_op jit(solution)/shard_map/ppermute | solution.py:317
  9.1 8.8 %collective-permute-start.5 = (bf16[32,1152]{1,0:T(8,128)(2,1)S(1)}, bf16[32,1152]{1,0:T(8,128)(2,1)S(1)}, u32[]{:S(2)}, u32[]{:S(2)}) collective-permute-start(bf16[32,1152]{1,0:T(8,128)(2,1)S(1)} %get-tuple-element.44), channel_id=1, source_target_pairs={{0,8},{2,10},{4,12},{6,14},{8,0},{10,2},{12,4},{14,6},{16,24},{18,... | collective-permute-start | bytes 221192 | tf_op jit(solution)/shard_map/ppermute | solution.py:317
  10.0 8.9 %collective-permute-start.6 = (bf16[32,1152]{1,0:T(8,128)(2,1)S(1)}, bf16[32,1152]{1,0:T(8,128)(2,1)S(1)}, u32[]{:S(2)}, u32[]{:S(2)}) collective-permute-start(bf16[32,1152]{1,0:T(8,128)(2,1)S(1)} %get-tuple-element.45), channel_id=1, source_target_pairs={{0,16},{2,18},{4,20},{6,22},{8,24},{10,26},{12,28},{14,30},{16,0},... | collective-permute-start | bytes 221192 | tf_op jit(solution)/shard_map/ppermute | solution.py:317
  13.5 6.3 %collective-permute-start.7 = (bf16[32,1152]{1,0:T(8,128)(2,1)S(1)}, bf16[32,1152]{1,0:T(8,128)(2,1)S(1)}, u32[]{:S(2)}, u32[]{:S(2)}) collective-permute-start(bf16[32,1152]{1,0:T(8,128)(2,1)S(1)} %get-tuple-element.46), channel_id=1, source_target_pairs={{0,24},{2,26},{4,28},{6,30},{8,16},{10,18},{12,20},{14,22},{16,8},... | collective-permute-start | bytes 221192 | tf_op jit(solution)/shard_map/ppermute | solution.py:317
  14.8 6.6 %collective-permute-start.4 = (bf16[64,1152]{1,0:T(8,128)(2,1)S(1)}, bf16[64,1152]{1,0:T(8,128)(2,1)S(1)}, u32[]{:S(2)}, u32[]{:S(2)}) collective-permute-start(bf16[64,1152]{1,0:T(8,128)(2,1)S(1)} %get-tuple-element.42), channel_id=1, source_target_pairs={{0,4},{2,6},{4,0},{6,2},{8,12},{10,14},{12,8},{14,10},{16,20},{18,... | collective-permute-start | bytes 442376 | tf_op jit(solution)/shard_map/ppermute | solution.py:317
  16.4 5.1 %collective-permute-start.3 = (bf16[64,1152]{1,0:T(8,128)(2,1)S(1)}, bf16[64,1152]{1,0:T(8,128)(2,1)S(1)}, u32[]{:S(2)}, u32[]{:S(2)}) collective-permute-start(bf16[64,1152]{1,0:T(8,128)(2,1)S(1)} %get-tuple-element.41.refs_0_), channel_id=1, source_target_pairs={{0,2},{2,0},{4,6},{6,4},{8,10},{10,8},{12,14},{14,12},{16,18},{18,... | collective-permute-start | bytes 442376 | tf_op jit(solution)/shard_map/ppermute | solution.py:325
  19.8 5.2 %collective-permute-start.9 = (bf16[64,1152]{1,0:T(8,128)(2,1)S(1)}, bf16[64,1152]{1,0:T(8,128)(2,1)S(1)}, u32[]{:S(2)}, u32[]{:S(2)}) collective-permute-start(bf16[64,1152]{1,0:T(8,128)(2,1)S(1)} %get-tuple-element.47), channel_id=1, source_target_pairs={{0,4},{2,6},{4,0},{6,2},{8,12},{10,14},{12,8},{14,10},{16,20},{18,... | collective-permute-start | bytes 442376 | tf_op jit(solution)/shard_map/ppermute | solution.py:317
  21.5 6.8 %collective-permute-start.8 = (bf16[64,1152]{1,0:T(8,128)(2,1)S(1)}, bf16[64,1152]{1,0:T(8,128)(2,1)S(1)}, u32[]{:S(2)}, u32[]{:S(2)}) collective-permute-start(bf16[64,1152]{1,0:T(8,128)(2,1)S(1)} %collective-permute-done.4.refs_2_), channel_id=1, source_target_pairs={{0,2},{2,0},{4,6},{6,4},{8,10},{10,8},{12,14},{14,12},{16,18},{18,... | collective-permute-start | bytes 442376 | tf_op jit(solution)/shard_map/ppermute | solution.py:325
  23.0 12.3 %collective-permute-start.11 = (bf16[64,1152]{1,0:T(8,128)(2,1)S(1)}, bf16[64,1152]{1,0:T(8,128)(2,1)S(1)}, u32[]{:S(2)}, u32[]{:S(2)}) collective-permute-start(bf16[64,1152]{1,0:T(8,128)(2,1)S(1)} %get-tuple-element.52.refs_0_), channel_id=1, source_target_pairs={{0,2},{2,0},{4,6},{6,4},{8,10},{10,8},{12,14},{14,12},{16,18},{18,... | collective-permute-start | bytes 442376 | tf_op jit(solution)/shard_map/ppermute | solution.py:325
  25.0 10.3 %collective-permute-start.12 = (bf16[64,1152]{1,0:T(8,128)(2,1)S(1)}, bf16[64,1152]{1,0:T(8,128)(2,1)S(1)}, u32[]{:S(2)}, u32[]{:S(2)}) collective-permute-start(bf16[64,1152]{1,0:T(8,128)(2,1)S(1)} %collective-permute-done.9.refs_2_), channel_id=1, source_target_pairs={{0,2},{2,0},{4,6},{6,4},{8,10},{10,8},{12,14},{14,12},{16,18},{18,... | collective-permute-start | bytes 442376 | tf_op jit(solution)/shard_map/ppermute | solution.py:325
  33.8 6.8 %collective-permute-start.10 = (bf16[288,512]{1,0:T(8,128)(2,1)S(1)}, bf16[288,512]{1,0:T(8,128)(2,1)S(1)}, u32[]{:S(2)}, u32[]{:S(2)}) collective-permute-start(bf16[288,512]{1,0:T(8,128)(2,1)S(1)} %get-tuple-element.51), channel_id=1, source_target_pairs={{0,2},{2,0},{4,6},{6,4},{8,10},{10,8},{12,14},{14,12},{16,18},{18,... | collective-permute-start | bytes 884744 | tf_op jit(solution)/shard_map/ppermute | solution.py:325
  38.1 1.0 %copy-start = (bf16[288,2048]{1,0:T(8,128)(2,1)}, bf16[288,2048]{1,0:T(8,128)(2,1)S(1)}, u32[]{:S(2)}) copy-start(bf16[288,2048]{1,0:T(8,128)(2,1)S(1)} %get-tuple-element.64.refs_6_) | copy-start | bytes 3538948
  41.8 24.8 %all-to-all-start = ((bf16[16,16,1792]{2,1,0:T(8,128)(2,1)}), bf16[16,16,1792]{2,1,0:T(8,128)(2,1)S(1)}, u32[]{:S(2)}, u32[]{:S(2)}) async-start(bf16[16,16,1792]{2,1,0:T(8,128)(2,1)} %bitcast.4), calls=%async_computation | async-start | bytes 1835008 | tf_op jit(solution)/shard_map/all_to_all | solution.py:392
  49.6 6.4 %collective-permute-start.14 = (bf16[288,2048]{1,0:T(8,128)(2,1)S(1)}, bf16[288,2048]{1,0:T(8,128)(2,1)}, u32[]{:S(2)}, u32[]{:S(2)}) collective-permute-start(bf16[288,2048]{1,0:T(8,128)(2,1)S(1)} %get-tuple-element.62.refs_2_), channel_id=1, source_target_pairs={{0,1},{1,0},{2,3},{3,2},{4,5},{5,4},{6,7},{7,6},{8,9},{9,8},{10,11... | collective-permute-start | bytes 3538952 | tf_op jit(solution)/shard_map/ppermute | solution.py:328
  49.7 6.3 %collective-permute-start.16 = (bf16[288,2048]{1,0:T(8,128)(2,1)}, bf16[288,2048]{1,0:T(8,128)(2,1)}, u32[]{:S(2)}, u32[]{:S(2)}) collective-permute-start(bf16[288,2048]{1,0:T(8,128)(2,1)} %copy-done), channel_id=1, source_target_pairs={{0,1},{1,0},{2,3},{3,2},{4,5},{5,4},{6,7},{7,6},{8,9},{9,8},{10,11... | collective-permute-start | bytes 3538952 | tf_op jit(solution)/shard_map/ppermute | solution.py:328
  50.2 5.0 %collective-permute-start.13 = (bf16[288,1024]{1,0:T(8,128)(2,1)S(1)}, bf16[288,1024]{1,0:T(8,128)(2,1)}, u32[]{:S(2)}, u32[]{:S(2)}) collective-permute-start(bf16[288,1024]{1,0:T(8,128)(2,1)S(1)} %shard_map.99.rows_ref.refs_0_), channel_id=1, source_target_pairs={{0,1},{1,0},{2,3},{3,2},{4,5},{5,4},{6,7},{7,6},{8,9},{9,8},{10,11... | collective-permute-start | bytes 1769480 | tf_op jit(solution)/shard_map/ppermute | solution.py:328
  50.3 5.8 %collective-permute-start.15 = (bf16[288,1024]{1,0:T(8,128)(2,1)S(1)}, bf16[288,1024]{1,0:T(8,128)(2,1)}, u32[]{:S(2)}, u32[]{:S(2)}) collective-permute-start(bf16[288,1024]{1,0:T(8,128)(2,1)S(1)} %shard_map.97.rows_ref.refs_4_), channel_id=1, source_target_pairs={{0,1},{1,0},{2,3},{3,2},{4,5},{5,4},{6,7},{7,6},{8,9},{9,8},{10,11... | collective-permute-start | bytes 1769480 | tf_op jit(solution)/shard_map/ppermute | solution.py:328
  56.1 10.5 %copy-start.1 = (s32[128]{0:T(128)S(1)}, s32[128]{0:T(128)}, u32[]{:S(2)}) copy-start(s32[128]{0:T(128)} %param.8) | copy-start | bytes 1540
  56.1 10.5 %copy-start.2 = (s32[128]{0:T(128)S(1)}, s32[128]{0:T(128)}, u32[]{:S(2)}) copy-start(s32[128]{0:T(128)} %param.9) | copy-start | bytes 1540

commit v7 on v6

--- a/solution.py
+++ b/solution.py
@@ -78,9 +78,12 @@
     return rows[:ROWS], spare_cut(rows[ROWS:])
 
 
+ARRIVAL = (0, 2, 3, 1)
+
+
 def split_kernel(*refs):
     messages, outs = refs[:4], refs[4:]
-    for z, message_ref in enumerate(messages):
+    for z, message_ref in zip(ARRIVAL, messages):
         for place, out_ref in enumerate(outs):
             out_ref[16 * z : 16 * (z + 1)] = message_ref[16 * place : 16 * (place + 1)]
 
@@ -331,7 +334,7 @@
         return [value] + [shift_group(value, s) for s in range(1, groups)]
 
     def over_near(blocks, micros):
-        got = [blocks[0]] + [shift_near(blocks[z], 2 * z) for z in (1, 2, 3)]
+        got = [blocks[0]] + [shift_near(blocks[z], 2 * z) for z in ARRIVAL[1:]]
         return local(split_kernel, [(64, packed_width)] * 2, *got, micros=micros)
 
     def unpack(low, high, micros):

time: 68.2 us -> 67.4 us (0.988)
    ppermute x8, waiting for transfers between devices: 4.64 us -> 3.69 us  [shift_near(): return lax.ppermute(value, 'lang', pairs)]
  transfers between devices with their start and end apart: 18 -> 18, of which waited for: 10 -> 9; matrix products, arithmetic and copies ran while one was open for 0% -> 0% of each run, Pallas kernels for 29% -> 29%
where the time goes in v7:
time: 67.4 us; the launch traced here: 67.1 us
  starting transfers between devices  28.6 us (42%)
  Pallas kernels  23.7 us (35%)
  waiting for transfers between devices  13.1 us (19%)
  local copies, waits for them, and re-layouts  1.03 us (2%)
  between operations  0.76 us (1%)
    ppermute x8, starting transfers between devices, shift_near(): return lax.ppermute(value, 'lang', pairs)  13.3 us
    pallas_call x1, Pallas kernels, weight_grads(): pl.pallas_call(functools.partial(weight_grads_kernel, n_parts), out_shape...  10 us
    all_to_all x1, starting transfers between devices, per_device(): lax.all_to_all(blocks, 'lang', split_axis=0, concat_axis=0, tiled=True)  7.47 us
    ppermute x5, starting transfers between devices, shift_group(): return lax.ppermute(value, 'lang', pairs)  6.73 us
    pallas_call x7, Pallas kernels, local(): pl.pallas_call(kernel, out_shape=[pltpu.VMEM(s.shape, s.dtype) if i in ke...  5.61 us
    ppermute x4, waiting for transfers between devices, shift_rep(): lax.ppermute(value, 'rep', [(r, (r + step) % n_rep) for r in range(n_rep)])  5.34 us
    pallas_call x1, Pallas kernels, forward(): pl.pallas_call(functools.partial(forward_kernel, groups), out_shape=[pltp...  5.32 us
    ppermute x8, waiting for transfers between devices, shift_near(): return lax.ppermute(value, 'lang', pairs)  3.69 us
  transfers between devices with their start and end apart: 18, of which 9 were waited for; matrix products, arithmetic and copies ran while one was open for 0% of the time, Pallas kernels for 29%

profile of v7, /device:TPU:0, one launch (start us, length us, event | category | flops | bytes accessed | tf_op | source)
XLA Modules:
  0.0 67.1 jit_solution(13724822511607120237)
XLA Ops:
  0.6 1.4 %shard_map.93 = (bf16[32,1152]{1,0:T(8,128)(2,1)S(1)}, bf16[32,1152]{1,0:T(8,128)(2,1)S(1)}, bf16[32,1152]{1,0:T(8,128)(2,1)S(1)}, bf16[32,1152]{1,0:T(8,128)(2,1)S(1)}) custom-call(s32[1]{0:T(128)} %bitcast.2.me_ref, s32[1,128]{1,0:T(1,128)} %bitcast.8, s32[1,128]{1,0:T(1,128)} %bitcast.11, bf16[128,1024]{1,0:T(8,128)(2,1)} %refs_2_.2), custom_call_target="tpu_custom_call" | custom-call | flops 2000000000 | tf_op jit(solution)/shard_map/pallas_call | solution.py:261
  2.0 4.1 %collective-permute-start = (bf16[32,1152]{1,0:T(8,128)(2,1)S(1)}, bf16[32,1152]{1,0:T(8,128)(2,1)S(1)}, u32[]{:S(2)}, u32[]{:S(2)}) collective-permute-start(bf16[32,1152]{1,0:T(8,128)(2,1)S(1)} %get-tuple-element.38), channel_id=1, source_target_pairs={{0,16},{2,18},{4,20},{6,22},{8,24},{10,26},{12,28},{14,30},{16,0},... | collective-permute-start | bytes 221192 | tf_op jit(solution)/shard_map/ppermute | solution.py:320
  6.1 1.4 %collective-permute-start.1 = (bf16[32,1152]{1,0:T(8,128)(2,1)S(1)}, bf16[32,1152]{1,0:T(8,128)(2,1)S(1)}, u32[]{:S(2)}, u32[]{:S(2)}) collective-permute-start(bf16[32,1152]{1,0:T(8,128)(2,1)S(1)} %get-tuple-element.39), channel_id=1, source_target_pairs={{0,24},{2,26},{4,28},{6,30},{8,16},{10,18},{12,20},{14,22},{16,8},... | collective-permute-start | bytes 221192 | tf_op jit(solution)/shard_map/ppermute | solution.py:320
  7.5 0.2 collective-permute-start.2
  7.7 1.4 %shard_map.95 = (bf16[32,1152]{1,0:T(8,128)(2,1)S(1)}, bf16[32,1152]{1,0:T(8,128)(2,1)S(1)}, bf16[32,1152]{1,0:T(8,128)(2,1)S(1)}, bf16[32,1152]{1,0:T(8,128)(2,1)S(1)}) custom-call(s32[1]{0:T(128)} %bitcast.2.me_ref, s32[1,128]{1,0:T(1,128)} %bitcast.9, s32[1,128]{1,0:T(1,128)} %bitcast.12, bf16[128,1024]{1,0:T(8,128)(2,1)} %refs_2_.3), custom_call_target="tpu_custom_call" | custom-call | flops 2000000000 | tf_op jit(solution)/shard_map/pallas_call | solution.py:261
  9.1 2.9 %collective-permute-start.5 = (bf16[32,1152]{1,0:T(8,128)(2,1)S(1)}, bf16[32,1152]{1,0:T(8,128)(2,1)S(1)}, u32[]{:S(2)}, u32[]{:S(2)}) collective-permute-start(bf16[32,1152]{1,0:T(8,128)(2,1)S(1)} %get-tuple-element.44), channel_id=1, source_target_pairs={{0,16},{2,18},{4,20},{6,22},{8,24},{10,26},{12,28},{14,30},{16,0},... | collective-permute-start | bytes 221192 | tf_op jit(solution)/shard_map/ppermute | solution.py:320
  11.9 1.4 %collective-permute-start.6 = (bf16[32,1152]{1,0:T(8,128)(2,1)S(1)}, bf16[32,1152]{1,0:T(8,128)(2,1)S(1)}, u32[]{:S(2)}, u32[]{:S(2)}) collective-permute-start(bf16[32,1152]{1,0:T(8,128)(2,1)S(1)} %get-tuple-element.45), channel_id=1, source_target_pairs={{0,24},{2,26},{4,28},{6,30},{8,16},{10,18},{12,20},{14,22},{16,8},... | collective-permute-start | bytes 221192 | tf_op jit(solution)/shard_map/ppermute | solution.py:320
  13.4 1.6 %collective-permute-start.4 = (bf16[64,1152]{1,0:T(8,128)(2,1)S(1)}, bf16[64,1152]{1,0:T(8,128)(2,1)S(1)}, u32[]{:S(2)}, u32[]{:S(2)}) collective-permute-start(bf16[64,1152]{1,0:T(8,128)(2,1)S(1)} %get-tuple-element.42), channel_id=1, source_target_pairs={{0,4},{2,6},{4,0},{6,2},{8,12},{10,14},{12,8},{14,10},{16,20},{18,... | collective-permute-start | bytes 442376 | tf_op jit(solution)/shard_map/ppermute | solution.py:320
  14.9 1.5 %collective-permute-start.3 = (bf16[64,1152]{1,0:T(8,128)(2,1)S(1)}, bf16[64,1152]{1,0:T(8,128)(2,1)S(1)}, u32[]{:S(2)}, u32[]{:S(2)}) collective-permute-start(bf16[64,1152]{1,0:T(8,128)(2,1)S(1)} %get-tuple-element.41.refs_0_), channel_id=1, source_target_pairs={{0,2},{2,0},{4,6},{6,4},{8,10},{10,8},{12,14},{14,12},{16,18},{18,... | collective-permute-start | bytes 442376 | tf_op jit(solution)/shard_map/ppermute | solution.py:328
  16.4 0.9 %collective-permute-done.5.refs_1_ = bf16[32,1152]{1,0:T(8,128)(2,1)S(1)} collective-permute-done((bf16[32,1152]{1,0:T(8,128)(2,1)S(1)}, bf16[32,1152]{1,0:T(8,128)(2,1)S(1)}, u32[]{:S(2)}, u32[]{:S(2)}) %collective-permute-start.5) | collective-permute-done | bytes 73760 | tf_op jit(solution)/shard_map/ppermute | solution.py:320
  17.3 0.9 %collective-permute-done.6.refs_2_ = bf16[32,1152]{1,0:T(8,128)(2,1)S(1)} collective-permute-done((bf16[32,1152]{1,0:T(8,128)(2,1)S(1)}, bf16[32,1152]{1,0:T(8,128)(2,1)S(1)}, u32[]{:S(2)}, u32[]{:S(2)}) %collective-permute-start.6) | collective-permute-done | bytes 73760 | tf_op jit(solution)/shard_map/ppermute | solution.py:320
  18.3 0.5 collective-permute-done.7.refs_3_
  18.7 1.8 %collective-permute-start.9 = (bf16[64,1152]{1,0:T(8,128)(2,1)S(1)}, bf16[64,1152]{1,0:T(8,128)(2,1)S(1)}, u32[]{:S(2)}, u32[]{:S(2)}) collective-permute-start(bf16[64,1152]{1,0:T(8,128)(2,1)S(1)} %get-tuple-element.47), channel_id=1, source_target_pairs={{0,4},{2,6},{4,0},{6,2},{8,12},{10,14},{12,8},{14,10},{16,20},{18,... | collective-permute-start | bytes 442376 | tf_op jit(solution)/shard_map/ppermute | solution.py:320
  20.6 1.5 %collective-permute-start.8 = (bf16[64,1152]{1,0:T(8,128)(2,1)S(1)}, bf16[64,1152]{1,0:T(8,128)(2,1)S(1)}, u32[]{:S(2)}, u32[]{:S(2)}) collective-permute-start(bf16[64,1152]{1,0:T(8,128)(2,1)S(1)} %collective-permute-done.4.refs_2_), channel_id=1, source_target_pairs={{0,2},{2,0},{4,6},{6,4},{8,10},{10,8},{12,14},{14,12},{16,18},{18,... | collective-permute-start | bytes 442376 | tf_op jit(solution)/shard_map/ppermute | solution.py:328
  22.0 0.5 collective-permute-start.11
  22.6 1.4 %collective-permute-done.9.refs_2_ = bf16[64,1152]{1,0:T(8,128)(2,1)S(1)} collective-permute-done((bf16[64,1152]{1,0:T(8,128)(2,1)S(1)}, bf16[64,1152]{1,0:T(8,128)(2,1)S(1)}, u32[]{:S(2)}, u32[]{:S(2)}) %collective-permute-start.9) | collective-permute-done | bytes 147488 | tf_op jit(solution)/shard_map/ppermute | solution.py:320
  24.0 1.7 %collective-permute-start.12 = (bf16[64,1152]{1,0:T(8,128)(2,1)S(1)}, bf16[64,1152]{1,0:T(8,128)(2,1)S(1)}, u32[]{:S(2)}, u32[]{:S(2)}) collective-permute-start(bf16[64,1152]{1,0:T(8,128)(2,1)S(1)} %collective-permute-done.9.refs_2_), channel_id=1, source_target_pairs={{0,2},{2,0},{4,6},{6,4},{8,10},{10,8},{12,14},{14,12},{16,18},{18,... | collective-permute-start | bytes 442376 | tf_op jit(solution)/shard_map/ppermute | solution.py:328
  25.7 1.7 %collective-permute-done.8.refs_3_ = bf16[64,1152]{1,0:T(8,128)(2,1)S(1)} collective-permute-done((bf16[64,1152]{1,0:T(8,128)(2,1)S(1)}, bf16[64,1152]{1,0:T(8,128)(2,1)S(1)}, u32[]{:S(2)}, u32[]{:S(2)}) %collective-permute-start.8) | collective-permute-done | bytes 147488 | tf_op jit(solution)/shard_map/ppermute | solution.py:328
  27.5 5.3 %shard_map.98 = (bf16[288,2048]{1,0:T(8,128)(2,1)S(1)}, f32[288,2048]{1,0:T(8,128)S(1)}, bf16[1024,2048]{1,0:T(8,128)(2,1)S(1)}, bf16[1024,2048]{1,0:T(8,128)(2,...) custom-call(s32[1]{0:T(128)} %bitcast.3.member_ref, ...), custom_call_target="tpu_custom_call" | custom-call | flops 4000000000 | tf_op jit(solution)/shard_map/pallas_call | solution.py:122
  32.8 1.5 %collective-permute-start.10 = (bf16[288,512]{1,0:T(8,128)(2,1)S(1)}, bf16[288,512]{1,0:T(8,128)(2,1)S(1)}, u32[]{:S(2)}, u32[]{:S(2)}) collective-permute-start(bf16[288,512]{1,0:T(8,128)(2,1)S(1)} %get-tuple-element.51), channel_id=1, source_target_pairs={{0,2},{2,0},{4,6},{6,4},{8,10},{10,8},{12,14},{14,12},{16,18},{18,... | collective-permute-start | bytes 884744 | tf_op jit(solution)/shard_map/ppermute | solution.py:328
  34.5 2.6 %shard_map.100 = (bf16[288,2048]{1,0:T(8,128)(2,1)S(1)}, bf16[144,1024]{1,0:T(8,128)(2,1)S(1)}, bf16[144,1024]{1,0:T(8,128)(2,1)S(1)}) custom-call(bf16[288,1024]{1,0:T(8,128)(2,1)S(1)} %shard_map.99.rows_ref.refs_0_, f32[288,2048]{1,0:T(8,128)S(1)} %get-tuple-element.54.slope_ref, bf16[1024,2048]{1,0:T(8,128)(2,1)S(1)} %get-tuple-element.55.up_ref, ...), custom_call_target="tpu_custom_call" | custom-call | flops 3000000000 | tf_op jit(solution)/shard_map/pallas_call | solution.py:249
  37.2 1.0 %copy-done = bf16[288,2048]{1,0:T(8,128)(2,1)} copy-done((bf16[288,2048]{1,0:T(8,128)(2,1)}, bf16[288,2048]{1,0:T(8,128)(2,1)S(1)}, u32[]{:S(2)}) %copy-start) | copy-done | bytes 1179672
  38.2 1.4 %collective-permute-done.10.refs_1_ = bf16[288,512]{1,0:T(8,128)(2,1)S(1)} collective-permute-done((bf16[288,512]{1,0:T(8,128)(2,1)S(1)}, bf16[288,512]{1,0:T(8,128)(2,1)S(1)}, u32[]{:S(2)}, u32[]{:S(2)}) %collective-permute-start.10) | collective-permute-done | bytes 294944 | tf_op jit(solution)/shard_map/ppermute | solution.py:328
  39.6 1.2 %shard_map.101 = bf16[256,1792]{1,0:T(8,128)(2,1)} custom-call(s32[1]{0:T(128)} %bitcast.2.me_ref, s32[1]{0:T(128)} %bitcast.3.member_ref, bf16[288,512]{1,0:T(8,128)(2,1)S(1)} %get-tuple-element.50.refs_0_, bf16[288,512]{1,0:T(8,128)(2,1)S(1)} %collective-permute-done.10.refs_1_, bf16[144,1024]{1,0:T(8,128)(2,1)S(1)} %get-tuple-element.57.refs_2_, ...), custom_call_target="tpu_custom_call" | custom-call | flops 1000000000 | tf_op jit(solution)/shard_map/pallas_call | solution.py:249
  40.8 7.5 %all-to-all-start = ((bf16[16,16,1792]{2,1,0:T(8,128)(2,1)}), bf16[16,16,1792]{2,1,0:T(8,128)(2,1)S(1)}, u32[]{:S(2)}, u32[]{:S(2)}) async-start(bf16[16,16,1792]{2,1,0:T(8,128)(2,1)} %bitcast.4), calls=%async_computation | async-start | bytes 1835008 | tf_op jit(solution)/shard_map/all_to_all | solution.py:395
  48.4 0.5 collective-permute-start.16
  49.0 0.4 collective-permute-start.15
  49.4 4.5 %collective-permute-done.13.refs_1_ = bf16[288,1024]{1,0:T(8,128)(2,1)} collective-permute-done((bf16[288,1024]{1,0:T(8,128)(2,1)S(1)}, bf16[288,1024]{1,0:T(8,128)(2,1)}, u32[]{:S(2)}, u32[]{:S(2)}) %collective-permute-start.13) | collective-permute-done | bytes 589856 | tf_op jit(solution)/shard_map/ppermute | solution.py:331
  53.9 0.8 %collective-permute-done.15.refs_5_ = bf16[288,1024]{1,0:T(8,128)(2,1)} collective-permute-done((bf16[288,1024]{1,0:T(8,128)(2,1)S(1)}, bf16[288,1024]{1,0:T(8,128)(2,1)}, u32[]{:S(2)}, u32[]{:S(2)}) %collective-permute-start.15) | collective-permute-done | bytes 589856 | tf_op jit(solution)/shard_map/ppermute | solution.py:331
  54.8 10.0 %shard_map.102 = (f32[512,2048]{1,0:T(8,128)}, f32[512,2048]{1,0:T(8,128)}) custom-call(s32[1]{0:T(128)} %bitcast.6.start_ref, bf16[288,1024]{1,0:T(8,128)(2,1)S(1)} %shard_map.99.rows_ref.refs_0_, bf16[288,1024]{1,0:T(8,128)(2,1)} %collective-permute-done.13.refs_1_, bf16[288,2048]{1,0:T(8,128)(2,1)S(1)} %get-tuple-element.62.refs_2_, ...), custom_call_target="tpu_custom_call" | custom-call | flops 4000000000 | tf_op jit(solution)/shard_map/pallas_call | solution.py:290
  64.8 0.9 %all-to-all-done = bf16[16,16,1792]{2,1,0:T(8,128)(2,1)S(1)} async-done(((bf16[16,16,1792]{2,1,0:T(8,128)(2,1)}), bf16[16,16,1792]{2,1,0:T(8,128)(2,1)S(1)}, u32[]{:S(2)}, u32[]{:S(2)}) %all-to-all-start) | async-done | bytes 917536 | tf_op jit(solution)/shard_map/all_to_all | solution.py:395
  65.7 1.4 %shard_map.103 = (bf16[128,1024]{1,0:T(8,128)(2,1)}, bf16[128,1024]{1,0:T(8,128)(2,1)}) custom-call(s32[1,128]{1,0:T(1,128)S(1)} %bitcast.10, s32[1,128]{1,0:T(1,128)S(1)} %bitcast.13, bf16[256,1792]{1,0:T(8,128)(2,1)S(1)} %bitcast.7), custom_call_target="tpu_custom_call" | custom-call | flops 1000000000 | tf_op jit(solution)/shard_map/pallas_call | solution.py:249
  (21 shorter events, 0.6 us)
Async XLA Ops:
  2.0 11.3 %collective-permute-start = (bf16[32,1152]{1,0:T(8,128)(2,1)S(1)}, bf16[32,1152]{1,0:T(8,128)(2,1)S(1)}, u32[]{:S(2)}, u32[]{:S(2)}) collective-permute-start(bf16[32,1152]{1,0:T(8,128)(2,1)S(1)} %get-tuple-element.38), channel_id=1, source_target_pairs={{0,16},{2,18},{4,20},{6,22},{8,24},{10,26},{12,28},{14,30},{16,0},... | collective-permute-start | bytes 221192 | tf_op jit(solution)/shard_map/ppermute | solution.py:320
  6.1 7.2 %collective-permute-start.1 = (bf16[32,1152]{1,0:T(8,128)(2,1)S(1)}, bf16[32,1152]{1,0:T(8,128)(2,1)S(1)}, u32[]{:S(2)}, u32[]{:S(2)}) collective-permute-start(bf16[32,1152]{1,0:T(8,128)(2,1)S(1)} %get-tuple-element.39), channel_id=1, source_target_pairs={{0,24},{2,26},{4,28},{6,30},{8,16},{10,18},{12,20},{14,22},{16,8},... | collective-permute-start | bytes 221192 | tf_op jit(solution)/shard_map/ppermute | solution.py:320
  7.5 5.8 %collective-permute-start.2 = (bf16[32,1152]{1,0:T(8,128)(2,1)S(1)}, bf16[32,1152]{1,0:T(8,128)(2,1)S(1)}, u32[]{:S(2)}, u32[]{:S(2)}) collective-permute-start(bf16[32,1152]{1,0:T(8,128)(2,1)S(1)} %get-tuple-element.40), channel_id=1, source_target_pairs={{0,8},{2,10},{4,12},{6,14},{8,0},{10,2},{12,4},{14,6},{16,24},{18,... | collective-permute-start | bytes 221192 | tf_op jit(solution)/shard_map/ppermute | solution.py:320
  9.1 8.2 %collective-permute-start.5 = (bf16[32,1152]{1,0:T(8,128)(2,1)S(1)}, bf16[32,1152]{1,0:T(8,128)(2,1)S(1)}, u32[]{:S(2)}, u32[]{:S(2)}) collective-permute-start(bf16[32,1152]{1,0:T(8,128)(2,1)S(1)} %get-tuple-element.44), channel_id=1, source_target_pairs={{0,16},{2,18},{4,20},{6,22},{8,24},{10,26},{12,28},{14,30},{16,0},... | collective-permute-start | bytes 221192 | tf_op jit(solution)/shard_map/ppermute | solution.py:320
  11.9 6.3 %collective-permute-start.6 = (bf16[32,1152]{1,0:T(8,128)(2,1)S(1)}, bf16[32,1152]{1,0:T(8,128)(2,1)S(1)}, u32[]{:S(2)}, u32[]{:S(2)}) collective-permute-start(bf16[32,1152]{1,0:T(8,128)(2,1)S(1)} %get-tuple-element.45), channel_id=1, source_target_pairs={{0,24},{2,26},{4,28},{6,30},{8,16},{10,18},{12,20},{14,22},{16,8},... | collective-permute-start | bytes 221192 | tf_op jit(solution)/shard_map/ppermute | solution.py:320
  13.3 5.4 %collective-permute-start.7 = (bf16[32,1152]{1,0:T(8,128)(2,1)S(1)}, bf16[32,1152]{1,0:T(8,128)(2,1)S(1)}, u32[]{:S(2)}, u32[]{:S(2)}) collective-permute-start(bf16[32,1152]{1,0:T(8,128)(2,1)S(1)} %get-tuple-element.46), channel_id=1, source_target_pairs={{0,8},{2,10},{4,12},{6,14},{8,0},{10,2},{12,4},{14,6},{16,24},{18,... | collective-permute-start | bytes 221192 | tf_op jit(solution)/shard_map/ppermute | solution.py:320
  13.4 7.2 %collective-permute-start.4 = (bf16[64,1152]{1,0:T(8,128)(2,1)S(1)}, bf16[64,1152]{1,0:T(8,128)(2,1)S(1)}, u32[]{:S(2)}, u32[]{:S(2)}) collective-permute-start(bf16[64,1152]{1,0:T(8,128)(2,1)S(1)} %get-tuple-element.42), channel_id=1, source_target_pairs={{0,4},{2,6},{4,0},{6,2},{8,12},{10,14},{12,8},{14,10},{16,20},{18,... | collective-permute-start | bytes 442376 | tf_op jit(solution)/shard_map/ppermute | solution.py:320
  14.9 5.6 %collective-permute-start.3 = (bf16[64,1152]{1,0:T(8,128)(2,1)S(1)}, bf16[64,1152]{1,0:T(8,128)(2,1)S(1)}, u32[]{:S(2)}, u32[]{:S(2)}) collective-permute-start(bf16[64,1152]{1,0:T(8,128)(2,1)S(1)} %get-tuple-element.41.refs_0_), channel_id=1, source_target_pairs={{0,2},{2,0},{4,6},{6,4},{8,10},{10,8},{12,14},{14,12},{16,18},{18,... | collective-permute-start | bytes 442376 | tf_op jit(solution)/shard_map/ppermute | solution.py:328
  18.7 5.2 %collective-permute-start.9 = (bf16[64,1152]{1,0:T(8,128)(2,1)S(1)}, bf16[64,1152]{1,0:T(8,128)(2,1)S(1)}, u32[]{:S(2)}, u32[]{:S(2)}) collective-permute-start(bf16[64,1152]{1,0:T(8,128)(2,1)S(1)} %get-tuple-element.47), channel_id=1, source_target_pairs={{0,4},{2,6},{4,0},{6,2},{8,12},{10,14},{12,8},{14,10},{16,20},{18,... | collective-permute-start | bytes 442376 | tf_op jit(solution)/shard_map/ppermute | solution.py:320
  20.6 6.8 %collective-permute-start.8 = (bf16[64,1152]{1,0:T(8,128)(2,1)S(1)}, bf16[64,1152]{1,0:T(8,128)(2,1)S(1)}, u32[]{:S(2)}, u32[]{:S(2)}) collective-permute-start(bf16[64,1152]{1,0:T(8,128)(2,1)S(1)} %collective-permute-done.4.refs_2_), channel_id=1, source_target_pairs={{0,2},{2,0},{4,6},{6,4},{8,10},{10,8},{12,14},{14,12},{16,18},{18,... | collective-permute-start | bytes 442376 | tf_op jit(solution)/shard_map/ppermute | solution.py:328
  22.0 12.3 %collective-permute-start.11 = (bf16[64,1152]{1,0:T(8,128)(2,1)S(1)}, bf16[64,1152]{1,0:T(8,128)(2,1)S(1)}, u32[]{:S(2)}, u32[]{:S(2)}) collective-permute-start(bf16[64,1152]{1,0:T(8,128)(2,1)S(1)} %get-tuple-element.52.refs_0_), channel_id=1, source_target_pairs={{0,2},{2,0},{4,6},{6,4},{8,10},{10,8},{12,14},{14,12},{16,18},{18,... | collective-permute-start | bytes 442376 | tf_op jit(solution)/shard_map/ppermute | solution.py:328
  24.0 10.4 %collective-permute-start.12 = (bf16[64,1152]{1,0:T(8,128)(2,1)S(1)}, bf16[64,1152]{1,0:T(8,128)(2,1)S(1)}, u32[]{:S(2)}, u32[]{:S(2)}) collective-permute-start(bf16[64,1152]{1,0:T(8,128)(2,1)S(1)} %collective-permute-done.9.refs_2_), channel_id=1, source_target_pairs={{0,2},{2,0},{4,6},{6,4},{8,10},{10,8},{12,14},{14,12},{16,18},{18,... | collective-permute-start | bytes 442376 | tf_op jit(solution)/shard_map/ppermute | solution.py:328
  32.8 6.8 %collective-permute-start.10 = (bf16[288,512]{1,0:T(8,128)(2,1)S(1)}, bf16[288,512]{1,0:T(8,128)(2,1)S(1)}, u32[]{:S(2)}, u32[]{:S(2)}) collective-permute-start(bf16[288,512]{1,0:T(8,128)(2,1)S(1)} %get-tuple-element.51), channel_id=1, source_target_pairs={{0,2},{2,0},{4,6},{6,4},{8,10},{10,8},{12,14},{14,12},{16,18},{18,... | collective-permute-start | bytes 884744 | tf_op jit(solution)/shard_map/ppermute | solution.py:328
  37.1 1.0 %copy-start = (bf16[288,2048]{1,0:T(8,128)(2,1)}, bf16[288,2048]{1,0:T(8,128)(2,1)S(1)}, u32[]{:S(2)}) copy-start(bf16[288,2048]{1,0:T(8,128)(2,1)S(1)} %get-tuple-element.64.refs_6_) | copy-start | bytes 3538948
  40.8 24.9 %all-to-all-start = ((bf16[16,16,1792]{2,1,0:T(8,128)(2,1)}), bf16[16,16,1792]{2,1,0:T(8,128)(2,1)S(1)}, u32[]{:S(2)}, u32[]{:S(2)}) async-start(bf16[16,16,1792]{2,1,0:T(8,128)(2,1)} %bitcast.4), calls=%async_computation | async-start | bytes 1835008 | tf_op jit(solution)/shard_map/all_to_all | solution.py:395
  48.3 6.4 %collective-permute-start.14 = (bf16[288,2048]{1,0:T(8,128)(2,1)S(1)}, bf16[288,2048]{1,0:T(8,128)(2,1)}, u32[]{:S(2)}, u32[]{:S(2)}) collective-permute-start(bf16[288,2048]{1,0:T(8,128)(2,1)S(1)} %get-tuple-element.62.refs_2_), channel_id=1, source_target_pairs={{0,1},{1,0},{2,3},{3,2},{4,5},{5,4},{6,7},{7,6},{8,9},{9,8},{10,11... | collective-permute-start | bytes 3538952 | tf_op jit(solution)/shard_map/ppermute | solution.py:331
  48.4 6.3 %collective-permute-start.16 = (bf16[288,2048]{1,0:T(8,128)(2,1)}, bf16[288,2048]{1,0:T(8,128)(2,1)}, u32[]{:S(2)}, u32[]{:S(2)}) collective-permute-start(bf16[288,2048]{1,0:T(8,128)(2,1)} %copy-done), channel_id=1, source_target_pairs={{0,1},{1,0},{2,3},{3,2},{4,5},{5,4},{6,7},{7,6},{8,9},{9,8},{10,11... | collective-permute-start | bytes 3538952 | tf_op jit(solution)/shard_map/ppermute | solution.py:331
  48.9 5.0 %collective-permute-start.13 = (bf16[288,1024]{1,0:T(8,128)(2,1)S(1)}, bf16[288,1024]{1,0:T(8,128)(2,1)}, u32[]{:S(2)}, u32[]{:S(2)}) collective-permute-start(bf16[288,1024]{1,0:T(8,128)(2,1)S(1)} %shard_map.99.rows_ref.refs_0_), channel_id=1, source_target_pairs={{0,1},{1,0},{2,3},{3,2},{4,5},{5,4},{6,7},{7,6},{8,9},{9,8},{10,11... | collective-permute-start | bytes 1769480 | tf_op jit(solution)/shard_map/ppermute | solution.py:331
  49.0 5.8 %collective-permute-start.15 = (bf16[288,1024]{1,0:T(8,128)(2,1)S(1)}, bf16[288,1024]{1,0:T(8,128)(2,1)}, u32[]{:S(2)}, u32[]{:S(2)}) collective-permute-start(bf16[288,1024]{1,0:T(8,128)(2,1)S(1)} %shard_map.97.rows_ref.refs_4_), channel_id=1, source_target_pairs={{0,1},{1,0},{2,3},{3,2},{4,5},{5,4},{6,7},{7,6},{8,9},{9,8},{10,11... | collective-permute-start | bytes 1769480 | tf_op jit(solution)/shard_map/ppermute | solution.py:331
  54.7 11.0 %copy-start.1 = (s32[128]{0:T(128)S(1)}, s32[128]{0:T(128)}, u32[]{:S(2)}) copy-start(s32[128]{0:T(128)} %param.8) | copy-start | bytes 1540
  54.8 11.0 %copy-start.2 = (s32[128]{0:T(128)S(1)}, s32[128]{0:T(128)}, u32[]{:S(2)}) copy-start(s32[128]{0:T(128)} %param.9) | copy-start | bytes 1540
